TPU v7x, 32 devices: a whole 2x2x4 slice. The times are simulated.
32 devices in a mesh: dp: 8 (over z, x), tensor: 4 (over y, core).
Axes of the slice: x: 2, y: 2, z: 4, core: 2. Of those that a mesh axis runs over, the one named last changes fastest.
Arguments:
- tokens: bfloat16 [16384, 1024], P(('dp', 'tensor')), may hold values from -6 to 6
- cotangent: bfloat16 [16384, 1024], P(('dp', 'tensor')), may hold values from -6 to 6
- lengths: int32 [8, 2], P('dp'), may hold values from 1 to 1024, as said below
- w_heads: float32 [1024, 4096], P('dp', 'tensor'), may hold values from -0.1875 to 0.1875
- first_heads: float32 [1024, 4096], P('dp', 'tensor'), may hold values from -28 to 28
- second_heads: float32 [1024, 4096], P('dp', 'tensor'), may hold values from 81.92 to 327.68
- w_shared: float32 [1024, 288], P('dp'), may hold values from -0.1875 to 0.1875
- first_shared: float32 [1024, 288], P('dp'), may hold values from -80 to 80
- second_shared: float32 [1024, 288], P('dp'), may hold values from 819.2 to 3276.8
- w_out: float32 [1024, 2048], P('dp', 'tensor'), may hold values from -0.125 to 0.125
- first_out: float32 [1024, 2048], P('dp', 'tensor'), may hold values from -64 to 64
- second_out: float32 [1024, 2048], P('dp', 'tensor'), may hold values from 491.52 to 1966.08
- chan_params: float32 [5, 2048], P(None, 'tensor'), may hold values from -2.5 to 2.5
- first_chan: float32 [5, 2048], P(None, 'tensor'), may hold values from -28 to 28
- second_chan: float32 [5, 2048], P(None, 'tensor'), may hold values from 81.92 to 327.68
- bc_params: float32 [5, 256], replicated, may hold values from -2.5 to 2.5
- first_bc: float32 [5, 256], replicated, may hold values from -80 to 80
- second_bc: float32 [5, 256], replicated, may hold values from 819.2 to 3276.8
- head_params: float32 [3, 32], P(None, 'tensor'), may hold values from -7 to 2.8
- first_head: float32 [3, 32], P(None, 'tensor'), may hold values from -224 to 224
- second_head: float32 [3, 32], P(None, 'tensor'), may hold values from 4915.2 to 19660.8
- gains: float32 [3072], replicated, may hold values from 0.48 to 2.16
- first_gains: float32 [3072], replicated, may hold values from -80 to 80
- second_gains: float32 [3072], replicated, may hold values from 819.2 to 3276.8
Outputs:
- output: float32 [16384, 1024], P(('dp', 'tensor'))
- input_grad: float32 [16384, 1024], P(('dp', 'tensor'))
- new_heads: float32 [1024, 4096], P('dp', 'tensor')
- new_first_heads: float32 [1024, 4096], P('dp', 'tensor')
- new_second_heads: float32 [1024, 4096], P('dp', 'tensor')
- new_shared: float32 [1024, 288], P('dp')
- new_first_shared: float32 [1024, 288], P('dp')
- new_second_shared: float32 [1024, 288], P('dp')
- new_out: float32 [1024, 2048], P('dp', 'tensor')
- new_first_out: float32 [1024, 2048], P('dp', 'tensor')
- new_second_out: float32 [1024, 2048], P('dp', 'tensor')
- new_chan: float32 [5, 2048], P(None, 'tensor')
- new_first_chan: float32 [5, 2048], P(None, 'tensor')
- new_second_chan: float32 [5, 2048], P(None, 'tensor')
- new_bc: float32 [5, 256], replicated
- new_first_bc: float32 [5, 256], replicated
- new_second_bc: float32 [5, 256], replicated
- new_head: float32 [3, 32], P(None, 'tensor')
- new_first_head: float32 [3, 32], P(None, 'tensor')
- new_second_head: float32 [3, 32], P(None, 'tensor')
- new_gains: float32 [3072], replicated
- new_first_gains: float32 [3072], replicated
- new_second_gains: float32 [3072], replicated
Inputs may be any that keep to these rules, and one draw needn't show every extreme that they name: In every group the lengths sum to at most 2048, and one sequence, in a slot drawn from the seed, has exactly 1024 rows.
All inputs are finite; a program needn't handle non-finite values.
Results may differ from a plain program's by a relative error of at most 0.008.
Values may be sent and summed in bfloat16 or wider, within the bound.
A program may use at most 192 MiB of HBM per device.

v0:
```python
import jax
import jax.numpy as jnp
from jax import lax
from jax.sharding import PartitionSpec as P

SPAN = 256
STEP = 10


NORM_EPS = 1e-05
BETA_ONE = 0.9
BETA_TWO = 0.95
ADAM_EPS = 1e-08
MATRIX_RATE = 0.03
SMALL_RATE = 0.1
HEAD_RATE = 1.0
GAIN_RATE = 0.5
WEIGHT_DECAY = 0.1
HIGHEST_PREC = lax.Precision.HIGHEST


def segment_ids(seq_lengths, group_rows):
    seq_ends = jnp.cumsum(seq_lengths)
    positions = jnp.arange(group_rows, dtype=jnp.int32)
    return jnp.sum((positions[:, None] >= seq_ends[None, :]).astype(jnp.int32), axis=1)


def causal_conv(raw_vals, conv_taps, seq_ids):
    result = conv_taps[4][None, :] + conv_taps[3][None, :] * raw_vals
    for offset in range(1, 4):
        shifted = jnp.concatenate(
            [jnp.zeros((offset, raw_vals.shape[1]), raw_vals.dtype), raw_vals[:-offset]], axis=0
        )
        shifted_ids = jnp.concatenate([jnp.full((offset,), -1, jnp.int32), seq_ids[:-offset]])
        same_seq = (shifted_ids == seq_ids).astype(raw_vals.dtype)
        result = result + conv_taps[3 - offset][None, :] * shifted * same_seq[:, None]
    return result


def state_space(values, in_maps, out_maps, log_decay, step_size, seq_ids, skip_gain):
    seq_rows, head_count, head_size = values.shape
    state_size = in_maps.shape[1]
    blocks = seq_rows // SPAN
    values_c = values.reshape(blocks, SPAN, head_count, head_size)
    in_c = in_maps.reshape(blocks, SPAN, state_size)
    out_c = out_maps.reshape(blocks, SPAN, state_size)
    decay_c = jnp.transpose(
        jnp.cumsum(log_decay.reshape(blocks, SPAN, head_count), axis=1), (0, 2, 1)
    )
    step_c = jnp.transpose(step_size.reshape(blocks, SPAN, head_count), (0, 2, 1))
    ids_c = seq_ids.reshape(blocks, SPAN)
    last_ids = ids_c[:, -1]
    prior_ids = jnp.concatenate([jnp.full((1,), -1, jnp.int32), last_ids[:-1]])
    positions = jnp.arange(SPAN, dtype=jnp.int32)
    allowed = (ids_c[:, :, None] == ids_c[:, None, :]) & (positions[:, None] >= positions[None, :])[
        None
    ]
    allowed = allowed[:, None, :, :]
    spread = decay_c[:, :, :, None] - decay_c[:, :, None, :]
    kernel = jnp.where(allowed, jnp.exp(jnp.where(allowed, spread, 0.0)), 0.0)
    inner_prod = jnp.einsum("cqn,ckn->cqk", out_c, in_c, precision=HIGHEST_PREC)
    mixing = kernel * inner_prod[:, None, :, :] * step_c[:, :, None, :]
    local_part = jnp.einsum("chqk,ckhp->cqhp", mixing, values_c, precision=HIGHEST_PREC)
    tail_decay = decay_c[:, :, -1]
    same_last = (ids_c == last_ids[:, None]).astype(jnp.float32)
    carry_w = jnp.exp(tail_decay[:, :, None] - decay_c) * step_c * same_last[:, None, :]
    fresh_states = jnp.einsum("chk,ckn,ckhp->chpn", carry_w, in_c, values_c, precision=HIGHEST_PREC)
    through = (last_ids == prior_ids).astype(jnp.float32)[:, None] * jnp.exp(tail_decay)

    def advance(carry_state, block_item):
        fresh_block, factor = block_item
        return (factor[:, None, None] * carry_state + fresh_block, carry_state)

    start_state = jnp.zeros((head_count, head_size, state_size), jnp.float32)
    _, entering = lax.scan(advance, start_state, (fresh_states, through))
    reach_w = jnp.exp(decay_c) * (ids_c == prior_ids[:, None]).astype(jnp.float32)[:, None, :]
    carried = jnp.einsum("cqn,chpn->cqhp", out_c, entering, precision=HIGHEST_PREC)
    carried = carried * jnp.transpose(reach_w, (0, 2, 1))[:, :, :, None]
    result = (local_part + carried).reshape(seq_rows, head_count, head_size)
    return result + skip_gain[None, :, None] * values


def contract_last(left, right):
    return lax.dot_general(
        left, right, (((1,), (1,)), ((), ())), preferred_element_type=jnp.float32
    )


def contract_first(left, right):
    return lax.dot_general(
        left, right, (((0,), (0,)), ((), ())), preferred_element_type=jnp.float32
    )


def adam_step(weight, grad, first_moment, second_moment, rate, decay_rate):
    first_new = BETA_ONE * first_moment + (1.0 - BETA_ONE) * grad
    second_new = BETA_TWO * second_moment + (1.0 - BETA_TWO) * grad * grad
    first_fix = 1.0 - BETA_ONE**STEP
    second_fix = 1.0 - BETA_TWO**STEP
    update = first_new / first_fix / (jnp.sqrt(second_new / second_fix) + ADAM_EPS)
    return (weight - rate * (update + decay_rate * weight), first_new, second_new)


def shards(
    tokens,
    cotangent,
    lengths,
    w_heads,
    first_heads,
    second_heads,
    w_shared,
    first_shared,
    second_shared,
    w_out,
    first_out,
    second_out,
    chan_params,
    first_chan,
    second_chan,
    bc_params,
    first_bc,
    second_bc,
    head_params,
    first_head,
    second_head,
    gains,
    first_gains,
    second_gains,
):
    tensor_ways = lax.axis_size("tensor")
    tensor_pos = lax.axis_index("tensor")
    own_rows = tokens.shape[0]
    group_rows = own_rows * tensor_ways
    model_width = tokens.shape[1]
    own_heads = head_params.shape[1]
    all_heads = own_heads * tensor_ways
    own_inner = chan_params.shape[1]
    all_inner = own_inner * tensor_ways
    head_size = own_inner // own_heads
    state_size = bc_params.shape[1] // 2
    seq_ids = segment_ids(lengths[0], group_rows)
    valid_rows = (seq_ids < lengths.shape[1]).astype(jnp.float32)
    own_valid = lax.dynamic_slice_in_dim(valid_rows, tensor_pos * own_rows, own_rows, 0)[:, None]
    norm_gain = gains[:model_width]
    gate_gain = gains[model_width:]
    inputs_f = tokens.astype(jnp.float32)
    norm_scale = lax.rsqrt(jnp.mean(inputs_f * inputs_f, axis=1, keepdims=True) + NORM_EPS)
    normed = (inputs_f * norm_scale * norm_gain[None, :]).astype(jnp.bfloat16)
    gathered = lax.all_gather(normed, "tensor", axis=0, tiled=True)
    heads_full, shared_full = (
        lax.all_gather(w_heads.astype(jnp.bfloat16), "dp", axis=0, tiled=True),
        lax.all_gather(w_shared.astype(jnp.bfloat16), "dp", axis=0, tiled=True),
    )
    out_cols = lax.all_gather(w_out.astype(jnp.bfloat16), "dp", axis=0, tiled=True)
    head_cols = jnp.dot(gathered, heads_full, preferred_element_type=jnp.float32).reshape(
        group_rows, own_heads, 2, head_size
    )
    shared = jnp.dot(gathered, shared_full, preferred_element_type=jnp.float32)
    gate_vals = head_cols[:, :, 0, :]
    conv_in = jnp.concatenate(
        [head_cols[:, :, 1, :].reshape(group_rows, own_inner), shared[:, : 2 * state_size]], axis=1
    )
    conv_taps = jnp.concatenate([chan_params, bc_params], axis=1)

    def convolve(raw_vals, taps_all):
        return jax.nn.silu(causal_conv(raw_vals, taps_all, seq_ids))

    conv_out, conv_pull = jax.vjp(convolve, conv_in, conv_taps)
    conv_low = lax.optimization_barrier(conv_out.astype(jnp.bfloat16)).astype(jnp.float32)
    step_raw = lax.dynamic_slice_in_dim(
        shared[:, 2 * state_size :], tensor_pos * own_heads, own_heads, 1
    )

    def mixer(conv_vals, gate_in, step_in, head_vals):
        step_size = jax.nn.softplus(step_in + head_vals[1][None, :])
        log_decay = -jnp.exp(head_vals[0])[None, :] * step_size
        value_part = conv_vals[:, :own_inner].reshape(group_rows, own_heads, head_size)
        in_maps = conv_vals[:, own_inner : own_inner + state_size]
        out_maps = conv_vals[:, own_inner + state_size :]
        ssd_out = state_space(
            value_part, in_maps, out_maps, log_decay, step_size, seq_ids, head_vals[2]
        )
        return (ssd_out * jax.nn.silu(gate_in)).reshape(group_rows, own_inner)

    gated_vals, mixer_pull = jax.vjp(mixer, conv_low, gate_vals, step_raw, head_params)
    cotangent_f = cotangent.astype(jnp.float32)
    masked = (cotangent_f * own_valid).astype(jnp.bfloat16)
    own_gain = lax.dynamic_slice_in_dim(gate_gain, tensor_pos * own_inner, own_inner, 0)[None, :]
    square_sum = lax.psum(jnp.sum(gated_vals * gated_vals, axis=1), "tensor")
    inv_gate = lax.rsqrt(square_sum / all_inner + NORM_EPS)[:, None]
    normal_out = (gated_vals * inv_gate * own_gain).astype(jnp.bfloat16)
    branch = lax.psum_scatter(
        contract_last(normal_out, out_cols), "tensor", scatter_dimension=0, tiled=True
    )
    masked_all = lax.all_gather(masked, "tensor", axis=0, tiled=True)
    d_normal = jnp.dot(masked_all, out_cols, preferred_element_type=jnp.float32)
    weighted = d_normal * own_gain
    row_dot = lax.psum(jnp.sum(gated_vals * weighted, axis=1), "tensor")[:, None]
    d_gated = inv_gate * weighted - gated_vals * inv_gate**3 * row_dot / all_inner
    own_gain_grad = jnp.sum(gated_vals * inv_gate * d_normal, axis=0)
    gate_gain_grad = lax.dynamic_update_slice_in_dim(
        jnp.zeros((all_inner,), jnp.float32), own_gain_grad, tensor_pos * own_inner, 0
    )
    out_grad = contract_first(masked_all, normal_out)
    output = inputs_f + own_valid * branch
    d_conv, d_gate, d_step, d_head = mixer_pull(d_gated)
    d_raw, d_taps = conv_pull(d_conv)
    d_value = d_raw[:, :own_inner].reshape(group_rows, own_heads, head_size)
    d_cols = (
        jnp.stack([d_gate, d_value], axis=2).reshape(group_rows, 2 * own_inner).astype(jnp.bfloat16)
    )
    d_step_all = lax.dynamic_update_slice_in_dim(
        jnp.zeros((group_rows, all_heads), jnp.float32), d_step, tensor_pos * own_heads, 1
    )
    d_shared_part = jnp.concatenate([d_raw[:, own_inner:], d_step_all], axis=1)
    d_normed_part = contract_last(d_cols, heads_full)
    d_normed_rows, d_shared_rows = (
        lax.psum_scatter(d_normed_part, "tensor", scatter_dimension=0, tiled=True),
        lax.psum_scatter(d_shared_part, "tensor", scatter_dimension=0, tiled=True),
    )
    d_shared_low = d_shared_rows.astype(jnp.bfloat16)
    d_normed = d_normed_rows + contract_last(d_shared_low, shared_full)
    weighted_in = d_normed * norm_gain[None, :]
    in_dot = jnp.sum(inputs_f * weighted_in, axis=1, keepdims=True)
    input_grad = (
        cotangent_f + norm_scale * weighted_in - inputs_f * norm_scale**3 * in_dot / model_width
    )
    heads_grad = contract_first(gathered, d_cols)
    heads_shard, out_shard = (
        lax.psum_scatter(heads_grad, "dp", scatter_dimension=0, tiled=True),
        lax.psum_scatter(out_grad, "dp", scatter_dimension=0, tiled=True),
    )
    gain_grad = jnp.concatenate([jnp.sum(inputs_f * norm_scale * d_normed, axis=0), gate_gain_grad])
    chan_all = lax.dynamic_update_slice_in_dim(
        jnp.zeros((5, all_inner), jnp.float32), d_taps[:, :own_inner], tensor_pos * own_inner, 1
    )
    head_all = lax.dynamic_update_slice_in_dim(
        jnp.zeros((3, all_heads), jnp.float32), d_head, tensor_pos * own_heads, 1
    )
    shared_grad = contract_first(normed, d_shared_low)
    shared_sum, bc_sum, gain_sum, chan_sum, head_sum = lax.psum(
        (shared_grad, d_taps[:, own_inner:], gain_grad, chan_all, head_all), ("dp", "tensor")
    )
    shared_rows = w_shared.shape[0]
    shared_shard = lax.dynamic_slice_in_dim(
        shared_sum, lax.axis_index("dp") * shared_rows, shared_rows, 0
    )
    chan_grad = lax.dynamic_slice_in_dim(chan_sum, tensor_pos * own_inner, own_inner, 1)
    head_grad = lax.dynamic_slice_in_dim(head_sum, tensor_pos * own_heads, own_heads, 1)
    new_heads, new_first_heads, new_second_heads = adam_step(
        w_heads, heads_shard, first_heads, second_heads, MATRIX_RATE, WEIGHT_DECAY
    )
    new_shared, new_first_shared, new_second_shared = adam_step(
        w_shared, shared_shard, first_shared, second_shared, MATRIX_RATE, WEIGHT_DECAY
    )
    new_out, new_first_out, new_second_out = adam_step(
        w_out, out_shard, first_out, second_out, MATRIX_RATE, WEIGHT_DECAY
    )
    new_chan, new_first_chan, new_second_chan = adam_step(
        chan_params, chan_grad, first_chan, second_chan, SMALL_RATE, 0.0
    )
    new_bc, new_first_bc, new_second_bc = adam_step(
        bc_params, bc_sum, first_bc, second_bc, SMALL_RATE, 0.0
    )
    new_head, new_first_head, new_second_head = adam_step(
        head_params, head_grad, first_head, second_head, HEAD_RATE, 0.0
    )
    new_gains, new_first_gains, new_second_gains = adam_step(
        gains, gain_sum, first_gains, second_gains, GAIN_RATE, 0.0
    )
    return (
        output,
        input_grad,
        new_heads,
        new_first_heads,
        new_second_heads,
        new_shared,
        new_first_shared,
        new_second_shared,
        new_out,
        new_first_out,
        new_second_out,
        new_chan,
        new_first_chan,
        new_second_chan,
        new_bc,
        new_first_bc,
        new_second_bc,
        new_head,
        new_first_head,
        new_second_head,
        new_gains,
        new_first_gains,
        new_second_gains,
    )


def solution(mesh):
    return jax.shard_map(
        shards,
        mesh=mesh,
        in_specs=(
            P(("dp", "tensor"), None),
            P(("dp", "tensor"), None),
            P("dp", None),
            P("dp", "tensor"),
            P("dp", "tensor"),
            P("dp", "tensor"),
            P("dp", None),
            P("dp", None),
            P("dp", None),
            P("dp", "tensor"),
            P("dp", "tensor"),
            P("dp", "tensor"),
            P(None, "tensor"),
            P(None, "tensor"),
            P(None, "tensor"),
            P(),
            P(),
            P(),
            P(None, "tensor"),
            P(None, "tensor"),
            P(None, "tensor"),
            P(),
            P(),
            P(),
        ),
        out_specs=(
            P(("dp", "tensor"), None),
            P(("dp", "tensor"), None),
            P("dp", "tensor"),
            P("dp", "tensor"),
            P("dp", "tensor"),
            P("dp", None),
            P("dp", None),
            P("dp", None),
            P("dp", "tensor"),
            P("dp", "tensor"),
            P("dp", "tensor"),
            P(None, "tensor"),
            P(None, "tensor"),
            P(None, "tensor"),
            P(),
            P(),
            P(),
            P(None, "tensor"),
            P(None, "tensor"),
            P(None, "tensor"),
            P(),
            P(),
            P(),
        ),
        check_vma=False,
    )
```

profile of v0, /device:TPU:0, one launch (start us, length us, event | category | flops | bytes accessed | tf_op | source)
XLA Modules:
  0.0 986.5 jit_solution(18223181324397656344)
XLA Ops:
  16.8 33.7 %all_gather.17 = bf16[1024,288]{0,1:T(8,128)(2,1)S(1)} all-gather(bf16[128,288]{0,1:T(8,128)(2,1)S(1)} %convert_element_type.75), channel_id=1, replica_groups=mesh['dp'=8,'tensor'=4] {'dp'}, dimensions={0}, use_global_device_ids=true | all-gather | bytes 663552 | tf_op jit(solution)/shard_map/all_gather | solution.py:152
  54.3 13.0 %all-gather.7.cloned.1.call-done = bf16[1024,1024]{1,0:T(8,128)(2,1)} async-done(((bf16[128,1024]{1,0:T(8,128)(2,1)}), bf16[1024,1024]{1,0:T(8,128)(2,1)}) %all-gather.7.cloned.1.call-update) | async-done | bytes 2097168 | tf_op jit(solution)/shard_map/all_gather | solution.py:151
  67.3 35.1 %all-gather.5.cloned.1.call-done = bf16[2048,1024]{1,0:T(8,128)(2,1)} async-done(((bf16[512,1024]{1,0:T(8,128)(2,1)}), bf16[2048,1024]{1,0:T(8,128)(2,1)}) %all-gather.5.cloned.1.call-update) | async-done | bytes 4194320 | tf_op jit(solution)/shard_map/all_gather | solution.py:149
  102.4 7.2 fusion.120
  122.9 11.7 %multiply_convert_fusion = (bf16[2048,768]{0,1:T(8,128)(2,1)S(1)}, f32[2048,768]{0,1:T(8,128)}) fusion(f32[2048]{0:T(1024)S(1)} %get-tuple-element.358, f32[2045,768]{0,1:T(8,128)S(1)} %fusion.26, f32[768]{0:T(1024)S(1)} %get-tuple-element.258, f32[2048]{0:T(1024)S(1)} %get-tuple-element.359, f32[2046,768]{0,1:T(8,128)} %fusion.25, ...), kind=kLoop, calls=%fused_computation.56 | loop fusion | flops 26738688 | bytes 34624512 | tf_op jit(solution)/shard_map/convert_element_type | solution.py:169
  144.6 8.2 reduce-window.24
  167.4 18.4 %while.34 = (s32[]{:T(128)}, f32[8,64,128]{2,1,0:T(8,128)S(1)}, f32[8,8,64,128]{3,2,1,0:T(8,128)}, f32[8,8,1,1]{1,3,2,0:T(1,128)}, f32[8,8]{1,0:T(8,128)S(1)}, /...) while((s32[]{:T(128)}, f32[8,64,128]{2,1,0:T(8,128)S(1)}, f32[8,8,64,128]{3,2,1,0:T(8,128)}, ...), condition=%wide.region_6.7_spmd.clone, body=%wide.region_5.6_spmd.clone.sunk | while | flops 262147 | bytes 1312488 | solution.py:75
  191.5 14.8 %bitcast_add_fusion.3 = f32[8,256,8,64]{1,3,2,0:T(8,128)S(1)} fusion(f32[8,256,8,64]{1,3,2,0:T(8,128)S(1)} %fusion.123, f32[8,8,256]{2,1,0:T(8,128)S(1)} %bitcast.275, f32[8,256,256]{2,1,0:T(8,128)S(1)} %copy-done.34, f32[8,8,256]{2,1,0:T(8,128)S(1)} %get-tuple-element.329, pred[8,256,256]{2,1,0:T(8,128)(4,1)S(1)} %copy-done.44, ...), kind=kOutput, calls=%fused_computation.78 | convolution fusion | flops 3244294144 | bytes 13303808 | tf_op jit(solution)/shard_map/jvp(chqk,ckhp->cqhp)/dot_general | solution.py:63
  222.6 7.5 fusion.105
  230.2 68.8 %reduce-scatter.14.cloned.1.call-done = f32[128,512]{1,0:T(8,128)} async-done(((f32[1024,512]{1,0:T(8,128)}), f32[128,512]{1,0:T(8,128)}) %reduce-scatter.14.cloned.1.call-update) | async-done | bytes 262160 | tf_op jit(solution)/shard_map/reduce_scatter | solution.py:231
  310.4 30.3 %all-gather.9.cloned.1.call-done = bf16[1024,512]{1,0:T(8,128)(2,1)} async-done(((bf16[128,512]{1,0:T(8,128)(2,1)}), bf16[1024,512]{1,0:T(8,128)(2,1)}) %all-gather.9.cloned.1.call-update) | async-done | bytes 1048592 | tf_op jit(solution)/shard_map/all_gather | solution.py:154
  340.7 9.6 multiply_reduce_fusion.7
  378.4 22.8 %fusion.11 = (f32[8,8,256]{2,1,0:T(8,128)S(1)}, f32[8,8,256]{2,1,0:T(8,128)S(1)}, f32[8,8,256]{2,1,0:T(8,128)S(1)}, f32[8,256,256]{2,1,0:T(8,128)}) fusion(f32[8,8,256]{2,1,0:T(8,128)S(1)} %bitcast.276, f32[8,256,256]{2,1,0:T(8,128)S(1)} %copy-done.35, f32[8,8,256]{2,1,0:T(8,128)S(1)} %get-tuple-element.329, pred[8,256,256]{2,1,0:T(8,128)(4,1)S(1)} %copy-done.45, ...), kind=kOutput, calls=%fused_computation.26 | convolution fusion | flops 3283566592 | bytes 11337728 | tf_op jit(solution)/shard_map/transpose(jvp(chqk,ckhp->cqhp))/dot_general | solution.py:63
  401.2 7.8 fusion.68
  410.5 20.6 %while.35 = (s32[]{:T(128)}, f32[8,64,128]{2,1,0:T(8,128)S(1)}, f32[8,8,64,128]{3,2,1,0:T(8,128)}, f32[8,8]{1,0:T(8,128)S(1)}, f32[8,8,64,128]{3,2,1,0:T(8,128)}...) while((s32[]{:T(128)}, f32[8,64,128]{2,1,0:T(8,128)S(1)}, ...), condition=%wide.region_15.16_spmd.clone, body=%wide.region_13.15_spmd.clone.sunk | while | flops 393212 | bytes 1573196 | solution.py:75
  431.1 10.2 %fusion.67 = f32[8,256,128]{2,1,0:T(8,128)} fusion(f32[8,8,64,128]{3,2,1,0:T(8,128)} %get-tuple-element.200, f32[8,256,8]{1,2,0:T(8,128)S(1)} %copy-done.48, bf16[8,256,8,64]{1,0,3,2:T(8,128)(2,1)} %bitcast.248), kind=kOutput, calls=%fused_computation.125 | convolution fusion | flops 1612709888 | bytes 5308416 | tf_op jit(solution)/shard_map/transpose(jvp(chk,ckn,ckhp->chpn))/dot_general | solution.py:67
  441.4 7.1 multiply_reduce_fusion.6
  449.0 19.8 %reduce-window.31 = f32[8,8,2,128]{3,1,2,0:T(8,128)S(1)} reduce-window(f32[8,8,2,128]{3,1,2,0:T(8,128)S(1)} %get-tuple-element.348, f32[]{:T(128)} %constant.91.clone.1), window={size=1x1x1x128 pad=0_0x0_0x0_0x0_127}, to_apply=%region_22.23 | reduce-window | flops 2080768 | bytes 131076 | tf_op jit(solution)/shard_map/reduce-window.3
  480.9 17.1 %bitcast_add_fusion.2 = f32[8,256,8,64]{1,3,2,0:T(8,128)S(1)} fusion(f32[8,256,8,64]{1,3,2,0:T(8,128)} %get-tuple-element.367, f32[8,256,8]{1,2,0:T(8,128)S(1)} %copy-done.49, f32[8,8,256]{2,1,0:T(8,128)S(1)} %bitcast.279, f32[8,256,256]{2,1,0:T(8,128)} %fusion.122, f32[8,8,256]{2,1,0:T(8,128)S(1)} %get-tuple-element.329, ...), kind=kOutput, calls=%fused_computation.74 | convolution fusion | flops 3244294144 | bytes 15400960 | tf_op jit(solution)/shard_map/transpose(jvp(chqk,ckhp->cqhp))/dot_general | solution.py:63
  511.7 12.6 %multiply_reduce_fusion.5 = (f32[768]{0:T(1024)S(1)}, f32[2048,768]{0,1:T(8,128)}, f32[2048,768]{0,1:T(8,128)}) fusion(f32[2045,768]{0,1:T(8,128)S(1)} %bitcast.237, f32[2048]{0:T(1024)S(1)} %copy-done.56, f32[2048,768]{0,1:T(8,128)} %get-tuple-element.333, f32[2048,512]{0,1:T(8,128)} %multiply_add_fusion.2, f32[2048,128]{0,1:T(8,128)} %copy.166, ...), kind=kLoop, calls=%fused_computation.53 | loop fusion | flops 22019328 | bytes 31459328 | tf_op jit(solution)/shard_map/transpose(jvp())/reduce_sum | solution.py:36
  524.3 8.4 multiply_reduce_fusion.4
  532.7 7.4 slice_multiply_fusion.1
  549.3 10.5 %multiply_reduce_fusion.2 = (f32[768]{0:T(1024)S(1)}, f32[768]{0:T(1024)S(1)}, f32[2048,768]{0,1:T(8,128)}) fusion(f32[2048,768]{0,1:T(8,128)S(1)} %bitcast.243, f32[2048,256]{0,1:T(8,128)S(1)} %copy-done.5, f32[2048,512]{0,1:T(8,128)S(1)} %bitcast.232, f32[768]{0:T(1024)S(1)} %copy-done.75, f32[2047,768]{0,1:T(8,128)} %slice_multiply_fusion, ...), kind=kLoop, calls=%fused_computation.50 | loop fusion | flops 12581376 | bytes 37739520 | tf_op jit(solution)/shard_map/transpose(jvp())/reduce_sum | solution.py:29
  582.0 14.6 %reduce-scatter.10.cloned.1.call-done = f32[512,288]{0,1:T(8,128)} async-done(((f32[2048,288]{0,1:T(8,128)}), f32[512,288]{0,1:T(8,128)}) %reduce-scatter.10.cloned.1.call-update) | async-done | bytes 589840 | tf_op jit(solution)/shard_map/reduce_scatter | solution.py:219
  599.4 10.0 %fusion.125 = f32[1024,1024]{1,0:T(8,128)} fusion(bf16[2048,1024]{1,0:T(8,128)(2,1)} %all-gather.5.cloned.1.call-done, bf16[2048,1024]{0,1:T(8,128)(2,1)} %bitcast.270), kind=kOutput, calls=%fused_computation.248 | convolution fusion | flops 4294967296 | bytes 12582912 | tf_op jit(solution)/shard_map/dot_general | solution.py:90
  611.0 9.1 fusion.124
  621.4 8.0 fusion.106
  630.9 103.6 %all-reduce.23.cloned.1.call-done = f32[1024,288]{0,1:T(8,128)} async-done(((f32[1024,288]{0,1:T(8,128)}), f32[1024,288]{0,1:T(8,128)}) %all-reduce.23.cloned.1.call-update) | async-done | bytes 1179664 | tf_op jit(solution)/shard_map/psum | solution.py:241
  736.2 88.9 %reduce-scatter.12.cloned.1.call-done = f32[128,1024]{1,0:T(8,128)} async-done(((f32[1024,1024]{1,0:T(8,128)}), f32[128,1024]{1,0:T(8,128)}) %reduce-scatter.12.cloned.1.call-update) | async-done | bytes 524304 | tf_op jit(solution)/shard_map/reduce_scatter | solution.py:230
  827.8 71.7 %reduce-scatter.8.cloned.1.call-done = f32[512,1024]{1,0:T(8,128)} async-done(((f32[2048,1024]{1,0:T(8,128)}), f32[512,1024]{1,0:T(8,128)}) %reduce-scatter.8.cloned.1.call-update) | async-done | bytes 2097168 | tf_op jit(solution)/shard_map/reduce_scatter | solution.py:218
  902.6 40.7 %all-reduce.20 = (f32[5,2048]{1,0:T(8,128)S(1)}, f32[5,256]{1,0:T(8,128)S(1)}, f32[3,32]{1,0:T(4,128)S(1)}, f32[3072]{0:T(1024)S(1)}) all-reduce(f32[5,2048]{1,0:T(8,128)S(1)} %slice_dynamic-update-slice_fusion, f32[5,256]{1,0:T(8,128)S(1)} %pad_add_fusion.1, ...), channel_id=1, replica_groups=mesh['dp'=8,'tensor'=4] {'dp','tensor'}, use_global_device_ids=true, to_apply=%region_34.35 | all-reduce | flops 14688 | bytes 117504 | tf_op jit(solution)/shard_map/psum | solution.py:241
  945.9 28.5 %reduce-scatter.6.cloned.1.call-done = f32[512,1024]{1,0:T(8,128)} async-done(((f32[2048,1024]{1,0:T(8,128)}), f32[512,1024]{1,0:T(8,128)}) %reduce-scatter.6.cloned.1.call-update) | async-done | bytes 2097168 | tf_op jit(solution)/shard_map/reduce_scatter | solution.py:192
  (455 shorter events, 231.3 us)
Async XLA Ops:
  7.2 60.1 %all-gather.7.cloned.1.call-start = ((), (), s32[]{:S(2)}) async-start(), calls=%async_computation.6 | async-start | bytes 2359296 | tf_op jit(solution)/shard_map/all_gather | solution.py:151
  9.2 93.2 %all-gather.5.cloned.1.call-start = ((), (), s32[]{:S(2)}) async-start(), calls=%async_computation.5 | async-start | bytes 5242880 | tf_op jit(solution)/shard_map/all_gather | solution.py:149
  14.6 208.0 %all-gather.11.cloned.1.call-start = ((), (), s32[]{:S(2)}) async-start(), calls=%async_computation.9 | async-start | bytes 5242880 | tf_op jit(solution)/shard_map/all_gather | solution.py:195
  16.3 282.7 %reduce-scatter.14.cloned.1.call-start = ((), (), s32[]{:S(2)}) async-start(), calls=%async_computation.14 | async-start | bytes 2359296 | tf_op jit(solution)/shard_map/reduce_scatter | solution.py:231
  53.4 108.6 %copy-start.53 = (f32[8,256]{1,0:T(8,128)}, f32[8,256]{1,0:T(8,128)S(1)}, u32[]{:S(2)}) copy-start(f32[8,256]{1,0:T(8,128)S(1)} %get-tuple-element.353) | copy-start | bytes 24580
  230.2 110.6 %all-gather.9.cloned.1.call-start = ((), (), s32[]{:S(2)}) async-start(), calls=%async_computation.7 | async-start | bytes 1179648 | tf_op jit(solution)/shard_map/all_gather | solution.py:154
  301.2 295.4 %reduce-scatter.10.cloned.1.call-start = ((), (), s32[]{:S(2)}) async-start(), calls=%async_computation.11 | async-start | bytes 2949120 | tf_op jit(solution)/shard_map/reduce_scatter | solution.py:219
  564.3 170.2 %all-reduce.23.cloned.1.call-start = ((), (), s32[]{:S(2)}) async-start(), calls=%async_computation.13 | async-start | bytes 2359296 | tf_op jit(solution)/shard_map/psum | solution.py:241
  599.1 226.1 %reduce-scatter.12.cloned.1.call-start = ((), (), s32[]{:S(2)}) async-start(), calls=%async_computation.12 | async-start | bytes 4718592 | tf_op jit(solution)/shard_map/reduce_scatter | solution.py:230
  609.5 290.0 %reduce-scatter.8.cloned.1.call-start = ((), (), s32[]{:S(2)}) async-start(), calls=%async_computation.10 | async-start | bytes 10485760 | tf_op jit(solution)/shard_map/reduce_scatter | solution.py:218
  620.2 354.2 %reduce-scatter.6.cloned.1.call-start = ((), (), s32[]{:S(2)}) async-start(), calls=%async_computation.8 | async-start | bytes 10485760 | tf_op jit(solution)/shard_map/reduce_scatter | solution.py:192
  629.4 105.1 %copy-start.40 = (f32[128,288]{0,1:T(8,128)S(1)}, f32[128,288]{0,1:T(8,128)}, u32[]{:S(2)}) copy-start(f32[128,288]{0,1:T(8,128)} %param.34) | copy-start | bytes 442372
  629.5 105.1 %copy-start.51 = (f32[128,288]{0,1:T(8,128)S(1)}, f32[128,288]{0,1:T(8,128)}, u32[]{:S(2)}) copy-start(f32[128,288]{0,1:T(8,128)} %param.35) | copy-start | bytes 442372
  629.5 195.7 %copy-start.33 = (f32[128,1024]{1,0:T(8,128)S(1)}, f32[128,1024]{1,0:T(8,128)}, u32[]{:S(2)}) copy-start(f32[128,1024]{1,0:T(8,128)} %param.31) | copy-start | bytes 1572868
  629.5 195.7 %copy-start.42 = (f32[128,1024]{1,0:T(8,128)S(1)}, f32[128,1024]{1,0:T(8,128)}, u32[]{:S(2)}) copy-start(f32[128,1024]{1,0:T(8,128)} %param.32) | copy-start | bytes 1572868
  629.5 195.7 %copy-start.43 = (f32[128,1024]{1,0:T(8,128)S(1)}, f32[128,1024]{1,0:T(8,128)}, u32[]{:S(2)}) copy-start(f32[128,1024]{1,0:T(8,128)} %param.33) | copy-start | bytes 1572868
  629.5 269.9 %copy-start.23 = (bf16[512,1024]{1,0:T(8,128)(2,1)S(1)}, bf16[512,1024]{1,0:T(8,128)(2,1)}, u32[]{:S(2)}) copy-start(bf16[512,1024]{1,0:T(8,128)(2,1)} %param.28) | copy-start | bytes 3145732
  629.5 269.9 %copy-start.66 = (f32[1024]{0:T(1024)S(1)}, f32[1024]{0:T(1024)}, u32[]{:S(2)}) copy-start(f32[1024]{0:T(1024)} %copy-done.65) | copy-start | bytes 12292
  629.6 269.9 %copy-start.79 = (f32[512]{0:T(512)S(1)}, f32[512]{0:T(512)}, u32[]{:S(2)}) copy-start(f32[512]{0:T(512)} %copy-done.78) | copy-start | bytes 6148
  736.2 207.0 %copy-start.104 = (f32[3,8]{1,0:T(4,128)S(1)}, f32[3,8]{1,0:T(4,128)}, u32[]{:S(2)}) copy-start(f32[3,8]{1,0:T(4,128)} %param.47) | copy-start | bytes 292
  736.2 207.0 %copy-start.105 = (f32[3,8]{1,0:T(4,128)S(1)}, f32[3,8]{1,0:T(4,128)}, u32[]{:S(2)}) copy-start(f32[3,8]{1,0:T(4,128)} %param.48) | copy-start | bytes 292
  827.7 116.3 %copy-start.77 = (f32[5,256]{1,0:T(8,128)S(1)}, f32[5,256]{1,0:T(8,128)}, u32[]{:S(2)}) copy-start(f32[5,256]{1,0:T(8,128)} %param.43) | copy-start | bytes 15364
  827.7 116.3 %copy-start.90 = (f32[5,256]{1,0:T(8,128)S(1)}, f32[5,256]{1,0:T(8,128)}, u32[]{:S(2)}) copy-start(f32[5,256]{1,0:T(8,128)} %param.44) | copy-start | bytes 15364
  827.7 116.3 %copy-start.91 = (f32[5,256]{1,0:T(8,128)S(1)}, f32[5,256]{1,0:T(8,128)}, u32[]{:S(2)}) copy-start(f32[5,256]{1,0:T(8,128)} %param.45) | copy-start | bytes 15364
  827.7 116.9 %copy-start.67 = (f32[3072]{0:T(1024)S(1)}, f32[3072]{0:T(1024)}, u32[]{:S(2)}) copy-start(f32[3072]{0:T(1024)} %param.49) | copy-start | bytes 36868
  827.7 116.9 %copy-start.87 = (f32[3072]{0:T(1024)S(1)}, f32[3072]{0:T(1024)}, u32[]{:S(2)}) copy-start(f32[3072]{0:T(1024)} %param.50) | copy-start | bytes 36868
  827.7 116.9 %copy-start.88 = (f32[3072]{0:T(1024)S(1)}, f32[3072]{0:T(1024)}, u32[]{:S(2)}) copy-start(f32[3072]{0:T(1024)} %param.51) | copy-start | bytes 36868
  827.7 117.5 %copy-start.64 = (f32[5,512]{1,0:T(8,128)S(1)}, f32[5,512]{1,0:T(8,128)}, u32[]{:S(2)}) copy-start(f32[5,512]{1,0:T(8,128)} %param.40) | copy-start | bytes 30724
  827.7 117.5 %copy-start.85 = (f32[5,512]{1,0:T(8,128)S(1)}, f32[5,512]{1,0:T(8,128)}, u32[]{:S(2)}) copy-start(f32[5,512]{1,0:T(8,128)} %param.41) | copy-start | bytes 30724
  827.7 117.5 %copy-start.86 = (f32[5,512]{1,0:T(8,128)S(1)}, f32[5,512]{1,0:T(8,128)}, u32[]{:S(2)}) copy-start(f32[5,512]{1,0:T(8,128)} %param.42) | copy-start | bytes 30724
  827.7 146.6 %copy-start.84 = (f32[512]{0:T(512)S(1)}, f32[512]{0:T(512)}, u32[]{:S(2)}) copy-start(f32[512]{0:T(512)} %copy-done.83) | copy-start | bytes 6148
  827.8 146.6 %copy-start.92 = (f32[512]{0:T(512)S(1)}, f32[512]{0:T(512)}, u32[]{:S(2)}) copy-start(f32[512]{0:T(512)} %get-tuple-element.360) | copy-start | bytes 6148
  (98 other events, 1975.2 us)
Sparse Core Ops, SparseCore 0:
  10.8 56.5 all-gather.6
  68.9 33.4 all-gather.4
  103.9 34.4 all-gather.10
  230.3 68.6 reduce-scatter.13
  301.5 39.1 all-gather.8
  564.4 32.0 reduce-scatter.9
  603.4 131.0 all-reduce.22
  738.1 87.0 reduce-scatter.11
  827.9 71.4 reduce-scatter.7
  901.9 72.4 reduce-scatter.5
where the time goes:
time: 996 us; the launch traced here: 986 us
  waiting for transfers between devices  454 us (46%)
  other arithmetic  188 us (19%)
  matrix products  159 us (16%)
  blocking collectives  87.3 us (9%)
  local copies, waits for them, and re-layouts  80.4 us (8%)
  between operations  16.1 us (2%)
    psum x1, waiting for transfers between devices, shards(): lax.psum((shared_grad, d_taps[:, own_inner:], gain_grad, chan_all, head_a...  104 us
    reduce_scatter x1, waiting for transfers between devices, shards(): lax.psum_scatter(heads_grad, 'dp', scatter_dimension=0, tiled=True)  88.9 us
    reduce_scatter x1, waiting for transfers between devices, shards(): lax.psum_scatter(d_normed_part, 'tensor', scatter_dimension=0, tiled=True)  71.7 us
    reduce_scatter x1, waiting for transfers between devices, shards(): lax.psum_scatter(out_grad, 'dp', scatter_dimension=0, tiled=True)  68.8 us
    dot_general x3, matrix products, state_space(): jnp.einsum('chqk,ckhp->cqhp', mixing, values_c, precision=HIGHEST_PREC)  54.7 us
    psum x1, blocking collectives, shards(): lax.psum((shared_grad, d_taps[:, own_inner:], gain_grad, chan_all, head_a...  40.7 us
    another operation x8, other arithmetic  35.5 us
    all_gather x1, waiting for transfers between devices, shards(): gathered = lax.all_gather(normed, 'tensor', axis=0, tiled=True)  35.1 us
  transfers between devices with their start and end apart: 10, of which 9 were waited for; matrix products, arithmetic and copies ran while one was open for 18% of the time, Pallas kernels for 0%

commit v1 on v0

--- a/solution.py
+++ b/solution.py
@@ -99,6 +99,76 @@
     second_fix = 1.0 - BETA_TWO**STEP
     update = first_new / first_fix / (jnp.sqrt(second_new / second_fix) + ADAM_EPS)
     return (weight - rate * (update + decay_rate * weight), first_new, second_new)
+
+
+def swap(vals, axis, bit):
+    ways = lax.axis_size(axis)
+    return lax.ppermute(vals, axis, [(i, i ^ bit) for i in range(ways)])
+
+
+def axis_bits(axis):
+    return [1 << i for i in range(lax.axis_size(axis).bit_length() - 1)]
+
+
+def gather_rows(vals, axis, order):
+    rows = vals.shape[0]
+    ways = lax.axis_size(axis)
+    pos = lax.axis_index(axis)
+    bits = axis_bits(axis)
+    held = vals.reshape((1,) * len(bits) + vals.shape)
+    for bit in order:
+        dim = len(bits) - bit.bit_length()
+        other = swap(held, axis, bit)
+        upper = (pos & bit) != 0
+        held = jnp.concatenate(
+            [jnp.where(upper, other, held), jnp.where(upper, held, other)], axis=dim
+        )
+    return held.reshape((ways * rows,) + vals.shape[1:])
+
+
+def scatter_rows(vals, axis, order):
+    ways = lax.axis_size(axis)
+    pos = lax.axis_index(axis)
+    bits = axis_bits(axis)
+    rows = vals.shape[0] // ways
+    held = vals.reshape((2,) * len(bits) + (rows,) + vals.shape[1:])
+    for bit in order:
+        dim = len(bits) - bit.bit_length()
+        mine = (pos & bit) // bit
+        keep = lax.dynamic_slice_in_dim(held, mine, 1, dim)
+        send = lax.dynamic_slice_in_dim(held, 1 - mine, 1, dim).astype(jnp.bfloat16)
+        held = keep.astype(jnp.float32) + swap(send, axis, bit).astype(jnp.float32)
+    return held.reshape((rows,) + vals.shape[1:])
+
+
+def sum_all(vals, axis):
+    for bit in axis_bits(axis):
+        vals = vals + swap(vals, axis, bit)
+    return vals
+
+
+def gather_two(vals, axis):
+    bits = axis_bits(axis)
+    half = (vals.shape[1] // 256) * 128
+    return jnp.concatenate(
+        [
+            gather_rows(vals[:, :half], axis, bits[::-1]),
+            gather_rows(vals[:, half:], axis, bits[:1] + bits[:0:-1]),
+        ],
+        axis=1,
+    )
+
+
+def scatter_two(vals, axis):
+    bits = axis_bits(axis)
+    half = (vals.shape[1] // 256) * 128
+    return jnp.concatenate(
+        [
+            scatter_rows(vals[:, :half], axis, bits),
+            scatter_rows(vals[:, half:], axis, bits[1:] + bits[:1]),
+        ],
+        axis=1,
+    )
 
 
 def shards(
@@ -146,12 +216,13 @@
     inputs_f = tokens.astype(jnp.float32)
     norm_scale = lax.rsqrt(jnp.mean(inputs_f * inputs_f, axis=1, keepdims=True) + NORM_EPS)
     normed = (inputs_f * norm_scale * norm_gain[None, :]).astype(jnp.bfloat16)
-    gathered = lax.all_gather(normed, "tensor", axis=0, tiled=True)
-    heads_full, shared_full = (
-        lax.all_gather(w_heads.astype(jnp.bfloat16), "dp", axis=0, tiled=True),
-        lax.all_gather(w_shared.astype(jnp.bfloat16), "dp", axis=0, tiled=True),
-    )
-    out_cols = lax.all_gather(w_out.astype(jnp.bfloat16), "dp", axis=0, tiled=True)
+    gathered = gather_rows(normed, "tensor", (2, 1))
+    in_width = w_heads.shape[1]
+    in_full = gather_two(
+        jnp.concatenate([w_heads.astype(jnp.bfloat16), w_shared.astype(jnp.bfloat16)], axis=1), "dp"
+    )
+    heads_full, shared_full = in_full[:, :in_width], in_full[:, in_width:]
+    out_cols = gather_two(w_out.astype(jnp.bfloat16), "dp")
     head_cols = jnp.dot(gathered, heads_full, preferred_element_type=jnp.float32).reshape(
         group_rows, own_heads, 2, head_size
     )
@@ -189,10 +260,8 @@
     square_sum = lax.psum(jnp.sum(gated_vals * gated_vals, axis=1), "tensor")
     inv_gate = lax.rsqrt(square_sum / all_inner + NORM_EPS)[:, None]
     normal_out = (gated_vals * inv_gate * own_gain).astype(jnp.bfloat16)
-    branch = lax.psum_scatter(
-        contract_last(normal_out, out_cols), "tensor", scatter_dimension=0, tiled=True
-    )
-    masked_all = lax.all_gather(masked, "tensor", axis=0, tiled=True)
+    branch = scatter_rows(contract_last(normal_out, out_cols), "tensor", (1, 2))
+    masked_all = gather_rows(masked, "tensor", (2, 1))
     d_normal = jnp.dot(masked_all, out_cols, preferred_element_type=jnp.float32)
     weighted = d_normal * own_gain
     row_dot = lax.psum(jnp.sum(gated_vals * weighted, axis=1), "tensor")[:, None]
@@ -215,8 +284,8 @@
     d_shared_part = jnp.concatenate([d_raw[:, own_inner:], d_step_all], axis=1)
     d_normed_part = contract_last(d_cols, heads_full)
     d_normed_rows, d_shared_rows = (
-        lax.psum_scatter(d_normed_part, "tensor", scatter_dimension=0, tiled=True),
-        lax.psum_scatter(d_shared_part, "tensor", scatter_dimension=0, tiled=True),
+        scatter_rows(d_normed_part, "tensor", (1, 2)),
+        scatter_rows(d_shared_part, "tensor", (1, 2)),
     )
     d_shared_low = d_shared_rows.astype(jnp.bfloat16)
     d_normed = d_normed_rows + contract_last(d_shared_low, shared_full)
@@ -227,26 +296,37 @@
     )
     heads_grad = contract_first(gathered, d_cols)
     heads_shard, out_shard = (
-        lax.psum_scatter(heads_grad, "dp", scatter_dimension=0, tiled=True),
-        lax.psum_scatter(out_grad, "dp", scatter_dimension=0, tiled=True),
-    )
-    gain_grad = jnp.concatenate([jnp.sum(inputs_f * norm_scale * d_normed, axis=0), gate_gain_grad])
-    chan_all = lax.dynamic_update_slice_in_dim(
-        jnp.zeros((5, all_inner), jnp.float32), d_taps[:, :own_inner], tensor_pos * own_inner, 1
-    )
-    head_all = lax.dynamic_update_slice_in_dim(
-        jnp.zeros((3, all_heads), jnp.float32), d_head, tensor_pos * own_heads, 1
-    )
-    shared_grad = contract_first(normed, d_shared_low)
-    shared_sum, bc_sum, gain_sum, chan_sum, head_sum = lax.psum(
-        (shared_grad, d_taps[:, own_inner:], gain_grad, chan_all, head_all), ("dp", "tensor")
-    )
-    shared_rows = w_shared.shape[0]
-    shared_shard = lax.dynamic_slice_in_dim(
-        shared_sum, lax.axis_index("dp") * shared_rows, shared_rows, 0
-    )
-    chan_grad = lax.dynamic_slice_in_dim(chan_sum, tensor_pos * own_inner, own_inner, 1)
-    head_grad = lax.dynamic_slice_in_dim(head_sum, tensor_pos * own_heads, own_heads, 1)
+        scatter_two(heads_grad, "dp"),
+        scatter_two(out_grad, "dp"),
+    )
+    norm_gain_grad = jnp.sum(inputs_f * norm_scale * d_normed, axis=0)
+    own_sums = sum_all(
+        jnp.concatenate(
+            [
+                norm_gain_grad,
+                d_taps[:, own_inner:].reshape(-1),
+                gate_gain_grad,
+                d_taps[:, :own_inner].reshape(-1),
+                d_head.reshape(-1),
+            ]
+        ),
+        "dp",
+    )
+    shared_part = scatter_rows(
+        contract_first(normed, d_shared_low), "dp", axis_bits("dp")
+    )
+    shared_rows, shared_width = shared_part.shape
+    gain_ends = model_width + 10 * state_size
+    chan_begin = gain_ends + all_inner
+    head_begin = chan_begin + 5 * own_inner
+    ring_sums = sum_all(
+        jnp.concatenate([own_sums[:chan_begin], shared_part.reshape(-1)]), "tensor"
+    )
+    gain_sum = jnp.concatenate([ring_sums[:model_width], ring_sums[gain_ends:chan_begin]])
+    bc_sum = ring_sums[model_width:gain_ends].reshape(5, 2 * state_size)
+    shared_shard = ring_sums[chan_begin:].reshape(shared_rows, shared_width)
+    chan_grad = own_sums[chan_begin:head_begin].reshape(5, own_inner)
+    head_grad = own_sums[head_begin:].reshape(3, own_heads)
     new_heads, new_first_heads, new_second_heads = adam_step(
         w_heads, heads_shard, first_heads, second_heads, MATRIX_RATE, WEIGHT_DECAY
     )

time: 996 us -> 658 us (0.66)
  waiting for transfers between devices: 454 us -> 118 us
  blocking collectives: 87.3 us -> 12.6 us
  local copies, waits for them, and re-layouts: 80.4 us -> 125 us
  starting transfers between devices: 1.43 us -> 39.6 us
  other arithmetic: 188 us -> 215 us
  matrix products: 159 us -> 136 us
  between operations: 16.1 us -> 3.2 us
    reduce_scatter x5 -> x0, waiting for transfers between devices: 272 us -> none  [the longest x1 88.9 us: shards(): lax.psum_scatter(heads_grad, 'dp', scatter_dimension=0, tiled=True)]
    ppermute x0 -> x42, waiting for transfers between devices: none -> 118 us  [swap(): return lax.ppermute(vals, axis, [(i, i ^ bit) for i in range(ways)])]
    psum x1 -> x0, waiting for transfers between devices: 104 us -> none  [shards(): lax.psum((shared_grad, d_taps[:, own_inner:], gain_grad, chan_all, head_a...]
    all_gather x4 -> x0, waiting for transfers between devices: 78.3 us -> none  [the longest x1 35.1 us: shards(): gathered = lax.all_gather(normed, 'tensor', axis=0, tiled=True)]
    psum x1 -> x0, blocking collectives: 40.7 us -> none  [shards(): lax.psum((shared_grad, d_taps[:, own_inner:], gain_grad, chan_all, head_a...]
    ppermute x0 -> x42, starting transfers between devices: none -> 39.6 us  [swap(): return lax.ppermute(vals, axis, [(i, i ^ bit) for i in range(ways)])]
    all_gather x1 -> x0, blocking collectives: 33.7 us -> none  [shards(): lax.all_gather(w_shared.astype(jnp.bfloat16), 'dp', axis=0, tiled=True)]
    unnamed x244 -> x286, local copies, waits for them, and re-layouts: 31.8 us -> 47.5 us
  transfers between devices with their start and end apart: 10 -> 42, of which waited for: 9 -> 20; matrix products, arithmetic and copies ran while one was open for 18% -> 29% of each run, Pallas kernels for 0% -> 0%
where the time goes in v1:
time: 658 us; the launch traced here: 650 us
  other arithmetic  215 us (33%)
  matrix products  136 us (21%)
  local copies, waits for them, and re-layouts  125 us (19%)
  waiting for transfers between devices  118 us (18%)
  starting transfers between devices  39.6 us (6%)
  blocking collectives  12.6 us (2%)
    ppermute x42, waiting for transfers between devices, swap(): return lax.ppermute(vals, axis, [(i, i ^ bit) for i in range(ways)])  118 us
    dot_general x3, matrix products, state_space(): jnp.einsum('chqk,ckhp->cqhp', mixing, values_c, precision=HIGHEST_PREC)  54.8 us
    unnamed x286, local copies, waits for them, and re-layouts  47.5 us
    ppermute x42, starting transfers between devices, swap(): return lax.ppermute(vals, axis, [(i, i ^ bit) for i in range(ways)])  39.6 us
    another operation x7, other arithmetic  25.7 us
    dot_general x3, matrix products, state_space(): jnp.einsum('chk,ckn,ckhp->chpn', carry_w, in_c, values_c, precision=HIGHE...  22.6 us
    reduce_sum x2, other arithmetic, causal_conv(): conv_taps[3 - offset][None, :] * shifted * same_seq[:, None]  21.3 us
    mul x3, other arithmetic, causal_conv(): conv_taps[3 - offset][None, :] * shifted * same_seq[:, None]  16.2 us
  transfers between devices with their start and end apart: 42, of which 20 were waited for; matrix products, arithmetic and copies ran while one was open for 29% of the time, Pallas kernels for 0%

profile of v1, /device:TPU:0, one launch (start us, length us, event | category | flops | bytes accessed | tf_op | source)
XLA Modules:
  0.0 650.3 jit_solution(1599637723680099195)
XLA Ops:
  25.2 5.8 collective-permute-done.2
  40.7 13.5 %collective-permute-done.13 = bf16[2,1,2,128,256]{4,3,2,1,0:T(8,128)(2,1)S(1)} collective-permute-done((bf16[2,1,2,128,256]{4,3,2,1,0:T(8,128)(2,1)S(1)}, bf16[2,1,2,128,256]{4,3,2,1,0:T(8,128)(2,1)S(1)}, u32[]{:S(2)}, u32[]{:S(2)}) %collective-permute-start.13) | collective-permute-done | bytes 262176 | tf_op jit(solution)/shard_map/ppermute | solution.py:106
  68.4 11.2 %collective-permute-done.4 = bf16[2,2,1,128,640]{3,4,2,1,0:T(8,128)(2,1)S(1)} collective-permute-done((bf16[2,2,1,128,640]{3,4,2,1,0:T(8,128)(2,1)S(1)}, bf16[2,2,1,128,640]{3,4,2,1,0:T(8,128)(2,1)S(1)}, u32[]{:S(2)}, u32[]{:S(2)}) %collective-permute-start.4) | collective-permute-done | bytes 655392 | tf_op jit(solution)/shard_map/ppermute | solution.py:106
  114.5 11.7 %multiply_convert_fusion = (bf16[2048,768]{0,1:T(8,128)(2,1)S(1)}, f32[2048,768]{0,1:T(8,128)}) fusion(f32[2048]{0:T(1024)S(1)} %get-tuple-element.487, f32[2045,768]{0,1:T(8,128)S(1)} %fusion.26, f32[768]{0:T(1024)S(1)} %get-tuple-element.350, f32[2048]{0:T(1024)S(1)} %get-tuple-element.488, f32[2046,768]{0,1:T(8,128)} %fusion.25, ...), kind=kLoop, calls=%fused_computation.57 | loop fusion | flops 26738688 | bytes 34624512 | tf_op jit(solution)/shard_map/convert_element_type | solution.py:240
  141.6 5.2 fusion.40
  148.4 14.5 %while.34 = (s32[]{:T(128)}, f32[8,64,128]{2,1,0:T(8,128)S(1)}, f32[8,8,64,128]{3,2,1,0:T(8,128)}, f32[8,8,1,1]{1,3,2,0:T(1,128)S(1)}, f32[8,8]{1,0:T(8,128)S(1)...) while((s32[]{:T(128)}, f32[8,64,128]{2,1,0:T(8,128)S(1)}, f32[8,8,64,128]{3,2,1,0:T(8,128)}, ...), condition=%wide.region_6.7_spmd.clone, body=%wide.region_5.6_spmd.clone.sunk | while | flops 262147 | bytes 1312460 | solution.py:75
  170.8 14.9 %bitcast_add_fusion.3 = f32[8,256,8,64]{1,3,2,0:T(8,128)S(1)} fusion(f32[8,256,8,64]{1,3,2,0:T(8,128)S(1)} %fusion.139, f32[8,8,256]{2,1,0:T(8,128)S(1)} %bitcast.369, f32[8,256,256]{2,1,0:T(8,128)S(1)} %fusion.138, f32[8,8,256]{2,1,0:T(8,128)S(1)} %get-tuple-element.417, pred[8,256,256]{2,1,0:T(8,128)(4,1)S(1)} %copy-done.68, ...), kind=kOutput, calls=%fused_computation.73 | convolution fusion | flops 3244294144 | bytes 13303808 | tf_op jit(solution)/shard_map/jvp(chqk,ckhp->cqhp)/dot_general | solution.py:63
  196.2 6.0 psum.14
  212.5 5.8 multiply_reduce_fusion.8
  218.3 6.6 %psum.15 = f32[2048]{0:T(1024)S(1)} all-reduce(f32[2048]{0:T(1024)S(1)} %get-tuple-element.344), channel_id=1, replica_groups=mesh['dp'=8,'tensor'=4] {'tensor'}, use_global_device_ids=true, to_apply=%region_10.11 | all-reduce | flops 2048 | bytes 16384 | tf_op jit(solution)/shard_map/psum | solution.py:267
  224.9 8.1 %multiply_reduce_fusion.7 = (f32[512]{0:T(512)S(1)}, f32[2048,512]{0,1:T(8,128)S(1)}, bf16[2048,512]{0,1:T(8,128)(2,1)}) fusion(bf16[2048,768]{0,1:T(8,128)(2,1)} %copy-done.11, f32[2048,8,1,64]{0,3,2,1:T(8,128)} %get-tuple-element.425, f32[2048]{0:T(1024)S(1)} %psum.15, f32[2048,512]{0,1:T(8,128)} %get-tuple-element.415, f32[2048]{0:T(1024)S(1)} %get-tuple-element.480, ...), kind=kLoop, calls=%fused_computation.78 | loop fusion | flops 17825280 | bytes 21000192 | tf_op jit(solution)/shard_map/transpose(jvp())/reduce_sum | solution.py:80
  248.4 22.9 %fusion.11 = (f32[8,8,256]{2,1,0:T(8,128)}, f32[8,8,256]{2,1,0:T(8,128)}, f32[8,8,256]{2,1,0:T(8,128)}, f32[8,256,256]{2,1,0:T(8,128)}) fusion(f32[8,8,256]{2,1,0:T(8,128)S(1)} %bitcast.370, f32[8,256,256]{2,1,0:T(8,128)S(1)} %copy-done.54, f32[8,8,256]{2,1,0:T(8,128)S(1)} %get-tuple-element.417, pred[8,256,256]{2,1,0:T(8,128)(4,1)S(1)} %copy-done.69, ...), kind=kOutput, calls=%fused_computation.26 | convolution fusion | flops 3283566592 | bytes 11337728 | tf_op jit(solution)/shard_map/transpose(jvp(chqk,ckhp->cqhp))/dot_general | solution.py:63
  271.4 7.7 %fusion.67 = f32[8,256,128]{2,1,0:T(8,128)} fusion(f32[8,8,64,128]{3,2,1,0:T(8,128)S(1)} %copy-done.13, f32[8,256,8,64]{1,3,2,0:T(8,128)S(1)} %get-tuple-element.413, f32[8,256,8]{1,2,0:T(8,128)S(1)} %get-tuple-element.416), kind=kOutput, calls=%fused_computation.139 | convolution fusion | flops 1611661312 | bytes 7405568 | tf_op jit(solution)/shard_map/transpose(jvp(cqn,chpn->cqhp))/dot_general | solution.py:77
  280.7 16.1 %while.35 = (s32[]{:T(128)}, f32[8,64,128]{2,1,0:T(8,128)S(1)}, f32[8,8,64,128]{3,2,1,0:T(8,128)}, f32[8,8]{1,0:T(8,128)S(1)}, f32[8,8,64,128]{3,2,1,0:T(8,128)}...) while((s32[]{:T(128)}, f32[8,64,128]{2,1,0:T(8,128)S(1)}, ...), condition=%wide.region_14.15_spmd.clone, body=%wide.region_12.14_spmd.clone.sunk | while | flops 393212 | bytes 1573196 | solution.py:75
  296.9 10.2 %fusion.66 = f32[8,256,128]{2,1,0:T(8,128)} fusion(f32[8,8,64,128]{3,2,1,0:T(8,128)} %get-tuple-element.200, f32[8,256,8]{1,2,0:T(8,128)S(1)} %multiply_bitcast_fusion.1, bf16[8,256,8,64]{1,0,3,2:T(8,128)(2,1)} %bitcast.320), kind=kOutput, calls=%fused_computation.138 | convolution fusion | flops 1612709888 | bytes 5308416 | tf_op jit(solution)/shard_map/transpose(jvp(chk,ckn,ckhp->chpn))/dot_general | solution.py:67
  307.1 7.1 %multiply_reduce_fusion.6 = (f32[8,8,256]{2,1,0:T(8,128)S(1)}, f32[8,256,8,64]{1,3,2,0:T(8,128)}) fusion(f32[8,8,256,64]{2,0,3,1:T(8,128)S(1)} %copy-done.19, bf16[8,256,128,1]{2,1,3,0:T(8,128)(2,1)S(1)} %bitcast.332, f32[8,8,64,128]{3,2,1,0:T(8,128)} %get-tuple-element.200), kind=kOutput, calls=%fused_computation.74 | convolution fusion | flops 1612693504 | bytes 11075584 | tf_op jit(solution)/shard_map/transpose(jvp(chk,ckn,ckhp->chpn))/dot_general | solution.py:67
  326.4 17.0 %bitcast_add_fusion.2 = f32[8,256,8,64]{1,3,2,0:T(8,128)S(1)} fusion(f32[8,256,8,64]{1,3,2,0:T(8,128)} %get-tuple-element.496, f32[8,256,8]{1,2,0:T(8,128)S(1)} %multiply_bitcast_fusion.1, f32[8,8,256]{2,1,0:T(8,128)S(1)} %bitcast.371, f32[8,256,256]{2,1,0:T(8,128)} %copy-done.53, f32[8,8,256]{2,1,0:T(8,128)S(1)} %get-tuple-element.417, ...), kind=kOutput, calls=%fused_computation.64 | convolution fusion | flops 3244294144 | bytes 15400960 | tf_op jit(solution)/shard_map/transpose(jvp(chqk,ckhp->cqhp))/dot_general | solution.py:63
  350.1 6.7 %multiply_add_fusion.2 = f32[2048,512]{0,1:T(8,128)} fusion(f32[2048,512]{0,1:T(8,128)} %bitcast.324, f32[512]{0:T(512)S(1)} %mul.834, f32[2048,512]{0,1:T(8,128)S(1)} %copy-done.6, f32[2048,8,1,64]{0,3,2,1:T(8,128)S(1)} %copy-done.4), kind=kLoop, calls=%fused_computation.83 | loop fusion | flops 7340032 | bytes 16779264 | tf_op jit(solution)/shard_map/transpose(jvp())/add_any | solution.py:44
  356.8 13.2 %multiply_reduce_fusion.5 = (f32[768]{0:T(1024)S(1)}, f32[2048,768]{0,1:T(8,128)}, f32[2048,768]{0,1:T(8,128)}) fusion(f32[2045,768]{0,1:T(8,128)S(1)} %bitcast.310, f32[2048]{0:T(1024)S(1)} %get-tuple-element.487, f32[2048,768]{0,1:T(8,128)} %get-tuple-element.421, f32[2048,512]{0,1:T(8,128)} %multiply_add_fusion.2, f32[2048,128]{0,1:T(8,128)} %copy.235, ...), kind=kLoop, calls=%fused_computation.54 | loop fusion | flops 22019328 | bytes 31459328 | tf_op jit(solution)/shard_map/transpose(jvp())/reduce_sum | solution.py:36
  370.0 8.1 %multiply_reduce_fusion.4 = (f32[768]{0:T(1024)S(1)}, f32[2048,768]{0,1:T(8,128)}, f32[768]{0:T(1024)S(1)}, f32[2048,768]{0,1:T(8,128)S(1)}) fusion(f32[2046,768]{0,1:T(8,128)S(1)} %bitcast.314, f32[2048,768]{0,1:T(8,128)} %get-tuple-element.404, f32[2048]{0:T(1024)S(1)} %get-tuple-element.488, f32[2047,768]{0,1:T(8,128)S(1)} %bitcast.312, ...), kind=kLoop, calls=%fused_computation.53 | loop fusion | flops 9435648 | bytes 31470592 | tf_op jit(solution)/shard_map/transpose(jvp())/reduce_sum | solution.py:36
  378.1 7.2 %slice_multiply_fusion.1 = f32[2046,768]{0,1:T(8,128)} fusion(f32[2048,768]{0,1:T(8,128)} %get-tuple-element.406, f32[768]{0:T(1024)S(1)} %get-tuple-element.351), kind=kLoop, calls=%fused_computation.49 | loop fusion | flops 1571328 | bytes 12573696 | tf_op jit(solution)/shard_map/transpose(jvp())/mul | solution.py:36
  394.4 12.2 %multiply_reduce_fusion.2 = (f32[768]{0:T(1024)S(1)}, f32[768]{0:T(1024)S(1)}, f32[2048,768]{0,1:T(8,128)}) fusion(f32[2048,768]{0,1:T(8,128)} %get-tuple-element.404, f32[2048,256]{0,1:T(8,128)S(1)} %slice.240, f32[2048,512]{0,1:T(8,128)S(1)} %bitcast.305, f32[768]{0:T(1024)S(1)} %get-tuple-element.353, f32[2047,768]{0,1:T(8,128)} %slice_multiply_fusion, ...), kind=kLoop, calls=%fused_computation.51 | loop fusion | flops 12581376 | bytes 37739520 | tf_op jit(solution)/shard_map/transpose(jvp())/reduce_sum | solution.py:29
  421.7 6.0 fusion.141
  428.1 19.8 %reduce-window.31 = f32[8,8,2,128]{3,1,2,0:T(8,128)S(1)} reduce-window(f32[8,8,2,128]{3,1,2,0:T(8,128)S(1)} %get-tuple-element.473, f32[]{:T(128)} %constant.276.clone.1), window={size=1x1x1x128 pad=0_0x0_0x0_0x0_127}, to_apply=%region_20.21 | reduce-window | flops 2080768 | bytes 131076 | tf_op jit(solution)/shard_map/reduce-window.3
  450.8 7.1 %fusion.30 = bf16[2048,8,1,64]{0,3,2,1:T(8,128)(2,1)S(1)} fusion(f32[2048,8,1,64]{0,3,2,1:T(8,128)} %bitcast.308, f32[2048,8,1,64]{0,3,2,1:T(8,128)} %reshape.518, f32[2048,8,1,64]{0,3,2,1:T(8,128)} %bitcast.327, f32[8]{0:T(128)S(1)} %copy-done.116, f32[2048,8,2,64]{0,3,2,1:T(8,128)} %copy-done.18), kind=kLoop, calls=%fused_computation.61 | loop fusion | flops 13631488 | bytes 18874400 | tf_op jit(solution)/shard_map/transpose(jvp(jit(silu)))/add_any | solution.py:254
  460.3 7.9 %convert_element_type.233 = bf16[2,2,512,1024]{2,1,0,3:T(2,128)(2,1)} reshape(bf16[2048,8,2,64]{0,3,2,1:T(8,128)(2,1)} %maximum_convert_fusion) | data formatting | bytes 8388608 | tf_op jit(solution)/shard_map/convert_element_type | solution.py:279
  468.3 6.4 fusion.37
  526.6 5.4 collective-permute-done.40
  532.6 5.7 collective-permute-done.38
  545.9 12.2 %collective-permute-done.25 = bf16[2,1,2,128,512]{4,3,2,1,0:T(8,128)(2,1)S(1)} collective-permute-done((bf16[2,1,2,128,512]{4,3,2,1,0:T(8,128)(2,1)S(1)}, bf16[2,1,2,128,512]{4,3,2,1,0:T(8,128)(2,1)S(1)}, u32[]{:S(2)}, u32[]{:S(2)}) %collective-permute-start.25) | collective-permute-done | bytes 524320 | tf_op jit(solution)/shard_map/ppermute | solution.py:106
  572.9 21.3 %collective-permute-done.19 = bf16[1,1,512,1024]{3,2,1,0:T(8,128)(2,1)S(1)} collective-permute-done((bf16[1,1,512,1024]{3,2,1,0:T(8,128)(2,1)S(1)}, bf16[1,1,512,1024]{3,2,1,0:T(8,128)(2,1)S(1)}, u32[]{:S(2)}, u32[]{:S(2)}) %collective-permute-start.19) | collective-permute-done | bytes 1048608 | tf_op jit(solution)/shard_map/ppermute | solution.py:106
  596.1 11.9 %collective-permute-done.15 = bf16[1,1,512,1024]{3,2,1,0:T(8,128)(2,1)S(1)} collective-permute-done((bf16[1,1,512,1024]{3,2,1,0:T(8,128)(2,1)S(1)}, bf16[1,1,512,1024]{3,2,1,0:T(8,128)(2,1)S(1)}, u32[]{:S(2)}, u32[]{:S(2)}) %collective-permute-start.15) | collective-permute-done | bytes 1048608 | tf_op jit(solution)/shard_map/ppermute | solution.py:106
  (650 shorter events, 341.3 us)
Async XLA Ops:
  3.1 28.0 %collective-permute-start.5 = (bf16[1,1,1,128,672]{3,4,2,1,0:T(8,128)(2,1)S(1)}, bf16[1,1,1,128,672]{3,4,2,1,0:T(8,128)(2,1)S(1)}, u32[]{:S(2)}, u32[]{:S(2)}) collective-permute-start(bf16[1,1,1,128,672]{3,4,2,1,0:T(8,128)(2,1)S(1)} %fusion.93), channel_id=1, source_target_pairs={{0,4},{4,0},{8,12},{12,8},{16,20},{20,16},{24,28},{28,24},{1,5},{5... | collective-permute-start | bytes 516104 | tf_op jit(solution)/shard_map/ppermute | solution.py:106
  9.5 44.7 %collective-permute-start.16 = (bf16[1,1,512,1024]{3,2,1,0:T(8,128)(2,1)}, bf16[1,1,512,1024]{3,2,1,0:T(8,128)(2,1)}, u32[]{:S(2)}, u32[]{:S(2)}) collective-permute-start(bf16[1,1,512,1024]{3,2,1,0:T(8,128)(2,1)} %fusion.74), channel_id=1, source_target_pairs={{0,2},{1,3},{2,0},{3,1},{4,6},{5,7},{6,4},{7,5},{8,10},{9,11},{10,... | collective-permute-start | bytes 3145736 | tf_op jit(solution)/shard_map/ppermute | solution.py:106
  13.2 43.7 %collective-permute-start = (bf16[1,1,512,1024]{3,2,1,0:T(8,128)(2,1)}, bf16[1,1,512,1024]{3,2,1,0:T(8,128)(2,1)}, u32[]{:S(2)}, u32[]{:S(2)}) collective-permute-start(bf16[1,1,512,1024]{3,2,1,0:T(8,128)(2,1)} %fusion.87), channel_id=1, source_target_pairs={{0,2},{1,3},{2,0},{3,1},{4,6},{5,7},{6,4},{7,5},{8,10},{9,11},{10,... | collective-permute-start | bytes 3145736 | tf_op jit(solution)/shard_map/ppermute | solution.py:106
  13.8 8.2 %collective-permute-start.11 = (bf16[1,1,1,128,256]{4,3,2,1,0:T(8,128)(2,1)S(1)}, bf16[1,1,1,128,256]{4,3,2,1,0:T(8,128)(2,1)S(1)}, u32[]{:S(2)}, u32[]{:S(2)}) collective-permute-start(bf16[1,1,1,128,256]{4,3,2,1,0:T(8,128)(2,1)S(1)} %get-tuple-element.479), channel_id=1, source_target_pairs={{0,4},{4,0},{8,12},{12,8},{16,20},{20,16},{24,28},{28,24},{1,5},{5... | collective-permute-start | bytes 196616 | tf_op jit(solution)/shard_map/ppermute | solution.py:106
  13.9 8.7 %collective-permute-start.8 = (bf16[1,1,1,128,256]{4,3,2,1,0:T(8,128)(2,1)S(1)}, bf16[1,1,1,128,256]{4,3,2,1,0:T(8,128)(2,1)}, u32[]{:S(2)}, u32[]{:S(2)}) collective-permute-start(bf16[1,1,1,128,256]{4,3,2,1,0:T(8,128)(2,1)S(1)} %get-tuple-element.478), channel_id=1, source_target_pairs={{0,16},{4,20},{8,24},{12,28},{16,0},{20,4},{24,8},{28,12},{1,17},{... | collective-permute-start | bytes 196616 | tf_op jit(solution)/shard_map/ppermute | solution.py:106
  22.0 9.0 %collective-permute-start.2 = (bf16[1,1,1,128,640]{3,4,2,1,0:T(8,128)(2,1)S(1)}, bf16[1,1,1,128,640]{3,4,2,1,0:T(8,128)(2,1)S(1)}, u32[]{:S(2)}, u32[]{:S(2)}) collective-permute-start(bf16[1,1,1,128,640]{3,4,2,1,0:T(8,128)(2,1)S(1)} %slice_bitcast_fusion), channel_id=1, source_target_pairs={{0,16},{4,20},{8,24},{12,28},{16,0},{20,4},{24,8},{28,12},{1,17},{... | collective-permute-start | bytes 491528 | tf_op jit(solution)/shard_map/ppermute | solution.py:106
  23.5 9.5 %collective-permute-start.9 = (bf16[2,1,1,128,256]{4,3,2,1,0:T(8,128)(2,1)S(1)}, bf16[2,1,1,128,256]{4,3,2,1,0:T(8,128)(2,1)S(1)}, u32[]{:S(2)}, u32[]{:S(2)}) collective-permute-start(bf16[2,1,1,128,256]{4,3,2,1,0:T(8,128)(2,1)S(1)} %pad_maximum_fusion.25), channel_id=1, source_target_pairs={{0,8},{4,12},{8,0},{12,4},{16,24},{20,28},{24,16},{28,20},{1,9},{5... | collective-permute-start | bytes 393224 | tf_op jit(solution)/shard_map/ppermute | solution.py:106
  31.0 6.9 %collective-permute-start.12 = (bf16[1,1,2,128,256]{4,3,2,1,0:T(8,128)(2,1)S(1)}, bf16[1,1,2,128,256]{4,3,2,1,0:T(8,128)(2,1)S(1)}, u32[]{:S(2)}, u32[]{:S(2)}) collective-permute-start(bf16[1,1,2,128,256]{4,3,2,1,0:T(8,128)(2,1)S(1)} %pad_maximum_fusion.26), channel_id=1, source_target_pairs={{0,16},{4,20},{8,24},{12,28},{16,0},{20,4},{24,8},{28,12},{1,17},{... | collective-permute-start | bytes 393224 | tf_op jit(solution)/shard_map/ppermute | solution.py:106
  31.1 31.6 %collective-permute-start.3 = (bf16[2,1,1,128,640]{3,4,2,1,0:T(8,128)(2,1)S(1)}, bf16[2,1,1,128,640]{3,4,2,1,0:T(8,128)(2,1)S(1)}, u32[]{:S(2)}, u32[]{:S(2)}) collective-permute-start(bf16[2,1,1,128,640]{3,4,2,1,0:T(8,128)(2,1)S(1)} %pad_maximum_fusion.19), channel_id=1, source_target_pairs={{0,8},{4,12},{8,0},{12,4},{16,24},{20,28},{24,16},{28,20},{1,9},{5... | collective-permute-start | bytes 983048 | tf_op jit(solution)/shard_map/ppermute | solution.py:106
  33.0 7.2 %collective-permute-start.10 = (bf16[2,2,1,128,256]{4,3,2,1,0:T(8,128)(2,1)S(1)}, bf16[2,2,1,128,256]{4,3,2,1,0:T(8,128)(2,1)S(1)}, u32[]{:S(2)}, u32[]{:S(2)}) collective-permute-start(bf16[2,2,1,128,256]{4,3,2,1,0:T(8,128)(2,1)S(1)} %pad_maximum_fusion.20), channel_id=1, source_target_pairs={{0,4},{4,0},{8,12},{12,8},{16,20},{20,16},{24,28},{28,24},{1,5},{5... | collective-permute-start | bytes 786440 | tf_op jit(solution)/shard_map/ppermute | solution.py:106
  37.9 16.3 %collective-permute-start.13 = (bf16[2,1,2,128,256]{4,3,2,1,0:T(8,128)(2,1)S(1)}, bf16[2,1,2,128,256]{4,3,2,1,0:T(8,128)(2,1)S(1)}, u32[]{:S(2)}, u32[]{:S(2)}) collective-permute-start(bf16[2,1,2,128,256]{4,3,2,1,0:T(8,128)(2,1)S(1)} %pad_maximum_fusion.21), channel_id=1, source_target_pairs={{0,8},{4,12},{8,0},{12,4},{16,24},{20,28},{24,16},{28,20},{1,9},{5... | collective-permute-start | bytes 786440 | tf_op jit(solution)/shard_map/ppermute | solution.py:106
  40.3 23.0 %collective-permute-start.6 = (bf16[1,1,2,128,672]{3,4,2,1,0:T(8,128)(2,1)S(1)}, bf16[1,1,2,128,672]{3,4,2,1,0:T(8,128)(2,1)S(1)}, u32[]{:S(2)}, u32[]{:S(2)}) collective-permute-start(bf16[1,1,2,128,672]{3,4,2,1,0:T(8,128)(2,1)S(1)} %pad_maximum_fusion.18), channel_id=1, source_target_pairs={{0,16},{4,20},{8,24},{12,28},{16,0},{20,4},{24,8},{28,12},{1,17},{... | collective-permute-start | bytes 1032200 | tf_op jit(solution)/shard_map/ppermute | solution.py:106
  61.5 32.0 %collective-permute-start.1 = (bf16[2,1,512,1024]{3,2,1,0:T(8,128)(2,1)}, bf16[2,1,512,1024]{3,2,1,0:T(8,128)(2,1)}, u32[]{:S(2)}, u32[]{:S(2)}) collective-permute-start(bf16[2,1,512,1024]{3,2,1,0:T(8,128)(2,1)} %pad_maximum_fusion.5), channel_id=1, source_target_pairs={{0,1},{1,0},{2,3},{3,2},{4,5},{5,4},{6,7},{7,6},{8,9},{9,8},{10,11... | collective-permute-start | bytes 6291464 | tf_op jit(solution)/shard_map/ppermute | solution.py:106
  62.8 16.8 %collective-permute-start.4 = (bf16[2,2,1,128,640]{3,4,2,1,0:T(8,128)(2,1)S(1)}, bf16[2,2,1,128,640]{3,4,2,1,0:T(8,128)(2,1)S(1)}, u32[]{:S(2)}, u32[]{:S(2)}) collective-permute-start(bf16[2,2,1,128,640]{3,4,2,1,0:T(8,128)(2,1)S(1)} %pad_maximum_fusion.14), channel_id=1, source_target_pairs={{0,4},{4,0},{8,12},{12,8},{16,20},{20,16},{24,28},{28,24},{1,5},{5... | collective-permute-start | bytes 1966088 | tf_op jit(solution)/shard_map/ppermute | solution.py:106
  64.2 17.5 %collective-permute-start.7 = (bf16[2,1,2,128,672]{3,4,2,1,0:T(8,128)(2,1)}, bf16[2,1,2,128,672]{3,4,2,1,0:T(8,128)(2,1)}, u32[]{:S(2)}, u32[]{:S(2)}) collective-permute-start(bf16[2,1,2,128,672]{3,4,2,1,0:T(8,128)(2,1)} %pad_maximum_fusion.11), channel_id=1, source_target_pairs={{0,8},{4,12},{8,0},{12,4},{16,24},{20,28},{24,16},{28,20},{1,9},{5... | collective-permute-start | bytes 2064392 | tf_op jit(solution)/shard_map/ppermute | solution.py:106
  68.4 137.9 %collective-permute-start.17 = (bf16[2,1,512,1024]{3,2,1,0:T(8,128)(2,1)}, bf16[2,1,512,1024]{3,2,1,0:T(8,128)(2,1)}, u32[]{:S(2)}, u32[]{:S(2)}) collective-permute-start(bf16[2,1,512,1024]{3,2,1,0:T(8,128)(2,1)} %pad_maximum_fusion.6), channel_id=1, source_target_pairs={{0,1},{1,0},{2,3},{3,2},{4,5},{5,4},{6,7},{7,6},{8,9},{9,8},{10,11... | collective-permute-start | bytes 6291464 | tf_op jit(solution)/shard_map/ppermute | solution.py:106
  479.7 83.0 %collective-permute-start.18 = (bf16[2,1,512,1024]{3,2,1,0:T(8,128)(2,1)}, bf16[2,1,512,1024]{3,2,1,0:T(8,128)(2,1)}, u32[]{:S(2)}, u32[]{:S(2)}) collective-permute-start(bf16[2,1,512,1024]{3,2,1,0:T(8,128)(2,1)} %dynamic-slice_convert_fusion), channel_id=1, source_target_pairs={{0,1},{1,0},{2,3},{3,2},{4,5},{5,4},{6,7},{7,6},{8,9},{9,8},{10,11... | collective-permute-start | bytes 6291464 | tf_op jit(solution)/shard_map/ppermute | solution.py:106
  489.2 71.0 %collective-permute-start.20 = (bf16[2,1,512,288]{2,3,1,0:T(8,128)(2,1)S(1)}, bf16[2,1,512,288]{2,3,1,0:T(8,128)(2,1)}, u32[]{:S(2)}, u32[]{:S(2)}) collective-permute-start(bf16[2,1,512,288]{2,3,1,0:T(8,128)(2,1)S(1)} %copy.263), channel_id=1, source_target_pairs={{0,1},{1,0},{2,3},{3,2},{4,5},{5,4},{6,7},{7,6},{8,9},{9,8},{10,11... | collective-permute-start | bytes 1769480 | tf_op jit(solution)/shard_map/ppermute | solution.py:106
  495.3 71.5 %collective-permute-start.14 = (bf16[2,1,512,1024]{3,2,1,0:T(8,128)(2,1)}, bf16[2,1,512,1024]{3,2,1,0:T(8,128)(2,1)}, u32[]{:S(2)}, u32[]{:S(2)}) collective-permute-start(bf16[2,1,512,1024]{3,2,1,0:T(8,128)(2,1)} %dynamic-slice_convert_fusion.1), channel_id=1, source_target_pairs={{0,1},{1,0},{2,3},{3,2},{4,5},{5,4},{6,7},{7,6},{8,9},{9,8},{10,11... | collective-permute-start | bytes 6291464 | tf_op jit(solution)/shard_map/ppermute | solution.py:106
  499.6 17.3 %collective-permute-start.36 = (bf16[2,2,1,128,256]{4,3,2,1,0:T(8,128)(2,1)}, bf16[2,2,1,128,256]{4,3,2,1,0:T(8,128)(2,1)}, u32[]{:S(2)}, u32[]{:S(2)}) collective-permute-start(bf16[2,2,1,128,256]{4,3,2,1,0:T(8,128)(2,1)} %dynamic-slice_convert_fusion.9), channel_id=1, source_target_pairs={{0,4},{4,0},{8,12},{12,8},{16,20},{20,16},{24,28},{28,24},{1,5},{5... | collective-permute-start | bytes 786440 | tf_op jit(solution)/shard_map/ppermute | solution.py:106
  501.8 16.9 %collective-permute-start.39 = (bf16[2,1,2,128,256]{4,3,2,1,0:T(8,128)(2,1)}, bf16[2,1,2,128,256]{4,3,2,1,0:T(8,128)(2,1)S(1)}, u32[]{:S(2)}, u32[]{:S(2)}) collective-permute-start(bf16[2,1,2,128,256]{4,3,2,1,0:T(8,128)(2,1)} %dynamic-slice_convert_fusion.8), channel_id=1, source_target_pairs={{0,8},{4,12},{8,0},{12,4},{16,24},{20,28},{24,16},{28,20},{1,9},{5... | collective-permute-start | bytes 786440 | tf_op jit(solution)/shard_map/ppermute | solution.py:106
  516.9 26.7 %collective-permute-start.22 = (bf16[2,2,1,128,512]{4,3,2,1,0:T(8,128)(2,1)}, bf16[2,2,1,128,512]{4,3,2,1,0:T(8,128)(2,1)S(1)}, u32[]{:S(2)}, u32[]{:S(2)}) collective-permute-start(bf16[2,2,1,128,512]{4,3,2,1,0:T(8,128)(2,1)} %dynamic-slice_convert_fusion.5), channel_id=1, source_target_pairs={{0,4},{4,0},{8,12},{12,8},{16,20},{20,16},{24,28},{28,24},{1,5},{5... | collective-permute-start | bytes 1572872 | tf_op jit(solution)/shard_map/ppermute | solution.py:106
  524.0 8.0 %collective-permute-start.40 = (bf16[1,1,2,128,256]{4,3,2,1,0:T(8,128)(2,1)S(1)}, bf16[1,1,2,128,256]{4,3,2,1,0:T(8,128)(2,1)S(1)}, u32[]{:S(2)}, u32[]{:S(2)}) collective-permute-start(bf16[1,1,2,128,256]{4,3,2,1,0:T(8,128)(2,1)S(1)} %dynamic-slice_convert_fusion.13), channel_id=1, source_target_pairs={{0,16},{4,20},{8,24},{12,28},{16,0},{20,4},{24,8},{28,12},{1,17},{... | collective-permute-start | bytes 393224 | tf_op jit(solution)/shard_map/ppermute | solution.py:106
  542.5 15.6 %collective-permute-start.25 = (bf16[2,1,2,128,512]{4,3,2,1,0:T(8,128)(2,1)S(1)}, bf16[2,1,2,128,512]{4,3,2,1,0:T(8,128)(2,1)S(1)}, u32[]{:S(2)}, u32[]{:S(2)}) collective-permute-start(bf16[2,1,2,128,512]{4,3,2,1,0:T(8,128)(2,1)S(1)} %dynamic-slice_convert_fusion.4), channel_id=1, source_target_pairs={{0,8},{4,12},{8,0},{12,4},{16,24},{20,28},{24,16},{28,20},{1,9},{5... | collective-permute-start | bytes 1572872 | tf_op jit(solution)/shard_map/ppermute | solution.py:106
  543.8 27.0 %collective-permute-start.23 = (bf16[2,1,1,128,512]{4,3,2,1,0:T(8,128)(2,1)S(1)}, bf16[2,1,1,128,512]{4,3,2,1,0:T(8,128)(2,1)S(1)}, u32[]{:S(2)}, u32[]{:S(2)}) collective-permute-start(bf16[2,1,1,128,512]{4,3,2,1,0:T(8,128)(2,1)S(1)} %dynamic-slice_convert_fusion.11), channel_id=1, source_target_pairs={{0,8},{4,12},{8,0},{12,4},{16,24},{20,28},{24,16},{28,20},{1,9},{5... | collective-permute-start | bytes 786440 | tf_op jit(solution)/shard_map/ppermute | solution.py:106
  558.3 13.7 %collective-permute-start.26 = (bf16[1,1,2,128,512]{4,3,2,1,0:T(8,128)(2,1)S(1)}, bf16[1,1,2,128,512]{4,3,2,1,0:T(8,128)(2,1)S(1)}, u32[]{:S(2)}, u32[]{:S(2)}) collective-permute-start(bf16[1,1,2,128,512]{4,3,2,1,0:T(8,128)(2,1)S(1)} %dynamic-slice_convert_fusion.10), channel_id=1, source_target_pairs={{0,16},{4,20},{8,24},{12,28},{16,0},{20,4},{24,8},{28,12},{1,17},{... | collective-permute-start | bytes 786440 | tf_op jit(solution)/shard_map/ppermute | solution.py:106
  561.8 11.2 %collective-permute-start.21 = (bf16[1,1,512,288]{2,3,1,0:T(8,128)(2,1)S(1)}, bf16[1,1,512,288]{2,3,1,0:T(8,128)(2,1)S(1)}, u32[]{:S(2)}, u32[]{:S(2)}) collective-permute-start(bf16[1,1,512,288]{2,3,1,0:T(8,128)(2,1)S(1)} %dynamic-slice_convert_fusion.7), channel_id=1, source_target_pairs={{0,2},{1,3},{2,0},{3,1},{4,6},{5,7},{6,4},{7,5},{8,10},{9,11},{10,... | collective-permute-start | bytes 884744 | tf_op jit(solution)/shard_map/ppermute | solution.py:106
  565.8 28.5 %collective-permute-start.19 = (bf16[1,1,512,1024]{3,2,1,0:T(8,128)(2,1)S(1)}, bf16[1,1,512,1024]{3,2,1,0:T(8,128)(2,1)S(1)}, u32[]{:S(2)}, u32[]{:S(2)}) collective-permute-start(bf16[1,1,512,1024]{3,2,1,0:T(8,128)(2,1)S(1)} %dynamic-slice_convert_fusion.2), channel_id=1, source_target_pairs={{0,2},{1,3},{2,0},{3,1},{4,6},{5,7},{6,4},{7,5},{8,10},{9,11},{10,... | collective-permute-start | bytes 3145736 | tf_op jit(solution)/shard_map/ppermute | solution.py:106
  569.6 38.4 %collective-permute-start.15 = (bf16[1,1,512,1024]{3,2,1,0:T(8,128)(2,1)S(1)}, bf16[1,1,512,1024]{3,2,1,0:T(8,128)(2,1)S(1)}, u32[]{:S(2)}, u32[]{:S(2)}) collective-permute-start(bf16[1,1,512,1024]{3,2,1,0:T(8,128)(2,1)S(1)} %dynamic-slice_convert_fusion.3), channel_id=1, source_target_pairs={{0,2},{1,3},{2,0},{3,1},{4,6},{5,7},{6,4},{7,5},{8,10},{9,11},{10,... | collective-permute-start | bytes 3145736 | tf_op jit(solution)/shard_map/ppermute | solution.py:106
  570.9 50.7 %collective-permute-start.24 = (bf16[1,1,1,128,512]{4,3,2,1,0:T(8,128)(2,1)S(1)}, bf16[1,1,1,128,512]{4,3,2,1,0:T(8,128)(2,1)}, u32[]{:S(2)}, u32[]{:S(2)}) collective-permute-start(bf16[1,1,1,128,512]{4,3,2,1,0:T(8,128)(2,1)S(1)} %dynamic-slice_convert_fusion.16), channel_id=1, source_target_pairs={{0,16},{4,20},{8,24},{12,28},{16,0},{20,4},{24,8},{28,12},{1,17},{... | collective-permute-start | bytes 393224 | tf_op jit(solution)/shard_map/ppermute | solution.py:106
  572.2 54.9 %collective-permute-start.27 = (bf16[1,1,1,128,512]{4,3,2,1,0:T(8,128)(2,1)S(1)}, bf16[1,1,1,128,512]{4,3,2,1,0:T(8,128)(2,1)}, u32[]{:S(2)}, u32[]{:S(2)}) collective-permute-start(bf16[1,1,1,128,512]{4,3,2,1,0:T(8,128)(2,1)S(1)} %dynamic-slice_convert_fusion.15), channel_id=1, source_target_pairs={{0,4},{4,0},{8,12},{12,8},{16,20},{20,16},{24,28},{28,24},{1,5},{5... | collective-permute-start | bytes 393224 | tf_op jit(solution)/shard_map/ppermute | solution.py:106
  614.3 12.0 %collective-permute-start.31 = (bf16[2,2,1,128,288]{3,4,2,1,0:T(8,128)(2,1)S(1)}, bf16[2,2,1,128,288]{3,4,2,1,0:T(8,128)(2,1)S(1)}, u32[]{:S(2)}, u32[]{:S(2)}) collective-permute-start(bf16[2,2,1,128,288]{3,4,2,1,0:T(8,128)(2,1)S(1)} %dynamic-slice_convert_fusion.6), channel_id=1, source_target_pairs={{0,4},{4,0},{8,12},{12,8},{16,20},{20,16},{24,28},{28,24},{1,5},{5... | collective-permute-start | bytes 884744 | tf_op jit(solution)/shard_map/ppermute | solution.py:106
  (145 other events, 2366.8 us)

commit v2 on v1

--- a/solution.py
+++ b/solution.py
@@ -1,6 +1,8 @@
 import jax
 import jax.numpy as jnp
 from jax import lax
+from jax.experimental import pallas as pl
+from jax.experimental.pallas import tpu as pltpu
 from jax.sharding import PartitionSpec as P
 
 SPAN = 256
@@ -25,59 +27,404 @@
     return jnp.sum((positions[:, None] >= seq_ends[None, :]).astype(jnp.int32), axis=1)
 
 
-def causal_conv(raw_vals, conv_taps, seq_ids):
-    result = conv_taps[4][None, :] + conv_taps[3][None, :] * raw_vals
+LANES = 128
+KERNEL_VMEM = 56 * 1024 * 1024
+
+
+def silu_slope(vals, sig):
+    return sig * (1.0 + vals * (1.0 - sig))
+
+
+def split_halves(vals):
+    high = vals.astype(jnp.bfloat16)
+    rest = (vals - high.astype(jnp.float32)).astype(jnp.bfloat16)
+    return jnp.concatenate([high, rest], axis=1)
+
+
+def mm(left, right):
+    return jnp.dot(left, right, preferred_element_type=jnp.float32)
+
+
+def ids_at(positions, ends_ref):
+    ids = jnp.zeros_like(positions)
+    for slot in range(ends_ref.shape[0]):
+        ids = ids + jnp.where(positions >= ends_ref[slot], 1, 0)
+    return ids
+
+
+def block_setup(block, ends_ref, step_raw, head_ref, spread_ref):
+    begin = block * SPAN
+    col = lax.broadcasted_iota(jnp.int32, (SPAN, 1), 0)
+    row = lax.broadcasted_iota(jnp.int32, (1, SPAN), 1)
+    id_col = ids_at(col + begin, ends_ref)
+    id_row = ids_at(row + begin, ends_ref)
+    prior, last = jnp.int32(0), jnp.int32(0)
+    for slot in range(ends_ref.shape[0]):
+        prior = prior + jnp.where(begin - 1 >= ends_ref[slot], 1, 0)
+        last = last + jnp.where(begin + SPAN - 1 >= ends_ref[slot], 1, 0)
+    prior = jnp.where(block == 0, -1, prior)
+    pre_step = step_raw + head_ref[1:2, :]
+    step = jnp.maximum(pre_step, 0.0) + jnp.log1p(jnp.exp(-jnp.abs(pre_step)))
+    decay = -jnp.exp(head_ref[0:1, :]) * step
+    lower = jnp.where(col >= row, 1.0, 0.0)
+    total = jnp.dot(
+        lower, decay, precision=HIGHEST_PREC, preferred_element_type=jnp.float32
+    )
+    tail = total[SPAN - 1 : SPAN, :]
+    reach = jnp.exp(total) * jnp.where(id_col == prior, 1.0, 0.0)
+    leave = jnp.exp(tail - total) * jnp.where(id_col == last, 1.0, 0.0)
+    through = jnp.exp(tail) * jnp.where(last == prior, 1.0, 0.0)
+    stacked = jnp.concatenate([step, reach, leave, jnp.broadcast_to(through, (8, LANES))], axis=0)
+    spread = mm(split_halves(stacked), spread_ref[...])
+    return (
+        col,
+        row,
+        id_col,
+        id_row,
+        pre_step,
+        decay,
+        total,
+        spread[:SPAN],
+        spread[SPAN : 2 * SPAN],
+        spread[2 * SPAN : 3 * SPAN],
+        spread[3 * SPAN : 3 * SPAN + 1],
+    )
+
+
+def forward_kernel(
+    ends_ref,
+    rows_ref,
+    weight_ref,
+    taps_ref,
+    head_ref,
+    skip_ref,
+    spread_ref,
+    gate_ref,
+    raw_ref,
+    pre_ref,
+    conv_ref,
+    step_ref,
+    ssd_ref,
+    gated_ref,
+    state_ref,
+    ext_ref,
+    carry_ref,
+):
+    block = pl.program_id(0)
+    inner = gate_ref.shape[1]
+    width = raw_ref.shape[1]
+    states = (width - inner) // 2
+
+    @pl.when(block == 0)
+    def _():
+        carry_ref[...] = jnp.zeros_like(carry_ref)
+        ext_ref[...] = jnp.zeros_like(ext_ref)
+
+    cols = mm(rows_ref[...], weight_ref[...])
+    gate = cols[:, :inner]
+    raw = cols[:, inner : inner + width]
+    step_raw = cols[:, inner + width :]
+    gate_ref[...] = gate
+    raw_ref[...] = raw
+    step_ref[...] = step_raw
+    (col, row, id_col, id_row, _, _, total, step_x, reach_x, leave_x, through_x) = block_setup(
+        block, ends_ref, step_raw, head_ref, spread_ref
+    )
+    ext_ref[0:8, :] = ext_ref[SPAN : SPAN + 8, :]
+    ext_ref[8 : SPAN + 8, :] = raw
+    pre = taps_ref[4:5, :] + taps_ref[3:4, :] * raw
     for offset in range(1, 4):
-        shifted = jnp.concatenate(
-            [jnp.zeros((offset, raw_vals.shape[1]), raw_vals.dtype), raw_vals[:-offset]], axis=0
+        same = jnp.where(ids_at(col + block * SPAN - offset, ends_ref) == id_col, 1.0, 0.0)
+        shifted = ext_ref[8 - offset : SPAN + 8 - offset, :]
+        pre = pre + taps_ref[3 - offset : 4 - offset, :] * shifted * same
+    pre_ref[...] = pre
+    conv = (pre * lax.logistic(pre)).astype(jnp.bfloat16)
+    conv_ref[...] = conv
+    values = conv[:, :inner].astype(jnp.float32)
+    in_maps = conv[:, inner : inner + states]
+    out_maps = conv[:, inner + states :]
+    stepped = (values * step_x).astype(jnp.bfloat16)
+    total_rows = total.T
+    allowed = (id_col == id_row) & (col >= row)
+    inner_prod = contract_last(out_maps, in_maps)
+    low_lane = lax.broadcasted_iota(jnp.int32, (1, LANES), 1) < LANES // 2
+    state = carry_ref[...]
+    state_ref[0] = state
+    carried = reach_x * mm(out_maps, state.astype(jnp.bfloat16))
+    for pair in range(inner // LANES):
+        lanes = slice(pair * LANES, (pair + 1) * LANES)
+        parts = []
+        for head in (2 * pair, 2 * pair + 1):
+            gap = total[:, head : head + 1] - total_rows[head : head + 1, :]
+            kernel = jnp.exp(jnp.where(allowed, gap, -1e30))
+            parts.append(mm((kernel * inner_prod).astype(jnp.bfloat16), stepped[:, lanes]))
+        local = jnp.where(low_lane, parts[0], parts[1])
+        ssd = local + carried[:, lanes] + skip_ref[:, lanes] * values[:, lanes]
+        ssd_ref[:, lanes] = ssd
+        gated_ref[:, lanes] = ssd * (gate[:, lanes] * lax.logistic(gate[:, lanes]))
+    leaving = (leave_x * stepped.astype(jnp.float32)).astype(jnp.bfloat16)
+    carry_ref[...] = through_x * state + contract_first(in_maps, leaving)
+
+
+def backward_kernel(
+    ends_ref,
+    stat_ref,
+    normal_ref,
+    gate_ref,
+    raw_ref,
+    pre_ref,
+    conv_ref,
+    step_ref,
+    ssd_ref,
+    state_ref,
+    next_ref,
+    taps_ref,
+    head_ref,
+    skip_ref,
+    gain_ref,
+    spread_ref,
+    group_ref,
+    cols_ref,
+    shared_ref,
+    taps_grad_ref,
+    inner_grad_ref,
+    head_grad_ref,
+    ext_ref,
+    carry_ref,
+):
+    place = pl.program_id(0)
+    block = pl.num_programs(0) - 1 - place
+    inner = gate_ref.shape[1]
+    width = raw_ref.shape[1]
+    states = (width - inner) // 2
+
+    @pl.when(place == 0)
+    def _():
+        carry_ref[...] = jnp.zeros_like(carry_ref)
+        ext_ref[...] = jnp.zeros_like(ext_ref)
+        taps_grad_ref[...] = jnp.zeros_like(taps_grad_ref)
+        inner_grad_ref[...] = jnp.zeros_like(inner_grad_ref)
+        head_grad_ref[...] = jnp.zeros_like(head_grad_ref)
+
+    step_raw = step_ref[...]
+    (col, row, id_col, id_row, pre_step, decay, total, step_x, reach_x, leave_x, through_x) = (
+        block_setup(block, ends_ref, step_raw, head_ref, spread_ref)
+    )
+    inv_gate, pull = stat_ref[:, 0:1], stat_ref[:, 1:2]
+    d_normal = normal_ref[...]
+    gate = gate_ref[...]
+    ssd = ssd_ref[...]
+    sig = lax.logistic(gate)
+    silu = gate * sig
+    gated = ssd * silu
+    d_gated = inv_gate * (gain_ref[...] * d_normal) - gated * pull
+    d_ssd = d_gated * silu
+    cols_ref[:, :inner] = (d_gated * ssd * silu_slope(gate, sig)).astype(jnp.bfloat16)
+    d_low = d_ssd.astype(jnp.bfloat16)
+    d_low_f = d_low.astype(jnp.float32)
+    conv = conv_ref[...]
+    values = conv[:, :inner].astype(jnp.float32)
+    in_maps = conv[:, inner : inner + states]
+    out_maps = conv[:, inner + states :]
+    inner_grad_ref[0:1, :] += jnp.sum(gated * inv_gate * d_normal, axis=0, keepdims=True)
+    inner_grad_ref[1:2, :] += jnp.sum(values * d_ssd, axis=0, keepdims=True)
+    stepped = (values * step_x).astype(jnp.bfloat16)
+    stepped_f = stepped.astype(jnp.float32)
+    total_rows = total.T
+    allowed = (id_col == id_row) & (row >= col)
+    inner_prod = contract_last(in_maps, out_maps)
+    low_lane = lax.broadcasted_iota(jnp.int32, (1, LANES), 1) < LANES // 2
+    d_inner = jnp.zeros((SPAN, SPAN), jnp.float32)
+    d_stepped = []
+    for pair in range(inner // LANES):
+        lanes = slice(pair * LANES, (pair + 1) * LANES)
+        d_pair = d_low[:, lanes]
+        parts = []
+        for head in (2 * pair, 2 * pair + 1):
+            gap = total_rows[head : head + 1, :] - total[:, head : head + 1]
+            kernel = jnp.exp(jnp.where(allowed, gap, -1e30))
+            parts.append(mm((kernel * inner_prod).astype(jnp.bfloat16), d_pair))
+            own = low_lane if head % 2 == 0 else jnp.logical_not(low_lane)
+            own_stepped = jnp.where(own, stepped_f[:, lanes], 0.0).astype(jnp.bfloat16)
+            d_inner = d_inner + contract_last(own_stepped, d_pair) * kernel
+        d_stepped.append(jnp.where(low_lane, parts[0], parts[1]))
+    d_state = carry_ref[...]
+    d_state_low = d_state.astype(jnp.bfloat16)
+    d_stepped = jnp.concatenate(d_stepped, axis=1) + leave_x * mm(in_maps, d_state_low)
+    d_values = step_x * d_stepped + skip_ref[...] * d_ssd
+    pulls = d_low_f * (ssd - skip_ref[...] * values) - stepped_f * d_stepped
+    ends = jnp.sum(next_ref[0] * d_state, axis=0, keepdims=True)
+    grouped = mm(
+        split_halves(
+            jnp.concatenate(
+                [pulls, values * d_stepped, jnp.broadcast_to(ends, (8, inner))], axis=0
+            )
+        ),
+        group_ref[...],
+    )
+    upper = jnp.where(row >= col, 1.0, 0.0)
+    d_decay = (
+        jnp.dot(
+            upper, grouped[:SPAN], precision=HIGHEST_PREC, preferred_element_type=jnp.float32
         )
-        shifted_ids = jnp.concatenate([jnp.full((offset,), -1, jnp.int32), seq_ids[:-offset]])
-        same_seq = (shifted_ids == seq_ids).astype(raw_vals.dtype)
-        result = result + conv_taps[3 - offset][None, :] * shifted * same_seq[:, None]
-    return result
-
-
-def state_space(values, in_maps, out_maps, log_decay, step_size, seq_ids, skip_gain):
-    seq_rows, head_count, head_size = values.shape
-    state_size = in_maps.shape[1]
-    blocks = seq_rows // SPAN
-    values_c = values.reshape(blocks, SPAN, head_count, head_size)
-    in_c = in_maps.reshape(blocks, SPAN, state_size)
-    out_c = out_maps.reshape(blocks, SPAN, state_size)
-    decay_c = jnp.transpose(
-        jnp.cumsum(log_decay.reshape(blocks, SPAN, head_count), axis=1), (0, 2, 1)
-    )
-    step_c = jnp.transpose(step_size.reshape(blocks, SPAN, head_count), (0, 2, 1))
-    ids_c = seq_ids.reshape(blocks, SPAN)
-    last_ids = ids_c[:, -1]
-    prior_ids = jnp.concatenate([jnp.full((1,), -1, jnp.int32), last_ids[:-1]])
-    positions = jnp.arange(SPAN, dtype=jnp.int32)
-    allowed = (ids_c[:, :, None] == ids_c[:, None, :]) & (positions[:, None] >= positions[None, :])[
-        None
-    ]
-    allowed = allowed[:, None, :, :]
-    spread = decay_c[:, :, :, None] - decay_c[:, :, None, :]
-    kernel = jnp.where(allowed, jnp.exp(jnp.where(allowed, spread, 0.0)), 0.0)
-    inner_prod = jnp.einsum("cqn,ckn->cqk", out_c, in_c, precision=HIGHEST_PREC)
-    mixing = kernel * inner_prod[:, None, :, :] * step_c[:, :, None, :]
-    local_part = jnp.einsum("chqk,ckhp->cqhp", mixing, values_c, precision=HIGHEST_PREC)
-    tail_decay = decay_c[:, :, -1]
-    same_last = (ids_c == last_ids[:, None]).astype(jnp.float32)
-    carry_w = jnp.exp(tail_decay[:, :, None] - decay_c) * step_c * same_last[:, None, :]
-    fresh_states = jnp.einsum("chk,ckn,ckhp->chpn", carry_w, in_c, values_c, precision=HIGHEST_PREC)
-    through = (last_ids == prior_ids).astype(jnp.float32)[:, None] * jnp.exp(tail_decay)
-
-    def advance(carry_state, block_item):
-        fresh_block, factor = block_item
-        return (factor[:, None, None] * carry_state + fresh_block, carry_state)
-
-    start_state = jnp.zeros((head_count, head_size, state_size), jnp.float32)
-    _, entering = lax.scan(advance, start_state, (fresh_states, through))
-    reach_w = jnp.exp(decay_c) * (ids_c == prior_ids[:, None]).astype(jnp.float32)[:, None, :]
-    carried = jnp.einsum("cqn,chpn->cqhp", out_c, entering, precision=HIGHEST_PREC)
-    carried = carried * jnp.transpose(reach_w, (0, 2, 1))[:, :, :, None]
-    result = (local_part + carried).reshape(seq_rows, head_count, head_size)
-    return result + skip_gain[None, :, None] * values
+        + grouped[2 * SPAN : 2 * SPAN + 1]
+    )
+    d_step = grouped[SPAN : 2 * SPAN] - jnp.exp(head_ref[0:1, :]) * d_decay
+    d_step_raw = d_step * lax.logistic(pre_step)
+    head_grad_ref[0:1, :] += jnp.sum(d_decay * decay, axis=0, keepdims=True)
+    head_grad_ref[1:2, :] += jnp.sum(d_step_raw, axis=0, keepdims=True)
+    reached = (reach_x * d_low_f).astype(jnp.bfloat16)
+    leaving = (leave_x * stepped_f).astype(jnp.bfloat16)
+    d_inner_low = d_inner.astype(jnp.bfloat16)
+    d_out = contract_first(d_inner_low, in_maps) + contract_last(
+        reached, state_ref[0].astype(jnp.bfloat16)
+    )
+    d_in = mm(d_inner_low, out_maps) + contract_last(leaving, d_state_low)
+    carry_ref[...] = through_x * d_state + contract_first(out_maps, reached)
+    pre = pre_ref[...]
+    raw = raw_ref[...]
+    d_pre = jnp.concatenate([d_values, d_in, d_out], axis=1) * silu_slope(pre, lax.logistic(pre))
+    ext_ref[SPAN : SPAN + 8, :] = ext_ref[0:8, :]
+    ext_ref[0:SPAN, :] = d_pre
+    d_raw = taps_ref[3:4, :] * d_pre
+    taps_grad_ref[3:4, :] += jnp.sum(raw * d_pre, axis=0, keepdims=True)
+    taps_grad_ref[4:5, :] += jnp.sum(d_pre, axis=0, keepdims=True)
+    for offset in range(1, 4):
+        same = jnp.where(ids_at(col + block * SPAN + offset, ends_ref) == id_col, 1.0, 0.0)
+        shifted = ext_ref[offset : SPAN + offset, :] * same
+        d_raw = d_raw + taps_ref[3 - offset : 4 - offset, :] * shifted
+        taps_grad_ref[3 - offset : 4 - offset, :] += jnp.sum(raw * shifted, axis=0, keepdims=True)
+    cols_ref[:, inner:] = d_raw[:, :inner].astype(jnp.bfloat16)
+    shared_ref[:, : 2 * states] = d_raw[:, inner:]
+    shared_ref[:, 2 * states :] = d_step_raw
+
+
+def whole_spec(array):
+    return pl.BlockSpec(array.shape, lambda i: (0,) * array.ndim)
+
+
+def run_forward(ends, rows, weight, taps, head, skip, spread):
+    group_rows = rows.shape[0]
+    blocks = group_rows // SPAN
+    inner, width = skip.shape[1], taps.shape[1]
+    states = (width - inner) // 2
+
+    def rows_spec(columns):
+        return pl.BlockSpec((SPAN, columns), lambda i: (i, 0))
+
+    def rows_out(columns, kind):
+        return jax.ShapeDtypeStruct((group_rows, columns), kind)
+
+    f32 = jnp.float32
+    return pl.pallas_call(
+        forward_kernel,
+        grid=(blocks,),
+        in_specs=[
+            pl.BlockSpec(memory_space=pltpu.SMEM),
+            rows_spec(rows.shape[1]),
+            whole_spec(weight),
+            whole_spec(taps),
+            whole_spec(head),
+            whole_spec(skip),
+            whole_spec(spread),
+        ],
+        out_specs=[
+            rows_spec(inner),
+            rows_spec(width),
+            rows_spec(width),
+            rows_spec(width),
+            rows_spec(LANES),
+            rows_spec(inner),
+            rows_spec(inner),
+            pl.BlockSpec((1, states, inner), lambda i: (i, 0, 0)),
+        ],
+        out_shape=[
+            rows_out(inner, f32),
+            rows_out(width, f32),
+            rows_out(width, f32),
+            rows_out(width, jnp.bfloat16),
+            rows_out(LANES, f32),
+            rows_out(inner, f32),
+            rows_out(inner, f32),
+            jax.ShapeDtypeStruct((blocks, states, inner), f32),
+        ],
+        scratch_shapes=[
+            pltpu.VMEM((SPAN + 8, width), f32),
+            pltpu.VMEM((states, inner), f32),
+        ],
+        compiler_params=pltpu.CompilerParams(
+            dimension_semantics=("arbitrary",), vmem_limit_bytes=KERNEL_VMEM
+        ),
+        cost_estimate=pl.CostEstimate(
+            flops=12_000_000_000, bytes_accessed=36_000_000, transcendentals=6_000_000
+        ),
+        name="scan_forward",
+    )(ends, rows, weight, taps, head, skip, spread)
+
+
+def run_backward(
+    ends, stats, d_normal, gate, raw, pre, conv, step, ssd, states_in, taps, head, skip, gain, spread, group
+):
+    group_rows, inner = gate.shape
+    blocks = group_rows // SPAN
+    width = raw.shape[1]
+    states = states_in.shape[1]
+
+    def rows_spec(columns):
+        return pl.BlockSpec((SPAN, columns), lambda i: (blocks - 1 - i, 0))
+
+    def fixed(rows, columns):
+        return pl.BlockSpec((rows, columns), lambda i: (0, 0))
+
+    f32 = jnp.float32
+    return pl.pallas_call(
+        backward_kernel,
+        grid=(blocks,),
+        in_specs=[
+            pl.BlockSpec(memory_space=pltpu.SMEM),
+            rows_spec(2),
+            rows_spec(inner),
+            rows_spec(inner),
+            rows_spec(width),
+            rows_spec(width),
+            rows_spec(width),
+            rows_spec(LANES),
+            rows_spec(inner),
+            pl.BlockSpec((1, states, inner), lambda i: (blocks - 1 - i, 0, 0)),
+            pl.BlockSpec((1, states, inner), lambda i: (jnp.minimum(blocks - i, blocks - 1), 0, 0)),
+            whole_spec(taps),
+            whole_spec(head),
+            whole_spec(skip),
+            whole_spec(gain),
+            whole_spec(spread),
+            whole_spec(group),
+        ],
+        out_specs=[
+            rows_spec(2 * inner),
+            rows_spec(width - inner + LANES),
+            fixed(8, width),
+            fixed(8, inner),
+            fixed(8, LANES),
+        ],
+        out_shape=[
+            jax.ShapeDtypeStruct((group_rows, 2 * inner), jnp.bfloat16),
+            jax.ShapeDtypeStruct((group_rows, width - inner + LANES), f32),
+            jax.ShapeDtypeStruct((8, width), f32),
+            jax.ShapeDtypeStruct((8, inner), f32),
+            jax.ShapeDtypeStruct((8, LANES), f32),
+        ],
+        scratch_shapes=[
+            pltpu.VMEM((SPAN + 8, width), f32),
+            pltpu.VMEM((states, inner), f32),
+        ],
+        compiler_params=pltpu.CompilerParams(
+            dimension_semantics=("arbitrary",), vmem_limit_bytes=KERNEL_VMEM
+        ),
+        cost_estimate=pl.CostEstimate(
+            flops=20_000_000_000, bytes_accessed=48_000_000, transcendentals=8_000_000
+        ),
+        name="scan_backward",
+    )(ends, stats, d_normal, gate, raw, pre, conv, step, ssd, states_in, states_in, taps, head, skip, gain, spread, group)
 
 
 def contract_last(left, right):
@@ -218,70 +565,95 @@
     normed = (inputs_f * norm_scale * norm_gain[None, :]).astype(jnp.bfloat16)
     gathered = gather_rows(normed, "tensor", (2, 1))
     in_width = w_heads.shape[1]
+    heads_low = (
+        w_heads.astype(jnp.bfloat16)
+        .reshape(-1, own_heads, 2, head_size)
+        .transpose(0, 2, 1, 3)
+        .reshape(-1, in_width)
+    )
     in_full = gather_two(
-        jnp.concatenate([w_heads.astype(jnp.bfloat16), w_shared.astype(jnp.bfloat16)], axis=1), "dp"
+        jnp.concatenate([heads_low, w_shared.astype(jnp.bfloat16)], axis=1), "dp"
     )
     heads_full, shared_full = in_full[:, :in_width], in_full[:, in_width:]
     out_cols = gather_two(w_out.astype(jnp.bfloat16), "dp")
-    head_cols = jnp.dot(gathered, heads_full, preferred_element_type=jnp.float32).reshape(
-        group_rows, own_heads, 2, head_size
-    )
-    shared = jnp.dot(gathered, shared_full, preferred_element_type=jnp.float32)
-    gate_vals = head_cols[:, :, 0, :]
-    conv_in = jnp.concatenate(
-        [head_cols[:, :, 1, :].reshape(group_rows, own_inner), shared[:, : 2 * state_size]], axis=1
+    step_at = in_width + 2 * state_size
+    weight_in = jnp.concatenate(
+        [
+            in_full[:, :step_at],
+            lax.dynamic_slice_in_dim(in_full, step_at + tensor_pos * own_heads, own_heads, 1),
+            jnp.zeros((model_width, LANES - own_heads), jnp.bfloat16),
+        ],
+        axis=1,
     )
     conv_taps = jnp.concatenate([chan_params, bc_params], axis=1)
-
-    def convolve(raw_vals, taps_all):
-        return jax.nn.silu(causal_conv(raw_vals, taps_all, seq_ids))
-
-    conv_out, conv_pull = jax.vjp(convolve, conv_in, conv_taps)
-    conv_low = lax.optimization_barrier(conv_out.astype(jnp.bfloat16)).astype(jnp.float32)
-    step_raw = lax.dynamic_slice_in_dim(
-        shared[:, 2 * state_size :], tensor_pos * own_heads, own_heads, 1
-    )
-
-    def mixer(conv_vals, gate_in, step_in, head_vals):
-        step_size = jax.nn.softplus(step_in + head_vals[1][None, :])
-        log_decay = -jnp.exp(head_vals[0])[None, :] * step_size
-        value_part = conv_vals[:, :own_inner].reshape(group_rows, own_heads, head_size)
-        in_maps = conv_vals[:, own_inner : own_inner + state_size]
-        out_maps = conv_vals[:, own_inner + state_size :]
-        ssd_out = state_space(
-            value_part, in_maps, out_maps, log_decay, step_size, seq_ids, head_vals[2]
-        )
-        return (ssd_out * jax.nn.silu(gate_in)).reshape(group_rows, own_inner)
-
-    gated_vals, mixer_pull = jax.vjp(mixer, conv_low, gate_vals, step_raw, head_params)
+    head_pad = jnp.pad(head_params, ((0, 0), (0, LANES - own_heads)))
+    skip_cols = jnp.repeat(head_params[2], head_size)[None, :]
+    spread_one = (
+        jnp.arange(own_inner, dtype=jnp.int32)[None, :] // head_size
+        == jnp.arange(LANES, dtype=jnp.int32)[:, None]
+    ).astype(jnp.bfloat16)
+    spread_two = jnp.concatenate([spread_one, spread_one], axis=0)
+    group_two = jnp.concatenate([spread_one.T, spread_one.T], axis=0)
+    seq_ends = jnp.cumsum(lengths[0])
+    gate_cols, raw_cols, pre_cols, conv_cols, step_cols, ssd_cols, gated_vals, states_in = (
+        run_forward(seq_ends, gathered, weight_in, conv_taps, head_pad, skip_cols, spread_two)
+    )
     cotangent_f = cotangent.astype(jnp.float32)
     masked = (cotangent_f * own_valid).astype(jnp.bfloat16)
     own_gain = lax.dynamic_slice_in_dim(gate_gain, tensor_pos * own_inner, own_inner, 0)[None, :]
-    square_sum = lax.psum(jnp.sum(gated_vals * gated_vals, axis=1), "tensor")
-    inv_gate = lax.rsqrt(square_sum / all_inner + NORM_EPS)[:, None]
-    normal_out = (gated_vals * inv_gate * own_gain).astype(jnp.bfloat16)
-    branch = scatter_rows(contract_last(normal_out, out_cols), "tensor", (1, 2))
     masked_all = gather_rows(masked, "tensor", (2, 1))
     d_normal = jnp.dot(masked_all, out_cols, preferred_element_type=jnp.float32)
-    weighted = d_normal * own_gain
-    row_dot = lax.psum(jnp.sum(gated_vals * weighted, axis=1), "tensor")[:, None]
-    d_gated = inv_gate * weighted - gated_vals * inv_gate**3 * row_dot / all_inner
-    own_gain_grad = jnp.sum(gated_vals * inv_gate * d_normal, axis=0)
-    gate_gain_grad = lax.dynamic_update_slice_in_dim(
-        jnp.zeros((all_inner,), jnp.float32), own_gain_grad, tensor_pos * own_inner, 0
-    )
+    row_sums = lax.psum(
+        jnp.stack(
+            [
+                jnp.sum(gated_vals * gated_vals, axis=1),
+                jnp.sum(gated_vals * (d_normal * own_gain), axis=1),
+            ]
+        ),
+        "tensor",
+    )
+    inv_gate = lax.rsqrt(row_sums[0] / all_inner + NORM_EPS)
+    stats = jnp.stack([inv_gate, inv_gate**3 * row_sums[1] / all_inner], axis=1)
+    normal_out = (gated_vals * inv_gate[:, None] * own_gain).astype(jnp.bfloat16)
+    branch = scatter_rows(contract_last(normal_out, out_cols), "tensor", (1, 2))
     out_grad = contract_first(masked_all, normal_out)
     output = inputs_f + own_valid * branch
-    d_conv, d_gate, d_step, d_head = mixer_pull(d_gated)
-    d_raw, d_taps = conv_pull(d_conv)
-    d_value = d_raw[:, :own_inner].reshape(group_rows, own_heads, head_size)
-    d_cols = (
-        jnp.stack([d_gate, d_value], axis=2).reshape(group_rows, 2 * own_inner).astype(jnp.bfloat16)
+    d_cols, d_shared_cols, taps_sums, inner_sums, head_sums = run_backward(
+        seq_ends,
+        stats,
+        d_normal,
+        gate_cols,
+        raw_cols,
+        pre_cols,
+        conv_cols,
+        step_cols,
+        ssd_cols,
+        states_in,
+        conv_taps,
+        head_pad,
+        skip_cols,
+        own_gain,
+        spread_two,
+        group_two,
+    )
+    d_taps = taps_sums[:5]
+    gate_gain_grad = lax.dynamic_update_slice_in_dim(
+        jnp.zeros((all_inner,), jnp.float32), inner_sums[0], tensor_pos * own_inner, 0
+    )
+    d_head = jnp.concatenate(
+        [
+            head_sums[:2, :own_heads],
+            jnp.sum(inner_sums[1].reshape(own_heads, head_size), axis=1)[None, :],
+        ],
+        axis=0,
     )
     d_step_all = lax.dynamic_update_slice_in_dim(
-        jnp.zeros((group_rows, all_heads), jnp.float32), d_step, tensor_pos * own_heads, 1
-    )
-    d_shared_part = jnp.concatenate([d_raw[:, own_inner:], d_step_all], axis=1)
+        jnp.zeros((group_rows, all_heads), jnp.float32),
+        d_shared_cols[:, 2 * state_size : 2 * state_size + own_heads],
+        tensor_pos * own_heads,
+        1,
+    )
+    d_shared_part = jnp.concatenate([d_shared_cols[:, : 2 * state_size], d_step_all], axis=1)
     d_normed_part = contract_last(d_cols, heads_full)
     d_normed_rows, d_shared_rows = (
         scatter_rows(d_normed_part, "tensor", (1, 2)),
@@ -298,6 +670,9 @@
     heads_shard, out_shard = (
         scatter_two(heads_grad, "dp"),
         scatter_two(out_grad, "dp"),
+    )
+    heads_shard = (
+        heads_shard.reshape(-1, 2, own_heads, head_size).transpose(0, 2, 1, 3).reshape(-1, in_width)
     )
     norm_gain_grad = jnp.sum(inputs_f * norm_scale * d_normed, axis=0)
     own_sums = sum_all(

time: 658 us -> 404 us (0.61)
  other arithmetic: 215 us -> 50.2 us
  matrix products: 136 us -> 29 us
  Pallas kernels: 0 us -> 68.3 us
  local copies, waits for them, and re-layouts: 125 us -> 83.7 us
  waiting for transfers between devices: 118 us -> 105 us
  starting transfers between devices: 39.6 us -> 48.7 us
    dot_general x14 -> x0, matrix products: 106 us -> none  [the longest x3 54.8 us: state_space(): jnp.einsum('chqk,ckhp->cqhp', mixing, values_c, precision=HIGHEST_PREC)]
    pallas_call x0 -> x2, Pallas kernels: none -> 68.3 us  [the longest x1 40.9 us: run_backward(): pl.pallas_call(backward_kernel, grid=(blocks,), in_specs=[pl.BlockSpec(me...]
    reduce_sum x17 -> x1, other arithmetic: 60.7 us -> 0.12 us  [shards(): jnp.sum(inner_sums[1].reshape(own_heads, head_size), axis=1)[None, :]]
    another operation x7 -> x3, other arithmetic: 25.7 us -> 0.21 us
    mul x9 -> x0, other arithmetic: 16.7 us -> none  [the longest x3 16.2 us: causal_conv(): conv_taps[3 - offset][None, :] * shifted * same_seq[:, None]]
    unnamed x286 -> x153, local copies, waits for them, and re-layouts: 47.5 us -> 30.9 us
    reshape x9 -> x0, local copies, waits for them, and re-layouts: 14.5 us -> none  [the longest x1 4.88 us: state_space(): result = (local_part + carried).reshape(seq_rows, head_count, head_size)]
    convert_element_type x4 -> x1, other arithmetic: 14.2 us -> 0.03 us  [shards(): w_heads.astype(jnp.bfloat16).reshape(-1, own_heads, 2, head_size)]
  transfers between devices with their start and end apart: 42 -> 42, of which waited for: 20 -> 17; matrix products, arithmetic and copies ran while one was open for 29% -> 29% of each run, Pallas kernels for 0% -> 0%
where the time goes in v2:
time: 404 us; the launch traced here: 398 us
  waiting for transfers between devices  105 us (26%)
  local copies, waits for them, and re-layouts  83.7 us (21%)
  Pallas kernels  68.3 us (17%)
  other arithmetic  50.2 us (12%)
  starting transfers between devices  48.7 us (12%)
  matrix products  29 us (7%)
  blocking collectives  10.8 us (3%)
    ppermute x42, waiting for transfers between devices, swap(): return lax.ppermute(vals, axis, [(i, i ^ bit) for i in range(ways)])  105 us
    ppermute x42, starting transfers between devices, swap(): return lax.ppermute(vals, axis, [(i, i ^ bit) for i in range(ways)])  48.7 us
    pallas_call x1, Pallas kernels, run_backward(): pl.pallas_call(backward_kernel, grid=(blocks,), in_specs=[pl.BlockSpec(me...  40.9 us
    unnamed x153, local copies, waits for them, and re-layouts  30.9 us
    pallas_call x1, Pallas kernels, run_forward(): pl.pallas_call(forward_kernel, grid=(blocks,), in_specs=[pl.BlockSpec(mem...  27.5 us
    dot_general x3, matrix products, contract_last(): lax.dot_general(left, right, (((1,), (1,)), ((), ())), preferred_element_...  14.4 us
    add x16, other arithmetic, scatter_rows(): held = keep.astype(jnp.float32) + swap(send, axis, bit).astype(jnp.float32)  11.4 us
    select_n x14, other arithmetic, gather_rows(): jnp.where(upper, other, held)  10.9 us
  transfers between devices with their start and end apart: 42, of which 17 were waited for; matrix products, arithmetic and copies ran while one was open for 29% of the time, Pallas kernels for 0%

profile of v2, /device:TPU:0, one launch (start us, length us, event | category | flops | bytes accessed | tf_op | source)
XLA Modules:
  0.0 397.7 jit_solution(10953129066886080344)
XLA Ops:
  2.4 4.0 %collective-permute-start.10 = (bf16[1,1,1,128,256]{4,3,2,1,0:T(8,128)(2,1)}, bf16[1,1,1,128,256]{4,3,2,1,0:T(8,128)(2,1)}, u32[]{:S(2)}, u32[]{:S(2)}) collective-permute-start(bf16[1,1,1,128,256]{4,3,2,1,0:T(8,128)(2,1)} %get-tuple-element.186), channel_id=1, source_target_pairs={{0,16},{4,20},{8,24},{12,28},{16,0},{20,4},{24,8},{28,12},{1,17},{... | collective-permute-start | bytes 196616 | tf_op jit(solution)/shard_map/ppermute | solution.py:453
  27.3 3.0 collective-permute-start.14
  38.7 9.2 %collective-permute-done.15 = bf16[2,1,2,128,256]{4,3,2,1,0:T(8,128)(2,1)S(1)} collective-permute-done((bf16[2,1,2,128,256]{4,3,2,1,0:T(8,128)(2,1)S(1)}, bf16[2,1,2,128,256]{4,3,2,1,0:T(8,128)(2,1)S(1)}, u32[]{:S(2)}, u32[]{:S(2)}) %collective-permute-start.15) | collective-permute-done | bytes 262176 | tf_op jit(solution)/shard_map/ppermute | solution.py:453
  49.4 9.5 %collective-permute-done.8 = bf16[1,1,512,1024]{3,2,1,0:T(8,128)(2,1)S(1)} collective-permute-done((bf16[1,1,512,1024]{3,2,1,0:T(8,128)(2,1)S(1)}, bf16[1,1,512,1024]{3,2,1,0:T(8,128)(2,1)S(1)}, u32[]{:S(2)}, u32[]{:S(2)}) %collective-permute-start.8) | collective-permute-done | bytes 1048608 | tf_op jit(solution)/shard_map/ppermute | solution.py:453
  71.4 9.1 %collective-permute-done.4 = bf16[2,2,1,128,640]{3,4,2,1,0:T(8,128)(2,1)S(1)} collective-permute-done((bf16[2,2,1,128,640]{3,4,2,1,0:T(8,128)(2,1)S(1)}, bf16[2,2,1,128,640]{3,4,2,1,0:T(8,128)(2,1)S(1)}, u32[]{:S(2)}, u32[]{:S(2)}) %collective-permute-start.4) | collective-permute-done | bytes 655392 | tf_op jit(solution)/shard_map/ppermute | solution.py:453
  91.8 5.3 %concatenate.109.weight_ref = bf16[1024,1408]{1,0:T(8,128)(2,1)} concatenate(bf16[1024,1280]{1,0:T(8,128)(2,1)} %fusion, bf16[1024,8]{1,0:T(8,128)(2,1)} %fusion.27, bf16[1024,120]{1,0:T(8,128)(2,1)S(1)} %broadcast_in_dim.12), dimensions={1} | concatenate | bytes 5767168 | tf_op jit(solution)/shard_map/concatenate | solution.py:580
  104.2 27.5 %scan_forward.1 = (f32[2048,512]{1,0:T(8,128)}, f32[2048,768]{1,0:T(8,128)}, f32[2048,768]{1,0:T(8,128)}, bf16[2048,768]{1,0:T(8,128)(2,1)}, f32[2048,128]{1,0:T...) custom-call(s32[2]{0:T(128)} %bitcast.155, bf16[2048,1024]{1,0:T(8,128)(2,1)} %bitcast.128, ...), custom_call_target="tpu_custom_call" | custom-call | flops 12000000000 | bytes 36000000 | tf_op jit(solution)/shard_map/scan_forward/pallas_call | solution.py:319
  131.7 6.9 %multiply_reduce_fusion.1 = (f32[2048]{0:T(1024)S(1)}, f32[2048]{0:T(1024)S(1)}, f32[2048,512]{1,0:T(8,128)}) fusion(f32[2048,512]{1,0:T(8,128)} %get-tuple-element.36, f32[512]{0:T(512)S(1)} %dynamic_slice.137, bf16[2048,1024]{1,0:T(8,128)(2,1)S(1)} %bitcast.130, bf16[1024,256]{1,0:T(8,128)(2,1)S(1)} %bitcast.139, bf16[1024,256]{1,0:T(8,128)(2,1)} %bitcast.141), kind=kOutput, calls=%fused_computation.8 | convolution fusion | flops 2154819584 | bytes 13649920 | tf_op jit(solution)/shard_map/dot_general | solution.py:605
  138.6 10.8 %psum.7 = f32[2,2048]{1,0:T(2,128)S(1)} all-reduce(f32[2,2048]{1,0:T(2,128)S(1)} %pad_maximum_fusion.25), channel_id=1, replica_groups=mesh['dp'=8,'tensor'=4] {'tensor'}, use_global_device_ids=true, to_apply=%region_5.6 | all-reduce | flops 4096 | bytes 32768 | tf_op jit(solution)/shard_map/psum | solution.py:606
  150.8 40.9 %scan_backward.1 = (bf16[2048,1024]{1,0:T(8,128)(2,1)}, f32[2048,384]{1,0:T(8,128)}, f32[8,768]{1,0:T(8,128)}, f32[8,512]{1,0:T(8,128)}, f32[8,128]{1,0:T(8,128)}) custom-call(s32[2]{0:T(128)} %bitcast.156, f32[2048,2]{1,0:T(8,128)} %copy.125.stat_ref, f32[2048,512]{1,0:T(8,128)} %get-tuple-element.192.normal_ref, f32[2048,512]{1,0:T(8,128)} %get-tuple-element.37.gate_ref, ...), custom_call_target="tpu_custom_call" | custom-call | flops 20000000000 | bytes 48000000 | tf_op jit(solution)/shard_map/scan_backward/pallas_call | solution.py:380
  195.4 3.2 slice.124
  201.2 5.7 %fusion.18 = f32[2048,1024]{1,0:T(8,128)} fusion(bf16[1024,256]{1,0:T(8,128)(2,1)S(1)} %bitcast.140, bf16[1024,256]{1,0:T(8,128)(2,1)S(1)} %bitcast.142, f32[2048,512]{1,0:T(8,128)S(1)} %copy-done.11, f32[2048]{0:T(1024)S(1)} %bitcast.148, f32[512]{0:T(512)S(1)} %copy-done.46), kind=kOutput, calls=%fused_computation.62 | convolution fusion | flops 2152726528 | bytes 13641728 | tf_op jit(solution)/shard_map/dot_general | solution.py:431
  206.9 4.6 %fusion.60 = f32[1024,1024]{1,0:T(8,128)S(1)} fusion(bf16[2048,1024]{1,0:T(8,128)(2,1)S(1)} %bitcast.129, bf16[2048,1024]{1,0:T(8,128)(2,1)S(1)} %copy-done.60), kind=kOutput, calls=%fused_computation.215 | convolution fusion | flops 4294967296 | bytes 12582912 | tf_op jit(solution)/shard_map/dot_general | solution.py:437
  211.6 7.4 %fusion.11 = f32[2048,1024]{1,0:T(8,128)} fusion(bf16[2048,1024]{1,0:T(8,128)(2,1)S(1)} %copy-done.60, bf16[1024,672]{1,0:T(8,128)(2,1)S(1)} %bitcast.112, bf16[1024,640]{1,0:T(8,128)(2,1)S(1)} %bitcast.116), kind=kOutput, calls=%fused_computation.33 | convolution fusion | flops 4299161600 | bytes 15269888 | tf_op jit(solution)/shard_map/dot_general | solution.py:431
  231.5 2.6 copy.157
  248.1 5.4 %dynamic_update_slice.6 = f32[2048,32]{1,0:T(8,128)} dynamic-update-slice(f32[2048,32]{1,0:T(8,128)} %broadcast_in_dim.15, f32[2048,8]{1,0:T(8,128)} %slice.125, s32[]{:T(128)} %constant.197.clone.1, s32[]{:T(128)S(6)} %select_n.354) | dynamic-update-slice | bytes 131076 | tf_op jit(solution)/shard_map/dynamic_update_slice | solution.py:650
  257.8 2.9 copy.153
  265.7 2.7 dynamic-slice_convert_fusion
  271.7 3.8 collective-permute-done.37
  275.5 2.6 collective-permute-start.40
  278.1 5.7 %collective-permute-done.40 = bf16[1,1,2,128,256]{4,3,2,1,0:T(8,128)(2,1)S(1)} collective-permute-done((bf16[1,1,2,128,256]{4,3,2,1,0:T(8,128)(2,1)S(1)}, bf16[1,1,2,128,256]{4,3,2,1,0:T(8,128)(2,1)S(1)}, u32[]{:S(2)}, u32[]{:S(2)}) %collective-permute-start.40) | collective-permute-done | bytes 131104 | tf_op jit(solution)/shard_map/ppermute | solution.py:453
  284.0 5.9 %collective-permute-done.38 = bf16[1,1,1,128,256]{4,3,2,1,0:T(8,128)(2,1)S(1)} collective-permute-done((bf16[1,1,1,128,256]{4,3,2,1,0:T(8,128)(2,1)S(1)}, bf16[1,1,1,128,256]{4,3,2,1,0:T(8,128)(2,1)S(1)}, u32[]{:S(2)}, u32[]{:S(2)}) %collective-permute-start.38) | collective-permute-done | bytes 65568 | tf_op jit(solution)/shard_map/ppermute | solution.py:453
  290.5 3.7 collective-permute-done.41
  298.8 2.8 collective-permute-start.26
  305.1 3.4 collective-permute-done.23
  311.9 2.6 convert_add_fusion.1
  317.1 6.2 %collective-permute-done.24 = bf16[1,1,1,128,512]{3,4,2,1,0:T(8,128)(2,1)S(1)} collective-permute-done((bf16[1,1,1,128,512]{3,4,2,1,0:T(8,128)(2,1)S(1)}, bf16[1,1,1,128,512]{3,4,2,1,0:T(8,128)(2,1)S(1)}, u32[]{:S(2)}, u32[]{:S(2)}) %collective-permute-start.24) | collective-permute-done | bytes 131104 | tf_op jit(solution)/shard_map/ppermute | solution.py:453
  324.0 12.0 %collective-permute-done.19 = bf16[1,1,512,1024]{3,2,1,0:T(8,128)(2,1)S(1)} collective-permute-done((bf16[1,1,512,1024]{3,2,1,0:T(8,128)(2,1)S(1)}, bf16[1,1,512,1024]{3,2,1,0:T(8,128)(2,1)S(1)}, u32[]{:S(2)}, u32[]{:S(2)}) %collective-permute-start.19) | collective-permute-done | bytes 1048608 | tf_op jit(solution)/shard_map/ppermute | solution.py:453
  337.2 20.2 %collective-permute-done.17 = bf16[1,1,512,1024]{3,2,1,0:T(8,128)(2,1)S(1)} collective-permute-done((bf16[1,1,512,1024]{3,2,1,0:T(8,128)(2,1)S(1)}, bf16[1,1,512,1024]{3,2,1,0:T(8,128)(2,1)S(1)}, u32[]{:S(2)}, u32[]{:S(2)}) %collective-permute-start.17) | collective-permute-done | bytes 1048608 | tf_op jit(solution)/shard_map/ppermute | solution.py:453
  357.4 3.0 fusion.22
  365.0 6.2 %collective-permute-done.31 = bf16[2,2,1,128,288]{3,4,2,1,0:T(8,128)(2,1)S(1)} collective-permute-done((bf16[2,2,1,128,288]{3,4,2,1,0:T(8,128)(2,1)S(1)}, bf16[2,2,1,128,288]{3,4,2,1,0:T(8,128)(2,1)S(1)}, u32[]{:S(2)}, u32[]{:S(2)}) %collective-permute-start.31) | collective-permute-done | bytes 294944 | tf_op jit(solution)/shard_map/ppermute | solution.py:453
  389.4 4.1 %collective-permute-done.35 = f32[41216]{0:T(1024)S(1)} collective-permute-done((f32[41216]{0:T(1024)S(1)}, f32[41216]{0:T(1024)S(1)}, u32[]{:S(2)}, u32[]{:S(2)}) %collective-permute-start.35) | collective-permute-done | bytes 164896 | tf_op jit(solution)/shard_map/ppermute | solution.py:453
  (377 shorter events, 152.6 us)
Async XLA Ops:
  2.4 23.7 %collective-permute-start.10 = (bf16[1,1,1,128,256]{4,3,2,1,0:T(8,128)(2,1)}, bf16[1,1,1,128,256]{4,3,2,1,0:T(8,128)(2,1)}, u32[]{:S(2)}, u32[]{:S(2)}) collective-permute-start(bf16[1,1,1,128,256]{4,3,2,1,0:T(8,128)(2,1)} %get-tuple-element.186), channel_id=1, source_target_pairs={{0,16},{4,20},{8,24},{12,28},{16,0},{20,4},{24,8},{28,12},{1,17},{... | collective-permute-start | bytes 196616 | tf_op jit(solution)/shard_map/ppermute | solution.py:453
  6.4 19.9 %collective-permute-start.13 = (bf16[1,1,1,128,256]{4,3,2,1,0:T(8,128)(2,1)}, bf16[1,1,1,128,256]{4,3,2,1,0:T(8,128)(2,1)}, u32[]{:S(2)}, u32[]{:S(2)}) collective-permute-start(bf16[1,1,1,128,256]{4,3,2,1,0:T(8,128)(2,1)} %get-tuple-element.187), channel_id=1, source_target_pairs={{0,4},{4,0},{8,12},{12,8},{16,20},{20,16},{24,28},{28,24},{1,5},{5... | collective-permute-start | bytes 196616 | tf_op jit(solution)/shard_map/ppermute | solution.py:453
  9.9 20.4 %collective-permute-start.2 = (bf16[1,1,1,128,640]{3,4,2,1,0:T(8,128)(2,1)}, bf16[1,1,1,128,640]{3,4,2,1,0:T(8,128)(2,1)}, u32[]{:S(2)}, u32[]{:S(2)}) collective-permute-start(bf16[1,1,1,128,640]{3,4,2,1,0:T(8,128)(2,1)} %slice_bitcast_fusion), channel_id=1, source_target_pairs={{0,16},{4,20},{8,24},{12,28},{16,0},{20,4},{24,8},{28,12},{1,17},{... | collective-permute-start | bytes 491528 | tf_op jit(solution)/shard_map/ppermute | solution.py:453
  10.3 22.6 %collective-permute-start.5 = (bf16[1,1,1,128,672]{3,4,2,1,0:T(8,128)(2,1)S(1)}, bf16[1,1,1,128,672]{3,4,2,1,0:T(8,128)(2,1)}, u32[]{:S(2)}, u32[]{:S(2)}) collective-permute-start(bf16[1,1,1,128,672]{3,4,2,1,0:T(8,128)(2,1)S(1)} %fusion.30), channel_id=1, source_target_pairs={{0,4},{4,0},{8,12},{12,8},{16,20},{20,16},{24,28},{28,24},{1,5},{5... | collective-permute-start | bytes 516104 | tf_op jit(solution)/shard_map/ppermute | solution.py:453
  12.2 37.2 %collective-permute-start = (bf16[1,1,512,1024]{3,2,1,0:T(8,128)(2,1)}, bf16[1,1,512,1024]{3,2,1,0:T(8,128)(2,1)}, u32[]{:S(2)}, u32[]{:S(2)}) collective-permute-start(bf16[1,1,512,1024]{3,2,1,0:T(8,128)(2,1)} %fusion.23), channel_id=1, source_target_pairs={{0,2},{1,3},{2,0},{3,1},{4,6},{5,7},{6,4},{7,5},{8,10},{9,11},{10,... | collective-permute-start | bytes 3145736 | tf_op jit(solution)/shard_map/ppermute | solution.py:453
  26.1 32.8 %collective-permute-start.8 = (bf16[1,1,512,1024]{3,2,1,0:T(8,128)(2,1)S(1)}, bf16[1,1,512,1024]{3,2,1,0:T(8,128)(2,1)S(1)}, u32[]{:S(2)}, u32[]{:S(2)}) collective-permute-start(bf16[1,1,512,1024]{3,2,1,0:T(8,128)(2,1)S(1)} %fusion.13), channel_id=1, source_target_pairs={{0,2},{1,3},{2,0},{3,1},{4,6},{5,7},{6,4},{7,5},{8,10},{9,11},{10,... | collective-permute-start | bytes 3145736 | tf_op jit(solution)/shard_map/ppermute | solution.py:453
  27.3 7.1 %collective-permute-start.14 = (bf16[1,1,2,128,256]{4,3,2,1,0:T(8,128)(2,1)S(1)}, bf16[1,1,2,128,256]{4,3,2,1,0:T(8,128)(2,1)S(1)}, u32[]{:S(2)}, u32[]{:S(2)}) collective-permute-start(bf16[1,1,2,128,256]{4,3,2,1,0:T(8,128)(2,1)S(1)} %pad_maximum_fusion.24), channel_id=1, source_target_pairs={{0,16},{4,20},{8,24},{12,28},{16,0},{20,4},{24,8},{28,12},{1,17},{... | collective-permute-start | bytes 393224 | tf_op jit(solution)/shard_map/ppermute | solution.py:453
  32.9 16.4 %collective-permute-start.3 = (bf16[2,1,1,128,640]{3,4,2,1,0:T(8,128)(2,1)S(1)}, bf16[2,1,1,128,640]{3,4,2,1,0:T(8,128)(2,1)S(1)}, u32[]{:S(2)}, u32[]{:S(2)}) collective-permute-start(bf16[2,1,1,128,640]{3,4,2,1,0:T(8,128)(2,1)S(1)} %pad_maximum_fusion.17), channel_id=1, source_target_pairs={{0,8},{4,12},{8,0},{12,4},{16,24},{20,28},{24,16},{28,20},{1,9},{5... | collective-permute-start | bytes 983048 | tf_op jit(solution)/shard_map/ppermute | solution.py:453
  34.5 13.4 %collective-permute-start.15 = (bf16[2,1,2,128,256]{4,3,2,1,0:T(8,128)(2,1)S(1)}, bf16[2,1,2,128,256]{4,3,2,1,0:T(8,128)(2,1)S(1)}, u32[]{:S(2)}, u32[]{:S(2)}) collective-permute-start(bf16[2,1,2,128,256]{4,3,2,1,0:T(8,128)(2,1)S(1)} %pad_maximum_fusion.19), channel_id=1, source_target_pairs={{0,8},{4,12},{8,0},{12,4},{16,24},{20,28},{24,16},{28,20},{1,9},{5... | collective-permute-start | bytes 786440 | tf_op jit(solution)/shard_map/ppermute | solution.py:453
  37.1 12.1 %collective-permute-start.12 = (bf16[2,2,1,128,256]{4,3,2,1,0:T(8,128)(2,1)S(1)}, bf16[2,2,1,128,256]{4,3,2,1,0:T(8,128)(2,1)S(1)}, u32[]{:S(2)}, u32[]{:S(2)}) collective-permute-start(bf16[2,2,1,128,256]{4,3,2,1,0:T(8,128)(2,1)S(1)} %pad_maximum_fusion.18), channel_id=1, source_target_pairs={{0,4},{4,0},{8,12},{12,8},{16,20},{20,16},{24,28},{28,24},{1,5},{5... | collective-permute-start | bytes 786440 | tf_op jit(solution)/shard_map/ppermute | solution.py:453
  47.9 17.0 %collective-permute-start.6 = (bf16[1,1,2,128,672]{3,4,2,1,0:T(8,128)(2,1)S(1)}, bf16[1,1,2,128,672]{3,4,2,1,0:T(8,128)(2,1)S(1)}, u32[]{:S(2)}, u32[]{:S(2)}) collective-permute-start(bf16[1,1,2,128,672]{3,4,2,1,0:T(8,128)(2,1)S(1)} %pad_maximum_fusion.16), channel_id=1, source_target_pairs={{0,16},{4,20},{8,24},{12,28},{16,0},{20,4},{24,8},{28,12},{1,17},{... | collective-permute-start | bytes 1032200 | tf_op jit(solution)/shard_map/ppermute | solution.py:453
  63.2 33.9 %collective-permute-start.1 = (bf16[2,1,512,1024]{3,2,1,0:T(8,128)(2,1)}, bf16[2,1,512,1024]{3,2,1,0:T(8,128)(2,1)}, u32[]{:S(2)}, u32[]{:S(2)}) collective-permute-start(bf16[2,1,512,1024]{3,2,1,0:T(8,128)(2,1)} %pad_maximum_fusion.5), channel_id=1, source_target_pairs={{0,1},{1,0},{2,3},{3,2},{4,5},{5,4},{6,7},{7,6},{8,9},{9,8},{10,11... | collective-permute-start | bytes 6291464 | tf_op jit(solution)/shard_map/ppermute | solution.py:453
  63.3 17.2 %collective-permute-start.4 = (bf16[2,2,1,128,640]{3,4,2,1,0:T(8,128)(2,1)S(1)}, bf16[2,2,1,128,640]{3,4,2,1,0:T(8,128)(2,1)S(1)}, u32[]{:S(2)}, u32[]{:S(2)}) collective-permute-start(bf16[2,2,1,128,640]{3,4,2,1,0:T(8,128)(2,1)S(1)} %pad_maximum_fusion.13), channel_id=1, source_target_pairs={{0,4},{4,0},{8,12},{12,8},{16,20},{20,16},{24,28},{28,24},{1,5},{5... | collective-permute-start | bytes 1966088 | tf_op jit(solution)/shard_map/ppermute | solution.py:453
  66.6 17.9 %collective-permute-start.7 = (bf16[2,1,2,128,672]{3,4,2,1,0:T(8,128)(2,1)}, bf16[2,1,2,128,672]{3,4,2,1,0:T(8,128)(2,1)}, u32[]{:S(2)}, u32[]{:S(2)}) collective-permute-start(bf16[2,1,2,128,672]{3,4,2,1,0:T(8,128)(2,1)} %pad_maximum_fusion.10), channel_id=1, source_target_pairs={{0,8},{4,12},{8,0},{12,4},{16,24},{20,28},{24,16},{28,20},{1,9},{5... | collective-permute-start | bytes 2064392 | tf_op jit(solution)/shard_map/ppermute | solution.py:453
  69.7 32.2 %collective-permute-start.9 = (bf16[2,1,512,1024]{3,2,1,0:T(8,128)(2,1)}, bf16[2,1,512,1024]{3,2,1,0:T(8,128)(2,1)}, u32[]{:S(2)}, u32[]{:S(2)}) collective-permute-start(bf16[2,1,512,1024]{3,2,1,0:T(8,128)(2,1)} %pad_maximum_fusion.6), channel_id=1, source_target_pairs={{0,1},{1,0},{2,3},{3,2},{4,5},{5,4},{6,7},{7,6},{8,9},{9,8},{10,11... | collective-permute-start | bytes 6291464 | tf_op jit(solution)/shard_map/ppermute | solution.py:453
  220.0 48.3 %collective-permute-start.36 = (bf16[2,2,1,128,256]{4,3,2,1,0:T(8,128)(2,1)}, bf16[2,2,1,128,256]{4,3,2,1,0:T(8,128)(2,1)}, u32[]{:S(2)}, u32[]{:S(2)}) collective-permute-start(bf16[2,2,1,128,256]{4,3,2,1,0:T(8,128)(2,1)} %dynamic-slice_convert_fusion.7), channel_id=1, source_target_pairs={{0,4},{4,0},{8,12},{12,8},{16,20},{20,16},{24,28},{28,24},{1,5},{5... | collective-permute-start | bytes 786440 | tf_op jit(solution)/shard_map/ppermute | solution.py:453
  221.1 48.8 %collective-permute-start.39 = (bf16[2,1,2,128,256]{4,3,2,1,0:T(8,128)(2,1)}, bf16[2,1,2,128,256]{4,3,2,1,0:T(8,128)(2,1)S(1)}, u32[]{:S(2)}, u32[]{:S(2)}) collective-permute-start(bf16[2,1,2,128,256]{4,3,2,1,0:T(8,128)(2,1)} %dynamic-slice_convert_fusion.6), channel_id=1, source_target_pairs={{0,8},{4,12},{8,0},{12,4},{16,24},{20,28},{24,16},{28,20},{1,9},{5... | collective-permute-start | bytes 786440 | tf_op jit(solution)/shard_map/ppermute | solution.py:453
  245.1 50.2 %collective-permute-start.22 = (bf16[2,2,1,128,512]{3,4,2,1,0:T(8,128)(2,1)}, bf16[2,2,1,128,512]{3,4,2,1,0:T(8,128)(2,1)}, u32[]{:S(2)}, u32[]{:S(2)}) collective-permute-start(bf16[2,2,1,128,512]{3,4,2,1,0:T(8,128)(2,1)} %copy.156), channel_id=1, source_target_pairs={{0,4},{4,0},{8,12},{12,8},{16,20},{20,16},{24,28},{28,24},{1,5},{5... | collective-permute-start | bytes 1572872 | tf_op jit(solution)/shard_map/ppermute | solution.py:453
  246.6 50.2 %collective-permute-start.25 = (bf16[2,1,2,128,512]{3,4,2,1,0:T(8,128)(2,1)}, bf16[2,1,2,128,512]{3,4,2,1,0:T(8,128)(2,1)}, u32[]{:S(2)}, u32[]{:S(2)}) collective-permute-start(bf16[2,1,2,128,512]{3,4,2,1,0:T(8,128)(2,1)} %copy.158), channel_id=1, source_target_pairs={{0,8},{4,12},{8,0},{12,4},{16,24},{20,28},{24,16},{28,20},{1,9},{5... | collective-permute-start | bytes 1572872 | tf_op jit(solution)/shard_map/ppermute | solution.py:453
  262.9 38.7 %collective-permute-start.20 = (bf16[2,1,512,288]{2,3,1,0:T(8,128)(2,1)}, bf16[2,1,512,288]{2,3,1,0:T(8,128)(2,1)}, u32[]{:S(2)}, u32[]{:S(2)}) collective-permute-start(bf16[2,1,512,288]{2,3,1,0:T(8,128)(2,1)} %copy.154), channel_id=1, source_target_pairs={{0,1},{1,0},{2,3},{3,2},{4,5},{5,4},{6,7},{7,6},{8,9},{9,8},{10,11... | collective-permute-start | bytes 1769480 | tf_op jit(solution)/shard_map/ppermute | solution.py:453
  268.4 40.3 %collective-permute-start.18 = (bf16[2,1,512,1024]{3,2,1,0:T(8,128)(2,1)S(1)}, bf16[2,1,512,1024]{3,2,1,0:T(8,128)(2,1)S(1)}, u32[]{:S(2)}, u32[]{:S(2)}) collective-permute-start(bf16[2,1,512,1024]{3,2,1,0:T(8,128)(2,1)S(1)} %dynamic-slice_convert_fusion), channel_id=1, source_target_pairs={{0,1},{1,0},{2,3},{3,2},{4,5},{5,4},{6,7},{7,6},{8,9},{9,8},{10,11... | collective-permute-start | bytes 6291464 | tf_op jit(solution)/shard_map/ppermute | solution.py:453
  275.5 8.3 %collective-permute-start.40 = (bf16[1,1,2,128,256]{4,3,2,1,0:T(8,128)(2,1)S(1)}, bf16[1,1,2,128,256]{4,3,2,1,0:T(8,128)(2,1)S(1)}, u32[]{:S(2)}, u32[]{:S(2)}) collective-permute-start(bf16[1,1,2,128,256]{4,3,2,1,0:T(8,128)(2,1)S(1)} %dynamic-slice_convert_fusion.11), channel_id=1, source_target_pairs={{0,16},{4,20},{8,24},{12,28},{16,0},{20,4},{24,8},{28,12},{1,17},{... | collective-permute-start | bytes 393224 | tf_op jit(solution)/shard_map/ppermute | solution.py:453
  294.2 17.7 %collective-permute-start.16 = (bf16[2,1,512,1024]{3,2,1,0:T(8,128)(2,1)S(1)}, bf16[2,1,512,1024]{3,2,1,0:T(8,128)(2,1)}, u32[]{:S(2)}, u32[]{:S(2)}) collective-permute-start(bf16[2,1,512,1024]{3,2,1,0:T(8,128)(2,1)S(1)} %dynamic-slice_convert_fusion.1), channel_id=1, source_target_pairs={{0,1},{1,0},{2,3},{3,2},{4,5},{5,4},{6,7},{7,6},{8,9},{9,8},{10,11... | collective-permute-start | bytes 6291464 | tf_op jit(solution)/shard_map/ppermute | solution.py:453
  296.5 12.0 %collective-permute-start.23 = (bf16[2,1,1,128,512]{3,4,2,1,0:T(8,128)(2,1)S(1)}, bf16[2,1,1,128,512]{3,4,2,1,0:T(8,128)(2,1)S(1)}, u32[]{:S(2)}, u32[]{:S(2)}) collective-permute-start(bf16[2,1,1,128,512]{3,4,2,1,0:T(8,128)(2,1)S(1)} %dynamic-slice_convert_fusion.9), channel_id=1, source_target_pairs={{0,8},{4,12},{8,0},{12,4},{16,24},{20,28},{24,16},{28,20},{1,9},{5... | collective-permute-start | bytes 786440 | tf_op jit(solution)/shard_map/ppermute | solution.py:453
  298.8 16.9 %collective-permute-start.26 = (bf16[1,1,2,128,512]{3,4,2,1,0:T(8,128)(2,1)}, bf16[1,1,2,128,512]{3,4,2,1,0:T(8,128)(2,1)S(1)}, u32[]{:S(2)}, u32[]{:S(2)}) collective-permute-start(bf16[1,1,2,128,512]{3,4,2,1,0:T(8,128)(2,1)} %dynamic-slice_convert_fusion.8), channel_id=1, source_target_pairs={{0,16},{4,20},{8,24},{12,28},{16,0},{20,4},{24,8},{28,12},{1,17},{... | collective-permute-start | bytes 786440 | tf_op jit(solution)/shard_map/ppermute | solution.py:453
  303.1 20.9 %collective-permute-start.21 = (bf16[1,1,512,288]{2,3,1,0:T(8,128)(2,1)S(1)}, bf16[1,1,512,288]{2,3,1,0:T(8,128)(2,1)S(1)}, u32[]{:S(2)}, u32[]{:S(2)}) collective-permute-start(bf16[1,1,512,288]{2,3,1,0:T(8,128)(2,1)S(1)} %dynamic-slice_convert_fusion.5), channel_id=1, source_target_pairs={{0,2},{1,3},{2,0},{3,1},{4,6},{5,7},{6,4},{7,5},{8,10},{9,11},{10,... | collective-permute-start | bytes 884744 | tf_op jit(solution)/shard_map/ppermute | solution.py:453
  309.9 26.1 %collective-permute-start.19 = (bf16[1,1,512,1024]{3,2,1,0:T(8,128)(2,1)S(1)}, bf16[1,1,512,1024]{3,2,1,0:T(8,128)(2,1)S(1)}, u32[]{:S(2)}, u32[]{:S(2)}) collective-permute-start(bf16[1,1,512,1024]{3,2,1,0:T(8,128)(2,1)S(1)} %dynamic-slice_convert_fusion.2), channel_id=1, source_target_pairs={{0,2},{1,3},{2,0},{3,1},{4,6},{5,7},{6,4},{7,5},{8,10},{9,11},{10,... | collective-permute-start | bytes 3145736 | tf_op jit(solution)/shard_map/ppermute | solution.py:453
  314.7 42.7 %collective-permute-start.17 = (bf16[1,1,512,1024]{3,2,1,0:T(8,128)(2,1)S(1)}, bf16[1,1,512,1024]{3,2,1,0:T(8,128)(2,1)S(1)}, u32[]{:S(2)}, u32[]{:S(2)}) collective-permute-start(bf16[1,1,512,1024]{3,2,1,0:T(8,128)(2,1)S(1)} %dynamic-slice_convert_fusion.3), channel_id=1, source_target_pairs={{0,2},{1,3},{2,0},{3,1},{4,6},{5,7},{6,4},{7,5},{8,10},{9,11},{10,... | collective-permute-start | bytes 3145736 | tf_op jit(solution)/shard_map/ppermute | solution.py:453
  315.6 7.6 %collective-permute-start.24 = (bf16[1,1,1,128,512]{3,4,2,1,0:T(8,128)(2,1)S(1)}, bf16[1,1,1,128,512]{3,4,2,1,0:T(8,128)(2,1)S(1)}, u32[]{:S(2)}, u32[]{:S(2)}) collective-permute-start(bf16[1,1,1,128,512]{3,4,2,1,0:T(8,128)(2,1)S(1)} %dynamic-slice_convert_fusion.14), channel_id=1, source_target_pairs={{0,16},{4,20},{8,24},{12,28},{16,0},{20,4},{24,8},{28,12},{1,17},{... | collective-permute-start | bytes 393224 | tf_op jit(solution)/shard_map/ppermute | solution.py:453
  316.5 55.6 %collective-permute-start.27 = (bf16[1,1,1,128,512]{3,4,2,1,0:T(8,128)(2,1)}, bf16[1,1,1,128,512]{3,4,2,1,0:T(8,128)(2,1)}, u32[]{:S(2)}, u32[]{:S(2)}) collective-permute-start(bf16[1,1,1,128,512]{3,4,2,1,0:T(8,128)(2,1)} %dynamic-slice_convert_fusion.13), channel_id=1, source_target_pairs={{0,4},{4,0},{8,12},{12,8},{16,20},{20,16},{24,28},{28,24},{1,5},{5... | collective-permute-start | bytes 393224 | tf_op jit(solution)/shard_map/ppermute | solution.py:453
  362.8 8.4 %collective-permute-start.31 = (bf16[2,2,1,128,288]{3,4,2,1,0:T(8,128)(2,1)S(1)}, bf16[2,2,1,128,288]{3,4,2,1,0:T(8,128)(2,1)S(1)}, u32[]{:S(2)}, u32[]{:S(2)}) collective-permute-start(bf16[2,2,1,128,288]{3,4,2,1,0:T(8,128)(2,1)S(1)} %dynamic-slice_convert_fusion.4), channel_id=1, source_target_pairs={{0,4},{4,0},{8,12},{12,8},{16,20},{20,16},{24,28},{28,24},{1,5},{5... | collective-permute-start | bytes 884744 | tf_op jit(solution)/shard_map/ppermute | solution.py:453
  363.4 9.6 %collective-permute-start.28 = (f32[6936]{0:T(1024)S(1)}, f32[6936]{0:T(1024)S(1)}, u32[]{:S(2)}, u32[]{:S(2)}) collective-permute-start(f32[6936]{0:T(1024)S(1)} %constant_dynamic-update-slice_fusion.3), channel_id=1, source_target_pairs={{0,4},{4,0},{8,12},{12,8},{16,20},{20,16},{24,28},{28,24},{1,5},{5... | collective-permute-start | bytes 83240 | tf_op jit(solution)/shard_map/ppermute | solution.py:453
  (76 other events, 831.3 us)

commit v3 on v2

--- a/solution.py
+++ b/solution.py
@@ -473,24 +473,48 @@
     return held.reshape((ways * rows,) + vals.shape[1:])
 
 
+def halve_rows(held, axis, order):
+    pos = lax.axis_index(axis)
+    for bit in order:
+        half = held.shape[0] // 2
+        mine = (pos & bit) // bit
+        keep = lax.dynamic_slice_in_dim(held, mine * half, half, 0)
+        send = lax.dynamic_slice_in_dim(held, (1 - mine) * half, half, 0).astype(jnp.bfloat16)
+        held = keep.astype(jnp.float32) + swap(send, axis, bit).astype(jnp.float32)
+    return held[0]
+
+
 def scatter_rows(vals, axis, order):
     ways = lax.axis_size(axis)
-    pos = lax.axis_index(axis)
+    depth = len(axis_bits(axis))
+    rows, columns = vals.shape[0] // ways, vals.shape[1]
+    held = vals.astype(jnp.bfloat16).reshape((2,) * depth + (rows, columns))
+    dims = [depth - bit.bit_length() for bit in order] + [depth, depth + 1]
+    return halve_rows(held.transpose(dims).reshape(ways, rows, columns), axis, order)
+
+
+def scatter_product(left, right, axis):
+    ways = lax.axis_size(axis)
+    core = lax.axis_index(axis) & 1
+    rows = left.shape[0] // ways
+    blocks = left.reshape(ways // 2, 2, rows, left.shape[1])
+    send_rows = lax.dynamic_slice_in_dim(blocks, 1 - core, 1, 1).reshape(-1, left.shape[1])
+    keep_rows = lax.dynamic_slice_in_dim(blocks, core, 1, 1).reshape(-1, left.shape[1])
+    got = swap(contract_last(send_rows, right).astype(jnp.bfloat16), axis, 1)
+    held = contract_last(keep_rows, right) + got.astype(jnp.float32)
+    return halve_rows(
+        held.reshape(ways // 2, rows, right.shape[0]), axis, axis_bits(axis)[:0:-1]
+    )
+
+
+def sum_all(vals, axis):
     bits = axis_bits(axis)
-    rows = vals.shape[0] // ways
-    held = vals.reshape((2,) * len(bits) + (rows,) + vals.shape[1:])
-    for bit in order:
-        dim = len(bits) - bit.bit_length()
-        mine = (pos & bit) // bit
-        keep = lax.dynamic_slice_in_dim(held, mine, 1, dim)
-        send = lax.dynamic_slice_in_dim(held, 1 - mine, 1, dim).astype(jnp.bfloat16)
-        held = keep.astype(jnp.float32) + swap(send, axis, bit).astype(jnp.float32)
-    return held.reshape((rows,) + vals.shape[1:])
-
-
-def sum_all(vals, axis):
-    for bit in axis_bits(axis):
-        vals = vals + swap(vals, axis, bit)
+    while bits:
+        group, bits = bits[:3], bits[3:]
+        parts = [vals] + [swap(vals, axis, group[0] * i) for i in range(1, 1 << len(group))]
+        while len(parts) > 1:
+            parts = [parts[i] + parts[i + 1] for i in range(0, len(parts), 2)]
+        vals = parts[0]
     return vals
 
 
@@ -615,7 +639,7 @@
     inv_gate = lax.rsqrt(row_sums[0] / all_inner + NORM_EPS)
     stats = jnp.stack([inv_gate, inv_gate**3 * row_sums[1] / all_inner], axis=1)
     normal_out = (gated_vals * inv_gate[:, None] * own_gain).astype(jnp.bfloat16)
-    branch = scatter_rows(contract_last(normal_out, out_cols), "tensor", (1, 2))
+    branch = scatter_product(normal_out, out_cols, "tensor")
     out_grad = contract_first(masked_all, normal_out)
     output = inputs_f + own_valid * branch
     d_cols, d_shared_cols, taps_sums, inner_sums, head_sums = run_backward(
@@ -654,9 +678,8 @@
         1,
     )
     d_shared_part = jnp.concatenate([d_shared_cols[:, : 2 * state_size], d_step_all], axis=1)
-    d_normed_part = contract_last(d_cols, heads_full)
     d_normed_rows, d_shared_rows = (
-        scatter_rows(d_normed_part, "tensor", (1, 2)),
+        scatter_product(d_cols, heads_full, "tensor"),
         scatter_rows(d_shared_part, "tensor", (1, 2)),
     )
     d_shared_low = d_shared_rows.astype(jnp.bfloat16)
@@ -666,19 +689,19 @@
     input_grad = (
         cotangent_f + norm_scale * weighted_in - inputs_f * norm_scale**3 * in_dot / model_width
     )
-    heads_grad = contract_first(gathered, d_cols)
-    heads_shard, out_shard = (
-        scatter_two(heads_grad, "dp"),
-        scatter_two(out_grad, "dp"),
-    )
+    dp_bits = axis_bits("dp")
+    gate_shard = scatter_rows(contract_first(gathered, d_cols[:, :own_inner]), "dp", dp_bits)
+    value_shard = scatter_rows(
+        contract_first(gathered, d_cols[:, own_inner:]), "dp", dp_bits[1:] + dp_bits[:1]
+    )
+    out_shard = scatter_two(out_grad, "dp")
     heads_shard = (
-        heads_shard.reshape(-1, 2, own_heads, head_size).transpose(0, 2, 1, 3).reshape(-1, in_width)
+        jnp.concatenate([gate_shard, value_shard], axis=1).reshape(-1, 2, own_heads, head_size).transpose(0, 2, 1, 3).reshape(-1, in_width)
     )
     norm_gain_grad = jnp.sum(inputs_f * norm_scale * d_normed, axis=0)
     own_sums = sum_all(
         jnp.concatenate(
             [
-                norm_gain_grad,
                 d_taps[:, own_inner:].reshape(-1),
                 gate_gain_grad,
                 d_taps[:, :own_inner].reshape(-1),
@@ -690,16 +713,15 @@
     shared_part = scatter_rows(
         contract_first(normed, d_shared_low), "dp", axis_bits("dp")
     )
-    shared_rows, shared_width = shared_part.shape
-    gain_ends = model_width + 10 * state_size
-    chan_begin = gain_ends + all_inner
+    bc_ends = 10 * state_size
+    chan_begin = bc_ends + all_inner
     head_begin = chan_begin + 5 * own_inner
-    ring_sums = sum_all(
-        jnp.concatenate([own_sums[:chan_begin], shared_part.reshape(-1)]), "tensor"
-    )
-    gain_sum = jnp.concatenate([ring_sums[:model_width], ring_sums[gain_ends:chan_begin]])
-    bc_sum = ring_sums[model_width:gain_ends].reshape(5, 2 * state_size)
-    shared_shard = ring_sums[chan_begin:].reshape(shared_rows, shared_width)
+    ring_sums = sum_all(own_sums[:chan_begin], "tensor")
+    shared_shard = sum_all(shared_part, "tensor")
+    gain_sum = jnp.concatenate(
+        [sum_all(sum_all(norm_gain_grad, "dp"), "tensor"), ring_sums[bc_ends:]]
+    )
+    bc_sum = ring_sums[:bc_ends].reshape(5, 2 * state_size)
     chan_grad = own_sums[chan_begin:head_begin].reshape(5, own_inner)
     head_grad = own_sums[head_begin:].reshape(3, own_heads)
     new_heads, new_first_heads, new_second_heads = adam_step(

time: 404 us -> 403 us (level)
  starting transfers between devices: 48.7 us -> 71.1 us
  local copies, waits for them, and re-layouts: 83.7 us -> 62.3 us
  waiting for transfers between devices: 105 us -> 92 us
  matrix products: 29 us -> 37 us
    ppermute x42 -> x60, starting transfers between devices: 48.7 us -> 71.1 us  [swap(): return lax.ppermute(vals, axis, [(i, i ^ bit) for i in range(ways)])]
    unnamed x153 -> x157, local copies, waits for them, and re-layouts: 30.9 us -> 17.9 us
    ppermute x42 -> x60, waiting for transfers between devices: 105 us -> 92 us  [swap(): return lax.ppermute(vals, axis, [(i, i ^ bit) for i in range(ways)])]
    convert_element_type x18 -> x13, local copies, waits for them, and re-layouts: 8.84 us -> 1.61 us  [halve_rows(): lax.dynamic_slice_in_dim(held, (1 - mine) * half, half, 0)]
    dot_general x3 -> x4, matrix products: 7.64 us -> 13.5 us  [contract_first(): lax.dot_general(left, right, (((0,), (0,)), ((), ())), preferred_element_...]
    sub x0 -> x1, other arithmetic: none -> 5.51 us  [shards(): cotangent_f + norm_scale * weighted_in]
    dynamic_update_slice x1, local copies, waits for them, and re-layouts: 5.44 us -> 0.01 us  [shards(): lax.dynamic_update_slice_in_dim(jnp.zeros((group_rows, all_heads), jnp.fl...]
    reshape x1 -> x3, local copies, waits for them, and re-layouts: 0.12 us -> 4.61 us  [scatter_rows(): held = vals.astype(jnp.bfloat16).reshape((2,) * depth + (rows, columns))]
  transfers between devices with their start and end apart: 42 -> 60, of which waited for: 17 -> 19; matrix products, arithmetic and copies ran while one was open for 29% -> 33% of each run, Pallas kernels for 0% -> 0%
where the time goes in v3:
time: 403 us; the launch traced here: 397 us
  waiting for transfers between devices  92 us (23%)
  starting transfers between devices  71.1 us (18%)
  Pallas kernels  68 us (17%)
  local copies, waits for them, and re-layouts  62.3 us (15%)
  other arithmetic  53.3 us (13%)
  matrix products  37 us (9%)
  blocking collectives  10.8 us (3%)
    ppermute x60, waiting for transfers between devices, swap(): return lax.ppermute(vals, axis, [(i, i ^ bit) for i in range(ways)])  92 us
    ppermute x60, starting transfers between devices, swap(): return lax.ppermute(vals, axis, [(i, i ^ bit) for i in range(ways)])  71.1 us
    pallas_call x1, Pallas kernels, run_backward(): pl.pallas_call(backward_kernel, grid=(blocks,), in_specs=[pl.BlockSpec(me...  40.5 us
    pallas_call x1, Pallas kernels, run_forward(): pl.pallas_call(forward_kernel, grid=(blocks,), in_specs=[pl.BlockSpec(mem...  27.5 us
    unnamed x157, local copies, waits for them, and re-layouts  17.9 us
    dot_general x5, matrix products, contract_last(): lax.dot_general(left, right, (((1,), (1,)), ((), ())), preferred_element_...  16.6 us
    dot_general x4, matrix products, contract_first(): lax.dot_general(left, right, (((0,), (0,)), ((), ())), preferred_element_...  13.5 us
    psum x1, blocking collectives, shards(): lax.psum(jnp.stack([jnp.sum(gated_vals * gated_vals, axis=1), jnp.sum(gat...  10.8 us
  transfers between devices with their start and end apart: 60, of which 19 were waited for; matrix products, arithmetic and copies ran while one was open for 33% of the time, Pallas kernels for 0%

profile of v3, /device:TPU:0, one launch (start us, length us, event | category | flops | bytes accessed | tf_op | source)
XLA Modules:
  0.0 396.8 jit_solution(10246161640018268510)
XLA Ops:
  2.4 4.0 %collective-permute-start.10 = (bf16[1,1,1,128,256]{4,3,2,1,0:T(8,128)(2,1)}, bf16[1,1,1,128,256]{4,3,2,1,0:T(8,128)(2,1)}, u32[]{:S(2)}, u32[]{:S(2)}) collective-permute-start(bf16[1,1,1,128,256]{4,3,2,1,0:T(8,128)(2,1)} %get-tuple-element.210), channel_id=1, source_target_pairs={{0,16},{4,20},{8,24},{12,28},{16,0},{20,4},{24,8},{28,12},{1,17},{... | collective-permute-start | bytes 196616 | tf_op jit(solution)/shard_map/ppermute | solution.py:453
  24.7 3.0 collective-permute-start.14
  36.1 9.2 %collective-permute-done.15 = bf16[2,1,2,128,256]{4,3,2,1,0:T(8,128)(2,1)S(1)} collective-permute-done((bf16[2,1,2,128,256]{4,3,2,1,0:T(8,128)(2,1)S(1)}, bf16[2,1,2,128,256]{4,3,2,1,0:T(8,128)(2,1)S(1)}, u32[]{:S(2)}, u32[]{:S(2)}) %collective-permute-start.15) | collective-permute-done | bytes 262176 | tf_op jit(solution)/shard_map/ppermute | solution.py:453
  46.8 12.7 %collective-permute-done.8 = bf16[1,1,512,1024]{3,2,1,0:T(8,128)(2,1)S(1)} collective-permute-done((bf16[1,1,512,1024]{3,2,1,0:T(8,128)(2,1)S(1)}, bf16[1,1,512,1024]{3,2,1,0:T(8,128)(2,1)S(1)}, u32[]{:S(2)}, u32[]{:S(2)}) %collective-permute-start.8) | collective-permute-done | bytes 1048608 | tf_op jit(solution)/shard_map/ppermute | solution.py:453
  71.9 9.1 %collective-permute-done.4 = bf16[2,2,1,128,640]{3,4,2,1,0:T(8,128)(2,1)S(1)} collective-permute-done((bf16[2,2,1,128,640]{3,4,2,1,0:T(8,128)(2,1)S(1)}, bf16[2,2,1,128,640]{3,4,2,1,0:T(8,128)(2,1)S(1)}, u32[]{:S(2)}, u32[]{:S(2)}) %collective-permute-start.4) | collective-permute-done | bytes 655392 | tf_op jit(solution)/shard_map/ppermute | solution.py:453
  92.3 5.3 %concatenate.112.weight_ref = bf16[1024,1408]{1,0:T(8,128)(2,1)} concatenate(bf16[1024,1280]{1,0:T(8,128)(2,1)} %fusion, bf16[1024,8]{1,0:T(8,128)(2,1)} %fusion.34, bf16[1024,120]{1,0:T(8,128)(2,1)S(1)} %broadcast_in_dim.12), dimensions={1} | concatenate | bytes 5767168 | tf_op jit(solution)/shard_map/concatenate | solution.py:604
  104.7 27.5 %scan_forward.1 = (f32[2048,512]{1,0:T(8,128)}, f32[2048,768]{1,0:T(8,128)}, f32[2048,768]{1,0:T(8,128)}, bf16[2048,768]{1,0:T(8,128)(2,1)}, f32[2048,128]{1,0:T...) custom-call(s32[2]{0:T(128)} %bitcast.190, bf16[2048,1024]{1,0:T(8,128)(2,1)} %bitcast.140, ...), custom_call_target="tpu_custom_call" | custom-call | flops 12000000000 | bytes 36000000 | tf_op jit(solution)/shard_map/scan_forward/pallas_call | solution.py:319
  132.2 6.9 %multiply_reduce_fusion.1 = (f32[2048]{0:T(1024)S(1)}, f32[2048]{0:T(1024)S(1)}, f32[2048,512]{1,0:T(8,128)}) fusion(f32[2048,512]{1,0:T(8,128)} %get-tuple-element.36, f32[512]{0:T(512)S(1)} %dynamic_slice.137, bf16[2048,1024]{1,0:T(8,128)(2,1)S(1)} %bitcast.143, bf16[1024,256]{1,0:T(8,128)(2,1)S(1)} %bitcast.176, bf16[1024,256]{1,0:T(8,128)(2,1)} %bitcast.179), kind=kOutput, calls=%fused_computation.6 | convolution fusion | flops 2154819584 | bytes 13649920 | tf_op jit(solution)/shard_map/dot_general | solution.py:629
  139.1 10.8 %psum.7 = f32[2,2048]{1,0:T(2,128)S(1)} all-reduce(f32[2,2048]{1,0:T(2,128)S(1)} %pad_maximum_fusion.31), channel_id=1, replica_groups=mesh['dp'=8,'tensor'=4] {'tensor'}, use_global_device_ids=true, to_apply=%region_5.6 | all-reduce | flops 4096 | bytes 32768 | tf_op jit(solution)/shard_map/psum | solution.py:630
  151.3 40.5 %scan_backward.1 = (bf16[2048,1024]{1,0:T(8,128)(2,1)}, f32[2048,384]{1,0:T(8,128)}, f32[8,768]{1,0:T(8,128)}, f32[8,512]{1,0:T(8,128)}, f32[8,128]{1,0:T(8,128)}) custom-call(s32[2]{0:T(128)} %bitcast.191, f32[2048,2]{1,0:T(8,128)} %copy.140.stat_ref, f32[2048,512]{1,0:T(8,128)} %get-tuple-element.216.normal_ref, f32[2048,512]{1,0:T(8,128)} %get-tuple-element.37.gate_ref, ...), custom_call_target="tpu_custom_call" | custom-call | flops 20000000000 | bytes 48000000 | tf_op jit(solution)/shard_map/scan_backward/pallas_call | solution.py:380
  195.5 3.6 collective-permute-start.46
  206.5 2.7 slice.203
  209.2 6.4 %fusion.18 = bf16[1024,512]{1,0:T(8,128)(2,1)} fusion(bf16[2048,1024]{1,0:T(8,128)(2,1)} %bitcast.141, bf16[2048,1024]{1,0:T(8,128)(2,1)} %get-tuple-element.44), kind=kOutput, calls=%fused_computation.48 | convolution fusion | flops 2148007936 | bytes 7340032 | tf_op jit(solution)/shard_map/dot_general | solution.py:437
  215.6 3.3 fusion.15
  237.2 3.7 convolution_convert_fusion
  262.7 10.3 %collective-permute-done.35 = bf16[2,128,256]{2,1,0:T(8,128)(2,1)S(1)} collective-permute-done((bf16[2,128,256]{2,1,0:T(8,128)(2,1)S(1)}, bf16[2,128,256]{2,1,0:T(8,128)(2,1)S(1)}, u32[]{:S(2)}, u32[]{:S(2)}) %collective-permute-start.35) | collective-permute-done | bytes 131104 | tf_op jit(solution)/shard_map/ppermute | solution.py:453
  273.0 2.8 collective-permute-start.38
  275.8 5.4 %collective-permute-done.38 = bf16[2,128,256]{2,1,0:T(8,128)(2,1)S(1)} collective-permute-done((bf16[2,128,256]{2,1,0:T(8,128)(2,1)S(1)}, bf16[2,128,256]{2,1,0:T(8,128)(2,1)S(1)}, u32[]{:S(2)}, u32[]{:S(2)}) %collective-permute-start.38) | collective-permute-done | bytes 131104 | tf_op jit(solution)/shard_map/ppermute | solution.py:453
  281.7 5.7 %collective-permute-done.36 = bf16[1,128,256]{2,1,0:T(8,128)(2,1)S(1)} collective-permute-done((bf16[1,128,256]{2,1,0:T(8,128)(2,1)S(1)}, bf16[1,128,256]{2,1,0:T(8,128)(2,1)S(1)}, u32[]{:S(2)}, u32[]{:S(2)}) %collective-permute-start.36) | collective-permute-done | bytes 65568 | tf_op jit(solution)/shard_map/ppermute | solution.py:453
  287.7 3.9 collective-permute-done.39
  295.6 3.0 collective-permute-start.26
  300.7 6.1 %collective-permute-done.23 = bf16[2,128,512]{2,1,0:T(8,128)(2,1)S(1)} collective-permute-done((bf16[2,128,512]{2,1,0:T(8,128)(2,1)S(1)}, bf16[2,128,512]{2,1,0:T(8,128)(2,1)S(1)}, u32[]{:S(2)}, u32[]{:S(2)}) %collective-permute-start.23) | collective-permute-done | bytes 262176 | tf_op jit(solution)/shard_map/ppermute | solution.py:453
  307.0 7.1 %collective-permute-done.26 = bf16[2,128,512]{2,1,0:T(8,128)(2,1)S(1)} collective-permute-done((bf16[2,128,512]{2,1,0:T(8,128)(2,1)S(1)}, bf16[2,128,512]{2,1,0:T(8,128)(2,1)S(1)}, u32[]{:S(2)}, u32[]{:S(2)}) %collective-permute-start.26) | collective-permute-done | bytes 262176 | tf_op jit(solution)/shard_map/ppermute | solution.py:453
  317.7 3.1 reshape.348
  328.8 2.8 collective-permute-done.28
  332.8 5.0 %convert_add_fusion = f32[1024,1024]{1,0:T(8,128)S(1)} fusion(bf16[1024,1024]{1,0:T(8,128)(2,1)} %collective-permute-done.18, bf16[1024,1024]{1,0:T(8,128)(2,1)} %bitcast.161, bf16[1024,672]{1,0:T(8,128)(2,1)S(1)} %bitcast.131, bf16[1024,640]{1,0:T(8,128)(2,1)} %bitcast.134), kind=kOutput, calls=%fused_computation.2 | convolution fusion | flops 2153775104 | bytes 11075584 | tf_op jit(solution)/shard_map/dot_general | solution.py:431
  339.9 3.0 collective-permute-start.30
  347.2 2.9 convert_add_fusion.1
  351.7 12.5 %collective-permute-done.19 = bf16[1,512,1024]{2,1,0:T(8,128)(2,1)S(1)} collective-permute-done((bf16[1,512,1024]{2,1,0:T(8,128)(2,1)S(1)}, bf16[1,512,1024]{2,1,0:T(8,128)(2,1)S(1)}, u32[]{:S(2)}, u32[]{:S(2)}) %collective-permute-start.19) | collective-permute-done | bytes 1048608 | tf_op jit(solution)/shard_map/ppermute | solution.py:453
  366.6 3.6 collective-permute-start.56
  371.6 3.1 collective-permute-start.54
  390.3 5.5 %fusion.6 = (f32[512,1024]{1,0:T(8,128)}, f32[512,1024]{1,0:T(8,128)}) fusion(bf16[512,1024]{1,0:T(8,128)(2,1)S(1)} %copy-done.4, bf16[512,1024]{1,0:T(8,128)(2,1)S(1)} %copy-done, f32[512,1024]{1,0:T(8,128)} %get-tuple-element.217, f32[512]{0:T(512)S(1)} %get-tuple-element.144, f32[512]{0:T(512)S(1)} %copy-done.66, f32[1024]{0:T(1024)S(1)} %slice.110, ...), kind=kLoop, calls=%fused_computation.24 | loop fusion | flops 6815744 | bytes 11546628 | tf_op jit(solution)/shard_map/sub | solution.py:690
  (417 shorter events, 160.1 us)
Async XLA Ops:
  2.4 21.2 %collective-permute-start.10 = (bf16[1,1,1,128,256]{4,3,2,1,0:T(8,128)(2,1)}, bf16[1,1,1,128,256]{4,3,2,1,0:T(8,128)(2,1)}, u32[]{:S(2)}, u32[]{:S(2)}) collective-permute-start(bf16[1,1,1,128,256]{4,3,2,1,0:T(8,128)(2,1)} %get-tuple-element.210), channel_id=1, source_target_pairs={{0,16},{4,20},{8,24},{12,28},{16,0},{20,4},{24,8},{28,12},{1,17},{... | collective-permute-start | bytes 196616 | tf_op jit(solution)/shard_map/ppermute | solution.py:453
  6.4 17.3 %collective-permute-start.13 = (bf16[1,1,1,128,256]{4,3,2,1,0:T(8,128)(2,1)}, bf16[1,1,1,128,256]{4,3,2,1,0:T(8,128)(2,1)}, u32[]{:S(2)}, u32[]{:S(2)}) collective-permute-start(bf16[1,1,1,128,256]{4,3,2,1,0:T(8,128)(2,1)} %get-tuple-element.211), channel_id=1, source_target_pairs={{0,4},{4,0},{8,12},{12,8},{16,20},{20,16},{24,28},{28,24},{1,5},{5... | collective-permute-start | bytes 196616 | tf_op jit(solution)/shard_map/ppermute | solution.py:453
  9.9 17.8 %collective-permute-start.2 = (bf16[1,1,1,128,640]{3,4,2,1,0:T(8,128)(2,1)}, bf16[1,1,1,128,640]{3,4,2,1,0:T(8,128)(2,1)}, u32[]{:S(2)}, u32[]{:S(2)}) collective-permute-start(bf16[1,1,1,128,640]{3,4,2,1,0:T(8,128)(2,1)} %slice_bitcast_fusion), channel_id=1, source_target_pairs={{0,16},{4,20},{8,24},{12,28},{16,0},{20,4},{24,8},{28,12},{1,17},{... | collective-permute-start | bytes 491528 | tf_op jit(solution)/shard_map/ppermute | solution.py:453
  10.3 20.0 %collective-permute-start.5 = (bf16[1,1,1,128,672]{3,4,2,1,0:T(8,128)(2,1)S(1)}, bf16[1,1,1,128,672]{3,4,2,1,0:T(8,128)(2,1)S(1)}, u32[]{:S(2)}, u32[]{:S(2)}) collective-permute-start(bf16[1,1,1,128,672]{3,4,2,1,0:T(8,128)(2,1)S(1)} %fusion.36), channel_id=1, source_target_pairs={{0,4},{4,0},{8,12},{12,8},{16,20},{20,16},{24,28},{28,24},{1,5},{5... | collective-permute-start | bytes 516104 | tf_op jit(solution)/shard_map/ppermute | solution.py:453
  12.8 34.0 %collective-permute-start = (bf16[1,1,512,1024]{3,2,1,0:T(8,128)(2,1)}, bf16[1,1,512,1024]{3,2,1,0:T(8,128)(2,1)}, u32[]{:S(2)}, u32[]{:S(2)}) collective-permute-start(bf16[1,1,512,1024]{3,2,1,0:T(8,128)(2,1)} %fusion.32), channel_id=1, source_target_pairs={{0,2},{1,3},{2,0},{3,1},{4,6},{5,7},{6,4},{7,5},{8,10},{9,11},{10,... | collective-permute-start | bytes 3145736 | tf_op jit(solution)/shard_map/ppermute | solution.py:453
  23.6 35.9 %collective-permute-start.8 = (bf16[1,1,512,1024]{3,2,1,0:T(8,128)(2,1)S(1)}, bf16[1,1,512,1024]{3,2,1,0:T(8,128)(2,1)S(1)}, u32[]{:S(2)}, u32[]{:S(2)}) collective-permute-start(bf16[1,1,512,1024]{3,2,1,0:T(8,128)(2,1)S(1)} %fusion.21), channel_id=1, source_target_pairs={{0,2},{1,3},{2,0},{3,1},{4,6},{5,7},{6,4},{7,5},{8,10},{9,11},{10,... | collective-permute-start | bytes 3145736 | tf_op jit(solution)/shard_map/ppermute | solution.py:453
  30.4 16.4 %collective-permute-start.3 = (bf16[2,1,1,128,640]{3,4,2,1,0:T(8,128)(2,1)S(1)}, bf16[2,1,1,128,640]{3,4,2,1,0:T(8,128)(2,1)S(1)}, u32[]{:S(2)}, u32[]{:S(2)}) collective-permute-start(bf16[2,1,1,128,640]{3,4,2,1,0:T(8,128)(2,1)S(1)} %pad_maximum_fusion.18), channel_id=1, source_target_pairs={{0,8},{4,12},{8,0},{12,4},{16,24},{20,28},{24,16},{28,20},{1,9},{5... | collective-permute-start | bytes 983048 | tf_op jit(solution)/shard_map/ppermute | solution.py:453
  31.7 13.6 %collective-permute-start.15 = (bf16[2,1,2,128,256]{4,3,2,1,0:T(8,128)(2,1)S(1)}, bf16[2,1,2,128,256]{4,3,2,1,0:T(8,128)(2,1)S(1)}, u32[]{:S(2)}, u32[]{:S(2)}) collective-permute-start(bf16[2,1,2,128,256]{4,3,2,1,0:T(8,128)(2,1)S(1)} %pad_maximum_fusion.25), channel_id=1, source_target_pairs={{0,8},{4,12},{8,0},{12,4},{16,24},{20,28},{24,16},{28,20},{1,9},{5... | collective-permute-start | bytes 786440 | tf_op jit(solution)/shard_map/ppermute | solution.py:453
  45.4 20.1 %collective-permute-start.6 = (bf16[1,1,2,128,672]{3,4,2,1,0:T(8,128)(2,1)S(1)}, bf16[1,1,2,128,672]{3,4,2,1,0:T(8,128)(2,1)S(1)}, u32[]{:S(2)}, u32[]{:S(2)}) collective-permute-start(bf16[1,1,2,128,672]{3,4,2,1,0:T(8,128)(2,1)S(1)} %pad_maximum_fusion.17), channel_id=1, source_target_pairs={{0,16},{4,20},{8,24},{12,28},{16,0},{20,4},{24,8},{28,12},{1,17},{... | collective-permute-start | bytes 1032200 | tf_op jit(solution)/shard_map/ppermute | solution.py:453
  63.8 33.8 %collective-permute-start.1 = (bf16[2,1,512,1024]{3,2,1,0:T(8,128)(2,1)}, bf16[2,1,512,1024]{3,2,1,0:T(8,128)(2,1)}, u32[]{:S(2)}, u32[]{:S(2)}) collective-permute-start(bf16[2,1,512,1024]{3,2,1,0:T(8,128)(2,1)} %pad_maximum_fusion.3), channel_id=1, source_target_pairs={{0,1},{1,0},{2,3},{3,2},{4,5},{5,4},{6,7},{7,6},{8,9},{9,8},{10,11... | collective-permute-start | bytes 6291464 | tf_op jit(solution)/shard_map/ppermute | solution.py:453
  63.8 17.2 %collective-permute-start.4 = (bf16[2,2,1,128,640]{3,4,2,1,0:T(8,128)(2,1)S(1)}, bf16[2,2,1,128,640]{3,4,2,1,0:T(8,128)(2,1)S(1)}, u32[]{:S(2)}, u32[]{:S(2)}) collective-permute-start(bf16[2,2,1,128,640]{3,4,2,1,0:T(8,128)(2,1)S(1)} %pad_maximum_fusion.14), channel_id=1, source_target_pairs={{0,4},{4,0},{8,12},{12,8},{16,20},{20,16},{24,28},{28,24},{1,5},{5... | collective-permute-start | bytes 1966088 | tf_op jit(solution)/shard_map/ppermute | solution.py:453
  67.1 17.9 %collective-permute-start.7 = (bf16[2,1,2,128,672]{3,4,2,1,0:T(8,128)(2,1)}, bf16[2,1,2,128,672]{3,4,2,1,0:T(8,128)(2,1)}, u32[]{:S(2)}, u32[]{:S(2)}) collective-permute-start(bf16[2,1,2,128,672]{3,4,2,1,0:T(8,128)(2,1)} %pad_maximum_fusion.13), channel_id=1, source_target_pairs={{0,8},{4,12},{8,0},{12,4},{16,24},{20,28},{24,16},{28,20},{1,9},{5... | collective-permute-start | bytes 2064392 | tf_op jit(solution)/shard_map/ppermute | solution.py:453
  70.2 32.2 %collective-permute-start.9 = (bf16[2,1,512,1024]{3,2,1,0:T(8,128)(2,1)}, bf16[2,1,512,1024]{3,2,1,0:T(8,128)(2,1)}, u32[]{:S(2)}, u32[]{:S(2)}) collective-permute-start(bf16[2,1,512,1024]{3,2,1,0:T(8,128)(2,1)} %pad_maximum_fusion.4), channel_id=1, source_target_pairs={{0,1},{1,0},{2,3},{3,2},{4,5},{5,4},{6,7},{7,6},{8,9},{9,8},{10,11... | collective-permute-start | bytes 6291464 | tf_op jit(solution)/shard_map/ppermute | solution.py:453
  195.5 48.3 %collective-permute-start.46 = (f32[5912]{0:T(1024)S(1)}, f32[5912]{0:T(1024)S(1)}, u32[]{:S(2)}, u32[]{:S(2)}) collective-permute-start(f32[5912]{0:T(1024)S(1)} %pad_maximum_fusion.30), channel_id=1, source_target_pairs={{0,28},{4,24},{8,20},{12,16},{16,12},{20,8},{24,4},{28,0},{1,29},{... | collective-permute-start | bytes 70952 | tf_op jit(solution)/shard_map/ppermute | solution.py:453
  199.1 45.5 %collective-permute-start.45 = (f32[5912]{0:T(1024)S(1)}, f32[5912]{0:T(1024)S(1)}, u32[]{:S(2)}, u32[]{:S(2)}) collective-permute-start(f32[5912]{0:T(1024)S(1)} %pad_maximum_fusion.30), channel_id=1, source_target_pairs={{0,24},{4,28},{8,16},{12,20},{16,8},{20,12},{24,0},{28,4},{1,25},{... | collective-permute-start | bytes 70952 | tf_op jit(solution)/shard_map/ppermute | solution.py:453
  199.4 47.5 %collective-permute-start.44 = (f32[5912]{0:T(1024)S(1)}, f32[5912]{0:T(1024)}, u32[]{:S(2)}, u32[]{:S(2)}) collective-permute-start(f32[5912]{0:T(1024)S(1)} %pad_maximum_fusion.30), channel_id=1, source_target_pairs={{0,20},{4,16},{8,28},{12,24},{16,4},{20,0},{24,12},{28,8},{1,21},{... | collective-permute-start | bytes 70952 | tf_op jit(solution)/shard_map/ppermute | solution.py:453
  201.1 46.3 %collective-permute-start.43 = (f32[5912]{0:T(1024)S(1)}, f32[5912]{0:T(1024)}, u32[]{:S(2)}, u32[]{:S(2)}) collective-permute-start(f32[5912]{0:T(1024)S(1)} %pad_maximum_fusion.30), channel_id=1, source_target_pairs={{0,16},{4,20},{8,24},{12,28},{16,0},{20,4},{24,8},{28,12},{1,17},{... | collective-permute-start | bytes 70952 | tf_op jit(solution)/shard_map/ppermute | solution.py:453
  203.2 45.4 %collective-permute-start.42 = (f32[5912]{0:T(1024)S(1)}, f32[5912]{0:T(1024)}, u32[]{:S(2)}, u32[]{:S(2)}) collective-permute-start(f32[5912]{0:T(1024)S(1)} %pad_maximum_fusion.30), channel_id=1, source_target_pairs={{0,12},{4,8},{8,4},{12,0},{16,28},{20,24},{24,20},{28,16},{1,13},{... | collective-permute-start | bytes 70952 | tf_op jit(solution)/shard_map/ppermute | solution.py:453
  254.4 44.1 %collective-permute-start.20 = (bf16[2,512,288]{1,2,0:T(8,128)(2,1)}, bf16[2,512,288]{1,2,0:T(8,128)(2,1)}, u32[]{:S(2)}, u32[]{:S(2)}) collective-permute-start(bf16[2,512,288]{1,2,0:T(8,128)(2,1)} %constant_dynamic-slice_fusion.5), channel_id=1, source_target_pairs={{0,1},{1,0},{2,3},{3,2},{4,5},{5,4},{6,7},{7,6},{8,9},{9,8},{10,11... | collective-permute-start | bytes 1769480 | tf_op jit(solution)/shard_map/ppermute | solution.py:453
  254.7 38.0 %collective-permute-start.22 = (bf16[4,128,512]{2,1,0:T(8,128)(2,1)}, bf16[4,128,512]{2,1,0:T(8,128)(2,1)}, u32[]{:S(2)}, u32[]{:S(2)}) collective-permute-start(bf16[4,128,512]{2,1,0:T(8,128)(2,1)} %constant_dynamic-slice_fusion.4), channel_id=1, source_target_pairs={{0,4},{4,0},{8,12},{12,8},{16,20},{20,16},{24,28},{28,24},{1,5},{5... | collective-permute-start | bytes 1572872 | tf_op jit(solution)/shard_map/ppermute | solution.py:453
  256.2 38.1 %collective-permute-start.25 = (bf16[4,128,512]{2,1,0:T(8,128)(2,1)}, bf16[4,128,512]{2,1,0:T(8,128)(2,1)}, u32[]{:S(2)}, u32[]{:S(2)}) collective-permute-start(bf16[4,128,512]{2,1,0:T(8,128)(2,1)} %constant_dynamic-slice_fusion.3), channel_id=1, source_target_pairs={{0,8},{4,12},{8,0},{12,4},{16,24},{20,28},{24,16},{28,20},{1,9},{5... | collective-permute-start | bytes 1572872 | tf_op jit(solution)/shard_map/ppermute | solution.py:453
  259.6 87.6 %collective-permute-start.16 = (bf16[1024,1024]{1,0:T(8,128)(2,1)}, bf16[1024,1024]{1,0:T(8,128)(2,1)}, u32[]{:S(2)}, u32[]{:S(2)}) collective-permute-start(bf16[1024,1024]{1,0:T(8,128)(2,1)} %convolution_convert_fusion.1), channel_id=1, source_target_pairs={{0,1},{1,0},{2,3},{3,2},{4,5},{5,4},{6,7},{7,6},{8,9},{9,8},{10,11... | collective-permute-start | bytes 6291464 | tf_op jit(solution)/shard_map/ppermute | solution.py:453
  291.6 41.2 %collective-permute-start.18 = (bf16[1024,1024]{1,0:T(8,128)(2,1)}, bf16[1024,1024]{1,0:T(8,128)(2,1)}, u32[]{:S(2)}, u32[]{:S(2)}) collective-permute-start(bf16[1024,1024]{1,0:T(8,128)(2,1)} %convolution_convert_fusion), channel_id=1, source_target_pairs={{0,1},{1,0},{2,3},{3,2},{4,5},{5,4},{6,7},{7,6},{8,9},{9,8},{10,11... | collective-permute-start | bytes 6291464 | tf_op jit(solution)/shard_map/ppermute | solution.py:453
  295.6 18.5 %collective-permute-start.26 = (bf16[2,128,512]{2,1,0:T(8,128)(2,1)S(1)}, bf16[2,128,512]{2,1,0:T(8,128)(2,1)S(1)}, u32[]{:S(2)}, u32[]{:S(2)}) collective-permute-start(bf16[2,128,512]{2,1,0:T(8,128)(2,1)S(1)} %dynamic-slice_convert_fusion.3), channel_id=1, source_target_pairs={{0,16},{4,20},{8,24},{12,28},{16,0},{20,4},{24,8},{28,12},{1,17},{... | collective-permute-start | bytes 786440 | tf_op jit(solution)/shard_map/ppermute | solution.py:453
  299.9 15.7 %collective-permute-start.21 = (bf16[1,512,288]{1,2,0:T(8,128)(2,1)S(1)}, bf16[1,512,288]{1,2,0:T(8,128)(2,1)S(1)}, u32[]{:S(2)}, u32[]{:S(2)}) collective-permute-start(bf16[1,512,288]{1,2,0:T(8,128)(2,1)S(1)} %dynamic-slice_convert_fusion.2), channel_id=1, source_target_pairs={{0,2},{1,3},{2,0},{3,1},{4,6},{5,7},{6,4},{7,5},{8,10},{9,11},{10,... | collective-permute-start | bytes 884744 | tf_op jit(solution)/shard_map/ppermute | solution.py:453
  306.9 18.0 %collective-permute-start.24 = (bf16[1,128,512]{2,1,0:T(8,128)(2,1)S(1)}, bf16[1,128,512]{2,1,0:T(8,128)(2,1)}, u32[]{:S(2)}, u32[]{:S(2)}) collective-permute-start(bf16[1,128,512]{2,1,0:T(8,128)(2,1)S(1)} %dynamic-slice_convert_fusion.9), channel_id=1, source_target_pairs={{0,16},{4,20},{8,24},{12,28},{16,0},{20,4},{24,8},{28,12},{1,17},{... | collective-permute-start | bytes 393224 | tf_op jit(solution)/shard_map/ppermute | solution.py:453
  338.0 26.2 %collective-permute-start.19 = (bf16[1,512,1024]{2,1,0:T(8,128)(2,1)S(1)}, bf16[1,512,1024]{2,1,0:T(8,128)(2,1)S(1)}, u32[]{:S(2)}, u32[]{:S(2)}) collective-permute-start(bf16[1,512,1024]{2,1,0:T(8,128)(2,1)S(1)} %dynamic-slice_convert_fusion), channel_id=1, source_target_pairs={{0,2},{1,3},{2,0},{3,1},{4,6},{5,7},{6,4},{7,5},{8,10},{9,11},{10,... | collective-permute-start | bytes 3145736 | tf_op jit(solution)/shard_map/ppermute | solution.py:453
  345.3 25.0 %collective-permute-start.33 = (f32[128,288]{0,1:T(8,128)S(1)}, f32[128,288]{0,1:T(8,128)S(1)}, u32[]{:S(2)}, u32[]{:S(2)}) collective-permute-start(f32[128,288]{0,1:T(8,128)S(1)} %add_bitcast_fusion), channel_id=1, source_target_pairs={{0,3},{1,2},{2,1},{3,0},{4,7},{5,6},{6,5},{7,4},{8,11},{9,10},{10,... | collective-permute-start | bytes 442376 | tf_op jit(solution)/shard_map/ppermute | solution.py:453
  345.3 26.3 %collective-permute-start.32 = (f32[128,288]{0,1:T(8,128)S(1)}, f32[128,288]{0,1:T(8,128)S(1)}, u32[]{:S(2)}, u32[]{:S(2)}) collective-permute-start(f32[128,288]{0,1:T(8,128)S(1)} %add_bitcast_fusion), channel_id=1, source_target_pairs={{0,2},{1,3},{2,0},{3,1},{4,6},{5,7},{6,4},{7,5},{8,10},{9,11},{10,... | collective-permute-start | bytes 442376 | tf_op jit(solution)/shard_map/ppermute | solution.py:453
  345.9 35.4 %collective-permute-start.31 = (f32[128,288]{0,1:T(8,128)S(1)}, f32[128,288]{0,1:T(8,128)}, u32[]{:S(2)}, u32[]{:S(2)}) collective-permute-start(f32[128,288]{0,1:T(8,128)S(1)} %add_bitcast_fusion), channel_id=1, source_target_pairs={{0,1},{1,0},{2,3},{3,2},{4,5},{5,4},{6,7},{7,6},{8,9},{9,8},{10,11... | collective-permute-start | bytes 442376 | tf_op jit(solution)/shard_map/ppermute | solution.py:453
  351.3 39.0 %collective-permute-start.17 = (bf16[1,512,1024]{2,1,0:T(8,128)(2,1)}, bf16[1,512,1024]{2,1,0:T(8,128)(2,1)}, u32[]{:S(2)}, u32[]{:S(2)}) collective-permute-start(bf16[1,512,1024]{2,1,0:T(8,128)(2,1)} %dynamic-slice_convert_fusion.1), channel_id=1, source_target_pairs={{0,2},{1,3},{2,0},{3,1},{4,6},{5,7},{6,4},{7,5},{8,10},{9,11},{10,... | collective-permute-start | bytes 3145736 | tf_op jit(solution)/shard_map/ppermute | solution.py:453
  366.6 14.7 %collective-permute-start.56 = (f32[1024]{0:T(1024)S(1)}, f32[1024]{0:T(1024)S(1)}, u32[]{:S(2)}, u32[]{:S(2)}) collective-permute-start(f32[1024]{0:T(1024)S(1)} %get-tuple-element.143), channel_id=1, source_target_pairs={{0,28},{4,24},{8,20},{12,16},{16,12},{20,8},{24,4},{28,0},{1,29},{... | collective-permute-start | bytes 12296 | tf_op jit(solution)/shard_map/ppermute | solution.py:453
  (104 other events, 1010.0 us)
